TPU v7x, 256 devices: a whole 4x4x8 slice. The times are simulated.
256 devices in a mesh: dp: 64 (over x, y, z_lo, core), fsdp: 4 (over z_hi).
Axes of the slice: x: 4, y: 4, z: 8 (z_hi: 4, z_lo: 2; z = z_hi * 2 + z_lo), core: 2. Of those that a mesh axis runs over, the one named last changes fastest.
Arguments:
- momentum: float32 [64, 64, 28672], P('dp', None, 'fsdp'), may hold values from -6 to 6
- gradient: bfloat16 [64, 64, 28672], P('dp', None, 'fsdp'), may hold values from -6 to 6
- weight: bfloat16 [64, 28672], P(None, 'fsdp'), may hold values from -0.75 to 0.75
- tokens: bfloat16 [32768, 64], P(('dp', 'fsdp')), may hold values from -6 to 6
- block_index: int32 [64, 1, 448, 4], P('dp', None, 'fsdp'), may hold values from 0 to 63, all different within a row
Outputs:
- new_momentum: float32 [64, 64, 28672], P('dp', None, 'fsdp')
- preact: bfloat16 [32768, 28672], P(('dp', 'fsdp'))
Inputs may be any that keep to these rules, and one draw needn't show every extreme that they name: Within each group the 4 entries of block_index name different blocks.
All inputs are finite; a program needn't handle non-finite values.
Results may differ from a plain program's by a relative error of at most 0.0049.
Values may be sent and summed in bfloat16 or wider, within the bound.
No kernel may reach another device: no remote copies, remote signals or barrier semaphores. Data moves between devices by JAX's collectives and lax.ppermute only.
A program may use at most 192 MiB of HBM per device.

v0:
```python
import math

import jax
import jax.numpy as jnp
from jax import lax
from jax.sharding import PartitionSpec as P

GROUP = 64
BLOCK = 8
KEEP = 4
POSITIONS = 64


decay_rate = 0.9
step_scale = 5.0
exact = lax.Precision.HIGHEST


def cosine_table(group_size):
    position = jnp.arange(group_size, dtype=jnp.float32)
    frequency = position[:, None]
    factor = jnp.where(frequency == 0, jnp.sqrt(1.0 / group_size), jnp.sqrt(2.0 / group_size))
    return factor * jnp.cos(
        jnp.pi * (2.0 * position[None, :] + 1.0) * frequency / (2.0 * group_size)
    )


def group_transform(field_grid, left_table, right_table, group_size):
    height, breadth = field_grid.shape
    stacked = field_grid.reshape(height // group_size, group_size, breadth)
    mixed = jnp.einsum("ka,rac->rkc", left_table, stacked, precision=exact)
    span = right_table.shape[0]
    result = jnp.dot(mixed.reshape(-1, span), right_table, precision=exact)
    return result.reshape(height, breadth)


def on_device(momentum, gradient, weight, tokens, block_index):
    height, breadth = weight.shape
    per_side = GROUP // BLOCK
    group_rows = height // GROUP
    group_cols = breadth // GROUP
    cosines = cosine_table(GROUP)
    pairing = math.gcd(group_cols, max(1, 128 // GROUP))
    forward_right = jnp.kron(jnp.eye(pairing, dtype=jnp.float32), cosines.T)
    inverse_right = jnp.kron(jnp.eye(pairing, dtype=jnp.float32), cosines)
    moment = decay_rate * momentum[0] + gradient[0].astype(jnp.float32)
    coefficients = group_transform(moment, cosines, forward_right, GROUP)
    picked = block_index[0]
    chosen = jax.nn.one_hot(picked, POSITIONS, dtype=jnp.float32).reshape(
        group_rows, group_cols, KEEP, per_side, per_side
    )
    small_mask = jnp.sum(chosen, axis=2).transpose(0, 2, 1, 3)
    dense_mask = jnp.broadcast_to(
        small_mask[:, :, None, :, :, None],
        (group_rows, per_side, BLOCK, group_cols, per_side, BLOCK),
    ).reshape(height, breadth)
    transmitted = group_transform(coefficients * dense_mask, cosines.T, inverse_right, GROUP)
    new_momentum = (moment - transmitted)[None]
    replicas = lax.axis_size("dp")
    shaped_coeffs = coefficients.reshape(group_rows, per_side, BLOCK, group_cols, per_side, BLOCK)
    values = jnp.einsum("xykij,xiayjb->xykab", chosen, shaped_coeffs, precision=exact)
    values = values.reshape(group_rows * group_cols, KEEP * BLOCK * BLOCK)
    flat_picked = picked.reshape(group_rows * group_cols, KEEP)
    all_values, all_picked = (
        lax.all_gather(values[None], "dp", axis=0, tiled=True),
        lax.all_gather(flat_picked[None], "dp", axis=0, tiled=True),
    )
    count = all_values.shape[0]
    every_chosen = jax.nn.one_hot(all_picked, POSITIONS, dtype=jnp.float32).reshape(
        count, group_rows, group_cols, KEEP, per_side, per_side
    )
    shaped_values = all_values.reshape(count, group_rows, group_cols, KEEP, BLOCK, BLOCK)
    total_grid = jnp.einsum(
        "rxykij,rxykab->xiayjb", every_chosen, shaped_values, precision=exact
    ).reshape(height, breadth)
    update = group_transform(total_grid / replicas, cosines.T, inverse_right, GROUP)
    new_weight = (weight.astype(jnp.float32) - step_scale * update).astype(jnp.bfloat16)
    preact = jnp.dot(
        tokens,
        lax.all_gather(new_weight, "fsdp", axis=1, tiled=True),
        preferred_element_type=jnp.float32,
    ).astype(jnp.bfloat16)
    return (new_momentum, preact)


def solution(mesh):
    return jax.shard_map(
        on_device,
        mesh=mesh,
        in_specs=(
            P("dp", None, "fsdp"),
            P("dp", None, "fsdp"),
            P(None, "fsdp"),
            P(("dp", "fsdp"), None),
            P("dp", None, "fsdp", None),
        ),
        out_specs=(P("dp", None, "fsdp"), P(("dp", "fsdp"), None)),
        check_vma=False,
    )
```

profile of v0, /device:TPU:35, one launch (start us, length us, event | category | flops | bytes accessed | tf_op | source)
XLA Modules:
  0.0 438.3 jit_solution(17452945074740958871)
XLA Ops:
  7.2 0.0 copy-start
  7.2 0.0 all-gather.4.cloned.1.call-start
  7.3 0.3 cosine_multiply_fusion.1
  7.6 3.9 convolution_bitcast_fusion.2
  11.5 1.5 reshape.210
  13.0 0.1 broadcast_multiply_fusion
  13.1 0.1 mul.237
  13.2 3.1 fusion.37
  16.3 0.0 copy-start.5
  16.3 19.0 %reshape.214 = f32[8,8,112,8,8]{4,3,2,1,0:T(8,128)} reshape(f32[3584,128]{1,0:T(8,128)S(1)} %fusion.37) | data formatting | bytes 3670016 | tf_op jit(solution)/shard_map/reshape.12
  35.3 0.0 copy-done.5
  35.3 0.1 copy.31
  35.4 19.8 %fusion.15 = f32[112,4,8,8]{3,1,2,0:T(4,128)} fusion(f32[8,8,112,8,8]{4,3,2,1,0:T(8,128)} %reshape.214, s32[8,8]{1,0:T(8,128)S(1)} %multiply_add_fusion, s32[112,4]{1,0:T(8,128)S(1)} %copy.31), kind=kOutput, calls=%fused_computation.21 | convolution fusion | flops 22048768 | bytes 1951744 | tf_op jit(solution)/shard_map/xykij,xiayjb->xykab/dot_general | solution.py:61
  55.2 1.9 copy.33
  57.1 0.7 copy.34
  57.8 0.0 all-gather.4.cloned.1.call-update
  57.9 0.0 all-gather.6.cloned.1.call-start
  57.9 0.1 mul.241
  58.0 67.8 %all-gather = s32[64,1,112,4]{2,3,1,0:T(4,128)S(1)} all-gather(s32[1,1,112,4]{2,3,1,0:T(4,128)S(1)} %copy-done.5), channel_id=2, replica_groups=mesh['dp'=64,'fsdp'=4] {'dp'}, dimensions={0}, use_global_device_ids=true | all-gather | bytes 116480 | tf_op jit(solution)/shard_map/all_gather | solution.py:66
  125.8 0.1 copy.36
  126.0 4.2 fusion.52
  130.2 42.4 %all-gather.4.cloned.1.call-done = f32[64,112,256]{2,1,0:T(8,128)} async-done(((f32[1,112,256]{2,1,0:T(8,128)}), f32[64,112,256]{2,1,0:T(8,128)}) %all-gather.4.cloned.1.call-update) | async-done | bytes 7340048 | tf_op jit(solution)/shard_map/all_gather | solution.py:65
  172.6 8.8 %copy.35 = f32[64,112,256]{1,2,0:T(8,128)} copy(f32[64,112,256]{2,1,0:T(8,128)} %all-gather.4.cloned.1.call-done) | data formatting | bytes 14680064 | tf_op jit(solution)/shard_map/all_gather | solution.py:65
  181.4 15.3 %copy.42 = f32[64,112,4,8,8,1]{0,4,2,5,3,1:T(8,128)} copy(f32[64,112,4,8,8,1]{1,4,3,2,0,5:T(8,128)} %bitcast.75) | data formatting | bytes 14680064 | tf_op jit(solution)/shard_map/reshape.15
  196.7 68.8 %fusion.1 = f32[1,8,8,112,8,8]{4,5,1,2,3,0:T(8,128)} fusion(f32[64,112,4,8,8,1]{0,4,2,5,3,1:T(8,128)} %copy.42, pred[64,112,4,8,8,1]{0,4,2,3,5,1:T(8,128)(4,1)} %fusion.52), kind=kOutput, calls=%fused_computation.3 | convolution fusion | flops 1409744896 | bytes 11010048 | tf_op jit(solution)/shard_map/rxykij,rxykab->xiayjb/dot_general | solution.py:73
  265.4 29.6 %copy.38 = f32[1,8,8,112,8,8]{5,4,3,2,1,0:T(8,128)} copy(f32[1,8,8,112,8,8]{4,5,1,2,3,0:T(8,128)} %fusion.1) | data formatting | bytes 3670016 | tf_op jit(solution)/shard_map/div | solution.py:76
  295.1 23.9 %div.35 = f32[64,7168]{1,0:T(8,128)} reshape(f32[1,8,8,112,8,8]{5,4,3,2,1,0:T(8,128)} %copy.38) | data formatting | bytes 3670016 | tf_op jit(solution)/shard_map/div | solution.py:76
  318.9 4.5 %convolution_bitcast_fusion = f32[1,64,7168]{2,1,0:T(8,128)} fusion(f32[64,7168]{1,0:T(8,128)} %div.35, f32[64]{0:T(128)S(1)} %get-tuple-element.15, f32[64]{0:T(128)S(1)} %get-tuple-element.14), kind=kOutput, calls=%fused_computation.9 | convolution fusion | flops 352333824 | bytes 3670528 | tf_op jit(solution)/shard_map/ka,rac->rkc/dot_general | solution.py:31
  323.5 2.7 reshape.216
  326.1 4.3 convolution_multiply_fusion
  330.5 2.7 mul.244
  333.2 0.0 copy-done.4
  333.2 2.6 subtract_convert_fusion
  335.8 0.0 all-gather.6.cloned.1.call-update
  335.9 1.5 reshape.211
  337.4 0.1 convert_reduce_fusion
  337.4 0.2 copy.30
  337.6 10.3 %broadcast_in_dim.34 = f32[8,8,112,8,8]{4,3,2,1,0:T(8,128)} broadcast(f32[8,112,8]{2,1,0:T(8,128)S(1)} %copy.30), dimensions={0,2,3} | broadcast | bytes 1863680 | tf_op jit(solution)/shard_map/broadcast_in_dim | solution.py:53
  347.9 24.3 %broadcast_in_dim.35 = f32[64,7168]{1,0:T(8,128)} reshape(f32[8,8,112,8,8]{4,3,2,1,0:T(8,128)} %broadcast_in_dim.34) | data formatting | bytes 3670016 | tf_op jit(solution)/shard_map/broadcast_in_dim | solution.py:53
  372.2 0.0 copy-done.2
  372.2 4.7 %convolution_bitcast_fusion.1 = f32[1,64,7168]{2,1,0:T(8,128)} fusion(f32[64,7168]{1,0:T(8,128)S(1)} %copy-done.2, f32[64,7168]{1,0:T(8,128)} %broadcast_in_dim.35, f32[64]{0:T(128)S(1)} %get-tuple-element.15, f32[64]{0:T(128)S(1)} %get-tuple-element.14), kind=kOutput, calls=%fused_computation.10 | convolution fusion | flops 352792576 | bytes 5505536 | tf_op jit(solution)/shard_map/ka,rac->rkc/dot_general | solution.py:31
  376.9 1.6 reshape.212
  378.5 2.8 fusion.38
  381.3 2.8 reshape.213
  384.2 3.0 fusion.20
  387.1 26.6 %all-gather.6.cloned.1.call-done = bf16[64,28672]{1,0:T(8,128)(2,1)} async-done(((bf16[64,7168]{1,0:T(8,128)(2,1)}), bf16[64,28672]{1,0:T(8,128)(2,1)}) %all-gather.6.cloned.1.call-update) | async-done | bytes 3670032 | tf_op jit(solution)/shard_map/all_gather | solution.py:80
  413.7 7.1 %fusion = bf16[128,28672]{0,1:T(8,128)(2,1)} fusion(bf16[64,28672]{1,0:T(8,128)(2,1)} %all-gather.6.cloned.1.call-done, bf16[128,64]{0,1:T(8,128)(2,1)S(1)} %copy-done), kind=kOutput, calls=%fused_computation.1 | convolution fusion | flops 473432064 | bytes 11026432 | tf_op jit(solution)/shard_map/dot_general | solution.py:78
  420.8 10.3 %copy.39 = bf16[128,28672]{1,0:T(8,128)(2,1)} copy(bf16[128,28672]{0,1:T(8,128)(2,1)} %fusion) | data formatting | bytes 14680064
  (10 shorter events, 0.0 us)
Async XLA Ops:
  7.2 406.5 %copy-start = (bf16[128,64]{0,1:T(8,128)(2,1)S(1)}, bf16[128,64]{0,1:T(8,128)(2,1)}, u32[]{:S(2)}) copy-start(bf16[128,64]{0,1:T(8,128)(2,1)} %param.8) | copy-start | bytes 49156
  7.2 165.4 %all-gather.4.cloned.1.call-start = ((), (), s32[]{:S(2)}) async-start(), calls=%async_computation | async-start | bytes 7454720 | tf_op jit(solution)/shard_map/all_gather | solution.py:65
  16.3 19.0 %copy-start.5 = (s32[1,1,112,4]{2,3,1,0:T(4,128)S(1)}, s32[1,1,112,4]{2,3,1,0:T(4,128)}, u32[]{:S(2)}) copy-start(s32[1,1,112,4]{2,3,1,0:T(4,128)} %param.9) | copy-start | bytes 5380
  57.9 355.8 %all-gather.6.cloned.1.call-start = ((), (), s32[]{:S(2)}) async-start(), calls=%async_computation.1 | async-start | bytes 4587520 | tf_op jit(solution)/shard_map/all_gather | solution.py:80
  330.5 2.8 copy-start.4
  347.9 24.3 %copy-start.2 = (f32[64,7168]{1,0:T(8,128)S(1)}, f32[64,7168]{1,0:T(8,128)}, u32[]{:S(2)}) copy-start(f32[64,7168]{1,0:T(8,128)} %reshape.211) | copy-start | bytes 5505028
  381.3 2.8 copy-start.1
  381.3 2.8 copy-start.3
Sparse Core Ops, SparseCore 0:
  58.0 114.5 all-gather.3
  336.0 77.6 all-gather.5
where the time goes:
time: 443 us; the launch traced here: 438 us
  local copies, waits for them, and re-layouts  158 us (36%)
  matrix products  119 us (27%)
  waiting for transfers between devices  69 us (16%)
  blocking collectives  67.8 us (15%)
  between operations  14.4 us (3%)
  other arithmetic  10.4 us (2%)
    dot_general x1, matrix products, on_device(): jnp.einsum('rxykij,rxykab->xiayjb', every_chosen, shaped_values, precisio...  68.8 us
    all_gather x1, blocking collectives, on_device(): lax.all_gather(flat_picked[None], 'dp', axis=0, tiled=True)  67.8 us
    div x2, local copies, waits for them, and re-layouts, on_device(): total_grid / replicas  53.5 us
    all_gather x1, waiting for transfers between devices, on_device(): lax.all_gather(values[None], 'dp', axis=0, tiled=True)  42.4 us
    broadcast_in_dim x3, local copies, waits for them, and re-layouts, on_device(): jnp.broadcast_to(small_mask[:, :, None, :, :, None], (group_rows, per_sid...  34.7 us
    another operation x2, local copies, waits for them, and re-layouts  34.3 us
    all_gather x1, waiting for transfers between devices, on_device(): lax.all_gather(new_weight, 'fsdp', axis=1, tiled=True)  26.6 us
    dot_general x1, matrix products, on_device(): jnp.einsum('xykij,xiayjb->xykab', chosen, shaped_coeffs, precision=exact)  19.8 us
  transfers between devices with their start and end apart: 2, of which 2 were waited for; matrix products, arithmetic and copies ran while one was open for 13% of the time, Pallas kernels for 0%

commit v1 on v0

v1 whole, which is shorter than its diff:
```python
import jax
import jax.numpy as jnp
import ml_dtypes
import numpy as np
from jax import lax
from jax.experimental import pallas as pl
from jax.experimental.pallas import tpu as pltpu
from jax.sharding import Mesh
from jax.sharding import PartitionSpec as P

GROUP = 64
BLOCK = 8
KEEP = 4
LANES = 128
ROWS = 16
DECAY = 0.9
STEP = 5.0
VMEM = 60 * 2**20
F32 = jnp.float32
BF16 = jnp.bfloat16
AXES = ("x", "y", "zl", "core", "fsdp")
SIZES = (4, 4, 2, 2)


def halves(table):
    high = table.astype(ml_dtypes.bfloat16)
    low = (table - high.astype(np.float64)).astype(ml_dtypes.bfloat16)
    return high, low


def cosine_table():
    position = np.arange(GROUP, dtype=np.float64)
    frequency = position[:, None]
    factor = np.where(frequency == 0, np.sqrt(1.0 / GROUP), np.sqrt(2.0 / GROUP))
    return factor * np.cos(np.pi * (2.0 * position[None, :] + 1.0) * frequency / (2.0 * GROUP))


def left_operand(table):
    high, low = halves(table)
    return np.concatenate([high, high, low, low], axis=1)


def right_operand(table):
    high, low = halves(np.kron(np.eye(LANES // GROUP), table))
    return np.block([[high, low], [high, low]])


def split(value):
    high = value.astype(BF16)
    return high, (value - high.astype(F32)).astype(BF16)


def mix_rows(operand, value):
    high, low = split(value)
    return jnp.dot(
        operand, jnp.concatenate([high, low, high, low], axis=0), preferred_element_type=F32
    )


def mix_columns(value, operand):
    high, low = split(value)
    both = jnp.dot(
        jnp.concatenate([high, low], axis=1), operand, preferred_element_type=F32
    )
    return both[:, :LANES] + both[:, LANES:]


def compress_kernel(
    first, tiles, place, picked, momentum, gradient, weight, row_fwd, col_fwd, row_inv, col_inv, *rest
):
    if first:
        new_momentum, sent, own_weight = rest
    else:
        _, new_momentum, sent = rest
    step = pl.program_id(0)
    core = place[2]
    half = (1 - core) if first else core
    moment = DECAY * momentum[0] + gradient[0].astype(F32)
    mixed = mix_rows(row_fwd[...], moment)
    stacked = jnp.concatenate(
        [mixed[:, t * LANES : (t + 1) * LANES] for t in range(tiles)], axis=0
    )
    coefficients = mix_columns(stacked, col_fwd[...])
    lane = lax.broadcasted_iota(jnp.int32, (BLOCK, LANES), 1)
    lane_block = (lane % GROUP) // BLOCK
    left_group = lane < GROUP
    row_block = lax.broadcasted_iota(jnp.int32, (GROUP // BLOCK, BLOCK, LANES), 0) * BLOCK
    start = (half * pl.num_programs(0) + step) * tiles * (LANES // GROUP)
    kept = []
    for t in range(tiles):
        mask = None
        for k in range(KEEP):
            wanted = jnp.where(
                left_group, picked[k, start + 2 * t], picked[k, start + 2 * t + 1]
            ) - lane_block
            hit = wanted[None] == row_block
            mask = hit if mask is None else mask | hit
        part = coefficients[t * GROUP : (t + 1) * GROUP].reshape(GROUP // BLOCK, BLOCK, LANES)
        kept.append(jnp.where(mask, part, 0.0).reshape(GROUP, LANES))
    unmixed = mix_columns(jnp.concatenate(kept, axis=0), col_inv[...])
    spread = jnp.concatenate(
        [unmixed[t * GROUP : (t + 1) * GROUP] for t in range(tiles)], axis=1
    )
    transmitted = mix_rows(row_inv[...], spread)
    new_momentum[0] = moment - transmitted
    for i in range(GROUP // ROWS):
        for t in range(tiles):
            sent[i, 0, t] = transmitted[i * ROWS : (i + 1) * ROWS, t * LANES : (t + 1) * LANES]
    if first:

        @pl.when(step == 0)
        def _():
            for t in range(tiles):
                own_weight[t] = weight[:, t * LANES : (t + 1) * LANES].astype(F32)


def compress(first, place, picked, momentum, gradient, weight, tables, partial=None):
    height, breadth = weight.shape
    steps = SIZES[1]
    wide = breadth // 2 // steps
    tiles = wide // LANES
    chunk = (tiles, ROWS, LANES)

    def columns(i, place, picked):
        half = (1 - place[2]) if first else place[2]
        return (0, 0, half * steps + i)

    fixed = lambda i, place, picked: (0, 0)
    slab = pl.BlockSpec((1, height, wide), columns)
    in_specs = [
        slab,
        slab,
        pl.BlockSpec((ROWS, wide), lambda i, place, picked: (place[0], place[2] * steps + place[1])),
    ] + [pl.BlockSpec(table.shape, fixed) for table in tables]
    out_shape = [
        jax.ShapeDtypeStruct((1, height, breadth), F32),
        jax.ShapeDtypeStruct((SIZES[0], steps) + chunk, F32),
    ]
    out_specs = [
        slab,
        pl.BlockSpec((SIZES[0], 1) + chunk, lambda i, place, picked: (0, i, 0, 0, 0)),
    ]
    operands = [place, picked, momentum, gradient, weight, *tables]
    aliases = {}
    if first:
        out_shape.append(jax.ShapeDtypeStruct(chunk, F32))
        out_specs.append(pl.BlockSpec(chunk, lambda i, place, picked: (0, 0, 0)))
    else:
        aliases = {len(operands): 0}
        operands.append(partial)
        in_specs.append(pl.BlockSpec(memory_space=pl.ANY))

    def body(*refs):
        compress_kernel(first, tiles, *refs)

    return pl.pallas_call(
        body,
        grid_spec=pltpu.PrefetchScalarGridSpec(
            num_scalar_prefetch=2, grid=(steps,), in_specs=in_specs, out_specs=out_specs
        ),
        out_shape=out_shape,
        input_output_aliases=aliases,
        compiler_params=pltpu.CompilerParams(vmem_limit_bytes=VMEM),
        cost_estimate=pl.CostEstimate(
            flops=2 * 4 * 256 * height * breadth, bytes_accessed=6 * height * breadth, transcendentals=0
        ),
        name="compress_first" if first else "compress_second",
    )(*operands)


def project(first, place, tokens, pieces, breadth, partial=None):
    count, depth = tokens.shape
    _, side, shifts, tiles, rows, lanes = pieces.shape
    wide = tiles * lanes

    def out_columns(k, place):
        half = place[2] if first else 1 - place[2]
        return (0, lax.rem(place[3] - k + shifts, shifts) * 2 + half)

    def body(place, tokens, pieces, *rest):
        out = rest[-1]
        for j in range(side):
            table = jnp.concatenate(
                [pieces[:, j, 0, t].reshape(depth, lanes) for t in range(tiles)], axis=1
            )
            out[:, j * wide : (j + 1) * wide] = jnp.dot(
                tokens[...], table, preferred_element_type=F32
            ).astype(BF16)

    in_specs = [
        pl.BlockSpec((count, depth), lambda k, place: (0, 0)),
        pl.BlockSpec((SIZES[0], side, 1, tiles, rows, lanes), lambda k, place: (0, 0, k, 0, 0, 0)),
    ]
    operands = [place, tokens, pieces]
    aliases = {}
    if not first:
        aliases = {3: 0}
        operands.append(partial)
        in_specs.append(pl.BlockSpec(memory_space=pl.ANY))
    return pl.pallas_call(
        body,
        grid_spec=pltpu.PrefetchScalarGridSpec(
            num_scalar_prefetch=1,
            grid=(shifts,),
            in_specs=in_specs,
            out_specs=pl.BlockSpec((count, side * wide), out_columns),
        ),
        out_shape=jax.ShapeDtypeStruct((count, breadth), BF16),
        input_output_aliases=aliases,
        compiler_params=pltpu.CompilerParams(vmem_limit_bytes=VMEM),
        cost_estimate=pl.CostEstimate(
            flops=count * depth * breadth, bytes_accessed=count * breadth, transcendentals=0
        ),
        name="project_first" if first else "project_second",
    )(*operands)


def shift(value, axis, size, by):
    return lax.ppermute(value, axis, [(i, (i + by) % size) for i in range(size)])


def on_device(momentum, gradient, weight, tokens, block_index):
    fsdp = lax.axis_size("fsdp")
    breadth = weight.shape[1]
    place = jnp.stack([lax.axis_index(a) for a in ("x", "y", "core", "fsdp")]).astype(jnp.int32)
    picked = block_index[0, 0].T
    cosines = cosine_table()
    tables = [
        jnp.asarray(left_operand(cosines)),
        jnp.asarray(right_operand(cosines.T)),
        jnp.asarray(left_operand(cosines.T)),
        jnp.asarray(right_operand(cosines)),
    ]
    partial, away, own_weight = compress(True, place, picked, momentum, gradient, weight, tables)
    arrived = shift(away, "core", 2, 1)
    new_momentum, kept = compress(
        False, place, picked, momentum, gradient, weight, tables, partial
    )
    pair = (kept + arrived).astype(BF16)
    plane = SIZES[0] * SIZES[1]
    pair = pair.reshape((plane,) + pair.shape[2:])
    parts = lax.all_to_all(pair, ("x", "y"), 0, 0, tiled=True)
    summed = jnp.sum(parts.astype(F32), axis=0)
    total = summed + shift(summed, "zl", 2, 1)
    replicas = float(np.prod(SIZES))
    chunk = (own_weight - (STEP / replicas) * total).astype(BF16)
    row = jnp.stack([chunk] + [shift(chunk, "fsdp", fsdp, k) for k in range(1, fsdp)])
    pieces = lax.all_to_all(
        jnp.broadcast_to(row[None], (plane,) + row.shape), ("x", "y"), 0, 0, tiled=True
    ).reshape(SIZES[:2] + row.shape)
    others = shift(pieces, "core", 2, 1)
    half = project(True, place, tokens, pieces, fsdp * breadth)
    preact = project(False, place, tokens, others, fsdp * breadth, half)
    return new_momentum, preact


def solution(mesh):
    split_mesh = Mesh(mesh.devices.reshape(SIZES + mesh.devices.shape[1:]), AXES)
    dp = AXES[:4]
    return jax.shard_map(
        on_device,
        mesh=split_mesh,
        in_specs=(
            P(dp, None, "fsdp"),
            P(dp, None, "fsdp"),
            P(None, "fsdp"),
            P(dp + ("fsdp",), None),
            P(dp, None, "fsdp", None),
        ),
        out_specs=(P(dp, None, "fsdp"), P(dp + ("fsdp",), None)),
        check_vma=False,
    )
```

time: 443 us -> 91.1 us (0.21)
  the two profiles are of different devices: /device:TPU:35 before, /device:TPU:1 now
where the time goes in v1:
time: 91.1 us; the launch traced here: 90.5 us
  blocking collectives  39 us (43%)
  Pallas kernels  22.8 us (25%)
  starting transfers between devices  19.8 us (22%)
  waiting for transfers between devices  5.05 us (6%)
  other arithmetic  2.01 us (2%)
  local copies, waits for them, and re-layouts  1.11 us (1%)
    all_to_all x1, blocking collectives, on_device(): lax.all_to_all(jnp.broadcast_to(row[None], (plane,) + row.shape), ('x', '...  24.6 us
    ppermute x6, starting transfers between devices, shift(): lax.ppermute(value, axis, [(i, (i + by) % size) for i in range(size)])  19.8 us
    all_to_all x1, blocking collectives, on_device(): parts = lax.all_to_all(pair, ('x', 'y'), 0, 0, tiled=True)  14.4 us
    pallas_call x2, Pallas kernels, compress(): pl.pallas_call(body, grid_spec=pltpu.PrefetchScalarGridSpec(num_scalar_pr...  12.1 us
    pallas_call x2, Pallas kernels, project(): pl.pallas_call(body, grid_spec=pltpu.PrefetchScalarGridSpec(num_scalar_pr...  10.7 us
    ppermute x6, waiting for transfers between devices, shift(): lax.ppermute(value, axis, [(i, (i + by) % size) for i in range(size)])  5.05 us
  transfers between devices with their start and end apart: 6, of which 2 were waited for; matrix products, arithmetic and copies ran while one was open for 1% of the time, Pallas kernels for 13%

profile of v1, /device:TPU:1, one launch (start us, length us, event | category | flops | bytes accessed | tf_op | source)
XLA Modules:
  0.0 90.5 jit_solution(18224877627014531907)
XLA Ops:
  0.6 0.6 pad_add_fusion.refs_0_.place
  1.2 6.1 %compress_first.1 = (f32[1,64,7168]{2,1,0:T(8,128)}, f32[4,4,7,16,128]{4,3,2,1,0:T(8,128)}, f32[7,16,128]{2,1,0:T(8,128)}) custom-call(s32[4]{0:T(128)} %pad_add_fusion.refs_0_.place, s32[4,112]{1,0:T(4,128)} %bitcast.20, f32[1,64,7168]{2,1,0:T(8,128)} %refs_2_.3, bf16[1,64,7168]{2,1,0:T(8,128)(2,1)} %refs_3_.3, bf16[64,7168]{1,0:T(8,128)(2,1)} %refs_4_.3, ...), custom_call_target="tpu_custom_call" | custom-call | flops 939524096 | bytes 2752512 | tf_op jit(solution)/shard_map/compress_first/pallas_call | solution.py:156
  7.3 3.3 %collective-permute-start = (f32[4,4,7,16,128]{4,3,2,1,0:T(8,128)}, f32[4,4,7,16,128]{4,3,2,1,0:T(8,128)S(1)}, u32[]{:S(2)}, u32[]{:S(2)}) collective-permute-start(f32[4,4,7,16,128]{4,3,2,1,0:T(8,128)} %get-tuple-element.11), channel_id=1, source_target_pairs={{0,4},{4,0},{1,5},{5,1},{2,6},{6,2},{3,7},{7,3},{8,12},{12,8},{9,1... | collective-permute-start | bytes 2752520 | tf_op jit(solution)/shard_map/ppermute | solution.py:219
  10.6 6.0 %compress_second.1 = (f32[1,64,7168]{2,1,0:T(8,128)}, f32[4,4,7,16,128]{4,3,2,1,0:T(8,128)}) custom-call(s32[4]{0:T(128)} %pad_add_fusion.refs_0_.place, s32[4,112]{1,0:T(4,128)} %bitcast.21, f32[1,64,7168]{2,1,0:T(8,128)} %refs_2_.3, bf16[1,64,7168]{2,1,0:T(8,128)(2,1)} %refs_3_.3, bf16[64,7168]{1,0:T(8,128)(2,1)} %refs_4_.3, ...), custom_call_target="tpu_custom_call", output_to_operand_aliasing={{0}: (9, {})} | custom-call | flops 939524096 | bytes 2752512 | tf_op jit(solution)/shard_map/compress_second/pallas_call | solution.py:156
  16.7 0.0 collective-permute-done
  16.7 0.0 copy-start.1
  16.7 1.3 %add_convert_fusion = bf16[4,4,7,16,128]{4,3,2,1,0:T(8,128)(2,1)S(1)} fusion(f32[4,4,7,16,128]{4,3,2,1,0:T(8,128)} %get-tuple-element.10, f32[4,4,7,16,128]{4,3,2,1,0:T(8,128)S(1)} %collective-permute-done), kind=kLoop, calls=%fused_computation.1 | loop fusion | flops 458752 | bytes 2293760 | tf_op jit(solution)/shard_map/convert_element_type | solution.py:239
  18.0 14.4 %all_to_all.10 = bf16[16,7,16,128]{3,2,1,0:T(8,128)(2,1)S(1)} all-to-all(bf16[16,7,16,128]{3,2,1,0:T(8,128)(2,1)S(1)} %bitcast.15), channel_id=1, replica_groups=mesh['x'=4,'y'=4,'zl'=2,'core'=2,'fsdp'=4] {'x','y'}, dimensions={0} | all-to-all | bytes 917504 | tf_op jit(solution)/shard_map/all_to_all | solution.py:242
  32.4 0.1 convert_reduce_fusion
  32.5 1.7 %collective-permute-start.1 = (f32[7,16,128]{2,1,0:T(8,128)S(1)}, f32[7,16,128]{2,1,0:T(8,128)S(1)}, u32[]{:S(2)}, u32[]{:S(2)}) collective-permute-start(f32[7,16,128]{2,1,0:T(8,128)S(1)} %convert_reduce_fusion), channel_id=1, source_target_pairs={{0,8},{8,0},{1,9},{9,1},{2,10},{10,2},{3,11},{11,3},{4,12},{12,4},... | collective-permute-start | bytes 172040 | tf_op jit(solution)/shard_map/ppermute | solution.py:219
  34.2 1.6 %collective-permute-done.1 = f32[7,16,128]{2,1,0:T(8,128)S(1)} collective-permute-done((f32[7,16,128]{2,1,0:T(8,128)S(1)}, f32[7,16,128]{2,1,0:T(8,128)S(1)}, u32[]{:S(2)}, u32[]{:S(2)}) %collective-permute-start.1) | collective-permute-done | bytes 57376 | tf_op jit(solution)/shard_map/ppermute | solution.py:219
  35.8 0.0 copy-done.1
  35.8 5.9 %collective-permute-start.4 = (bf16[7,16,128]{2,1,0:T(8,128)(2,1)S(1)}, bf16[7,16,128]{2,1,0:T(8,128)(2,1)S(1)}, u32[]{:S(2)}, u32[]{:S(2)}) collective-permute-start(bf16[7,16,128]{2,1,0:T(8,128)(2,1)S(1)} %subtract_convert_fusion), channel_id=1, source_target_pairs={{0,3},{1,0},{2,1},{3,2},{4,7},{5,4},{6,5},{7,6},{8,11},{9,8},{10,9... | collective-permute-start | bytes 86024 | tf_op jit(solution)/shard_map/ppermute | solution.py:219
  41.7 1.0 %collective-permute-start.3 = (bf16[7,16,128]{2,1,0:T(8,128)(2,1)S(1)}, bf16[7,16,128]{2,1,0:T(8,128)(2,1)S(1)}, u32[]{:S(2)}, u32[]{:S(2)}) collective-permute-start(bf16[7,16,128]{2,1,0:T(8,128)(2,1)S(1)} %subtract_convert_fusion), channel_id=1, source_target_pairs={{0,2},{1,3},{2,0},{3,1},{4,6},{5,7},{6,4},{7,5},{8,10},{9,11},{10,... | collective-permute-start | bytes 86024 | tf_op jit(solution)/shard_map/ppermute | solution.py:219
  42.7 2.3 %collective-permute-start.2 = (bf16[7,16,128]{2,1,0:T(8,128)(2,1)S(1)}, bf16[7,16,128]{2,1,0:T(8,128)(2,1)S(1)}, u32[]{:S(2)}, u32[]{:S(2)}) collective-permute-start(bf16[7,16,128]{2,1,0:T(8,128)(2,1)S(1)} %subtract_convert_fusion), channel_id=1, source_target_pairs={{0,1},{1,2},{2,3},{3,0},{4,5},{5,6},{6,7},{7,4},{8,9},{9,10},{10,1... | collective-permute-start | bytes 86024 | tf_op jit(solution)/shard_map/ppermute | solution.py:219
  45.0 0.0 collective-permute-done.4
  45.0 3.5 %collective-permute-done.3 = bf16[7,16,128]{2,1,0:T(8,128)(2,1)S(1)} collective-permute-done((bf16[7,16,128]{2,1,0:T(8,128)(2,1)S(1)}, bf16[7,16,128]{2,1,0:T(8,128)(2,1)S(1)}, u32[]{:S(2)}, u32[]{:S(2)}) %collective-permute-start.3) | collective-permute-done | bytes 28704 | tf_op jit(solution)/shard_map/ppermute | solution.py:219
  48.4 0.0 collective-permute-done.2
  48.5 0.4 broadcast_in_dim.2
  48.9 0.0 copy-start.2
  48.9 24.6 %all_to_all.11 = bf16[16,4,7,16,128]{4,3,2,1,0:T(8,128)(2,1)S(1)} all-to-all(bf16[16,4,7,16,128]{4,3,2,1,0:T(8,128)(2,1)S(1)} %broadcast_in_dim.2), channel_id=1, replica_groups=mesh['x'=4,'y'=4,'zl'=2,'core'=2,'fsdp'=4] {'x','y'}, dimensions={0} | all-to-all | bytes 3670016 | tf_op jit(solution)/shard_map/all_to_all | solution.py:248
  73.5 0.0 copy-start
  73.5 5.6 %collective-permute-start.5 = (bf16[4,4,4,7,16,128]{5,4,3,2,1,0:T(8,128)(2,1)S(1)}, bf16[4,4,4,7,16,128]{5,4,3,2,1,0:T(8,128)(2,1)}, u32[]{:S(2)}, u32[]{:S(2)}) collective-permute-start(bf16[4,4,4,7,16,128]{5,4,3,2,1,0:T(8,128)(2,1)S(1)} %bitcast.13), channel_id=1, source_target_pairs={{0,4},{4,0},{1,5},{5,1},{2,6},{6,2},{3,7},{7,3},{8,12},{12,8},{9,1... | collective-permute-start | bytes 5505032 | tf_op jit(solution)/shard_map/ppermute | solution.py:219
  79.1 0.0 copy-done.2
  79.1 0.7 copy.14.tokens
  79.8 0.0 copy-done
  79.8 5.4 %project_first.1.rest_0_ = bf16[128,28672]{1,0:T(8,128)(2,1)} custom-call(s32[4]{0:T(128)} %pad_add_fusion.refs_0_.place, bf16[128,64]{1,0:T(8,128)(2,1)} %copy.14.tokens, bf16[4,4,4,7,16,128]{5,4,3,2,1,0:T(8,128)(2,1)} %bitcast.14), custom_call_target="tpu_custom_call" | custom-call | flops 234881024 | bytes 3670016 | tf_op jit(solution)/shard_map/project_first/pallas_call | solution.py:200
  85.2 0.0 collective-permute-done.5.pieces
  85.2 5.4 %project_second.1 = bf16[128,28672]{1,0:T(8,128)(2,1)} custom-call(s32[4]{0:T(128)} %pad_add_fusion.refs_0_.place, bf16[128,64]{1,0:T(8,128)(2,1)} %copy.14.tokens, bf16[4,4,4,7,16,128]{5,4,3,2,1,0:T(8,128)(2,1)} %collective-permute-done.5.pieces, bf16[128,28672]{1,0:T(8,128)(2,1)} %project_first.1.rest_0_), custom_call_target="tpu_custom_call", output_to_operand_aliasing={{}: (3, {})} | custom-call | flops 234881024 | bytes 3670016 | tf_op jit(solution)/shard_map/project_second/pallas_call | solution.py:200
  (2 shorter events, 0.0 us)
Async XLA Ops:
  7.3 9.4 %collective-permute-start = (f32[4,4,7,16,128]{4,3,2,1,0:T(8,128)}, f32[4,4,7,16,128]{4,3,2,1,0:T(8,128)S(1)}, u32[]{:S(2)}, u32[]{:S(2)}) collective-permute-start(f32[4,4,7,16,128]{4,3,2,1,0:T(8,128)} %get-tuple-element.11), channel_id=1, source_target_pairs={{0,4},{4,0},{1,5},{5,1},{2,6},{6,2},{3,7},{7,3},{8,12},{12,8},{9,1... | collective-permute-start | bytes 2752520 | tf_op jit(solution)/shard_map/ppermute | solution.py:219
  16.7 19.1 %copy-start.1 = (f32[7,16,128]{2,1,0:T(8,128)S(1)}, f32[7,16,128]{2,1,0:T(8,128)}, u32[]{:S(2)}) copy-start(f32[7,16,128]{2,1,0:T(8,128)} %get-tuple-element.9) | copy-start | bytes 172036
  32.5 3.3 %collective-permute-start.1 = (f32[7,16,128]{2,1,0:T(8,128)S(1)}, f32[7,16,128]{2,1,0:T(8,128)S(1)}, u32[]{:S(2)}, u32[]{:S(2)}) collective-permute-start(f32[7,16,128]{2,1,0:T(8,128)S(1)} %convert_reduce_fusion), channel_id=1, source_target_pairs={{0,8},{8,0},{1,9},{9,1},{2,10},{10,2},{3,11},{11,3},{4,12},{12,4},... | collective-permute-start | bytes 172040 | tf_op jit(solution)/shard_map/ppermute | solution.py:219
  35.8 9.2 %collective-permute-start.4 = (bf16[7,16,128]{2,1,0:T(8,128)(2,1)S(1)}, bf16[7,16,128]{2,1,0:T(8,128)(2,1)S(1)}, u32[]{:S(2)}, u32[]{:S(2)}) collective-permute-start(bf16[7,16,128]{2,1,0:T(8,128)(2,1)S(1)} %subtract_convert_fusion), channel_id=1, source_target_pairs={{0,3},{1,0},{2,1},{3,2},{4,7},{5,4},{6,5},{7,6},{8,11},{9,8},{10,9... | collective-permute-start | bytes 86024 | tf_op jit(solution)/shard_map/ppermute | solution.py:219
  41.7 6.7 %collective-permute-start.3 = (bf16[7,16,128]{2,1,0:T(8,128)(2,1)S(1)}, bf16[7,16,128]{2,1,0:T(8,128)(2,1)S(1)}, u32[]{:S(2)}, u32[]{:S(2)}) collective-permute-start(bf16[7,16,128]{2,1,0:T(8,128)(2,1)S(1)} %subtract_convert_fusion), channel_id=1, source_target_pairs={{0,2},{1,3},{2,0},{3,1},{4,6},{5,7},{6,4},{7,5},{8,10},{9,11},{10,... | collective-permute-start | bytes 86024 | tf_op jit(solution)/shard_map/ppermute | solution.py:219
  42.7 5.7 %collective-permute-start.2 = (bf16[7,16,128]{2,1,0:T(8,128)(2,1)S(1)}, bf16[7,16,128]{2,1,0:T(8,128)(2,1)S(1)}, u32[]{:S(2)}, u32[]{:S(2)}) collective-permute-start(bf16[7,16,128]{2,1,0:T(8,128)(2,1)S(1)} %subtract_convert_fusion), channel_id=1, source_target_pairs={{0,1},{1,2},{2,3},{3,0},{4,5},{5,6},{6,7},{7,4},{8,9},{9,10},{10,1... | collective-permute-start | bytes 86024 | tf_op jit(solution)/shard_map/ppermute | solution.py:219
  48.9 30.2 %copy-start.2 = (bf16[128,64]{0,1:T(8,128)(2,1)S(1)}, bf16[128,64]{0,1:T(8,128)(2,1)}, u32[]{:S(2)}) copy-start(bf16[128,64]{0,1:T(8,128)(2,1)} %param.12) | copy-start | bytes 49156
  73.5 6.3 %copy-start = (bf16[16,4,7,16,128]{4,3,2,1,0:T(8,128)(2,1)}, bf16[16,4,7,16,128]{4,3,2,1,0:T(8,128)(2,1)S(1)}, u32[]{:S(2)}) copy-start(bf16[16,4,7,16,128]{4,3,2,1,0:T(8,128)(2,1)S(1)} %all_to_all.11) | copy-start | bytes 5505028
  73.5 11.7 %collective-permute-start.5 = (bf16[4,4,4,7,16,128]{5,4,3,2,1,0:T(8,128)(2,1)S(1)}, bf16[4,4,4,7,16,128]{5,4,3,2,1,0:T(8,128)(2,1)}, u32[]{:S(2)}, u32[]{:S(2)}) collective-permute-start(bf16[4,4,4,7,16,128]{5,4,3,2,1,0:T(8,128)(2,1)S(1)} %bitcast.13), channel_id=1, source_target_pairs={{0,4},{4,0},{1,5},{5,1},{2,6},{6,2},{3,7},{7,3},{8,12},{12,8},{9,1... | collective-permute-start | bytes 5505032 | tf_op jit(solution)/shard_map/ppermute | solution.py:219

commit v2 on v1

v2 whole, which is shorter than its diff:
```python
import jax
import jax.numpy as jnp
import ml_dtypes
import numpy as np
from jax import lax
from jax.experimental import pallas as pl
from jax.experimental.pallas import tpu as pltpu
from jax.sharding import Mesh
from jax.sharding import PartitionSpec as P

GROUP = 64
BLOCK = 8
KEEP = 4
LANES = 128
BATCHES = (0, 2, 4)
ROWS = 16
DECAY = 0.9
STEP = 5.0
F32 = jnp.float32
BF16 = jnp.bfloat16
AXES = ("x", "y", "zl", "core", "fsdp")
SIZES = (4, 4, 2, 2)


def halves(table):
    high = table.astype(ml_dtypes.bfloat16)
    low = (table - high.astype(np.float64)).astype(ml_dtypes.bfloat16)
    return high, low


def cosine_table():
    position = np.arange(GROUP, dtype=np.float64)
    frequency = position[:, None]
    factor = np.where(frequency == 0, np.sqrt(1.0 / GROUP), np.sqrt(2.0 / GROUP))
    return factor * np.cos(np.pi * (2.0 * position[None, :] + 1.0) * frequency / (2.0 * GROUP))


def left_operand(table):
    high, low = halves(table)
    return np.concatenate([high, high, low, low], axis=1)


def right_operand(table):
    high, low = halves(np.kron(np.eye(LANES // GROUP), table))
    return np.block([[high, low], [high, low]])


def split(value):
    high = value.astype(BF16)
    return high, (value - high.astype(F32)).astype(BF16)


def mix_rows(operand, value):
    high, low = split(value)
    return jnp.dot(
        operand, jnp.concatenate([high, low, high, low], axis=0), preferred_element_type=F32
    )


def mix_columns(value, operand):
    high, low = split(value)
    both = jnp.dot(
        jnp.concatenate([high, low], axis=1), operand, preferred_element_type=F32
    )
    return both[:, :LANES] + both[:, LANES:]


def whereabouts():
    x, y, core, shard = (lax.axis_index(a) for a in ("x", "y", "core", "fsdp"))
    return jnp.where(core == 0, x, y), jnp.where(core == 0, y, x), core, shard


def compress_kernel(first, tiles, steps, index, momentum, gradient, weight, *rest):
    place = whereabouts()
    operands, rest = rest[:4], rest[4:]
    if first:
        new_momentum, sent, own_weight = rest[:3]
    else:
        new_momentum, sent = rest[1:3]
    moment_buf, grad_buf, new_buf, weight_buf, *rest = rest[3:]
    tables, (in_sems, out_sems, table_sems, sent_buf, sent_sems, picked) = rest[:4], rest[4:]
    wide = tiles * LANES
    core = place[2]
    half = (1 - core) if first else core

    spans = [slice(a * wide, b * wide) for a, b in zip(BATCHES, BATCHES[1:])]

    def columns(span):
        return pl.ds(
            pl.multiple_of(half * steps * wide + span.start, LANES), span.stop - span.start
        )

    loads = [
        (
            pltpu.make_async_copy(
                momentum.at[0, :, columns(span)], moment_buf.at[:, span], in_sems.at[n, 0]
            ),
            pltpu.make_async_copy(
                gradient.at[0, :, columns(span)], grad_buf.at[:, span], in_sems.at[n, 1]
            ),
        )
        for n, span in enumerate(spans)
    ]
    table_loads = [
        pltpu.make_async_copy(operands[n], tables[n], table_sems.at[n]) for n in range(4)
    ]
    index_load = pltpu.make_async_copy(index, picked, table_sems.at[5])
    for copy in (*loads[0], index_load, *table_loads, *(copy for pair in loads[1:] for copy in pair)):
        copy.start()
    if first:
        at = pl.multiple_of((core * steps + place[1]) * wide, wide)
        row = pl.multiple_of(place[0] * ROWS, ROWS)
        weight_load = pltpu.make_async_copy(
            weight.at[pl.ds(row, ROWS), pl.ds(at, wide)], weight_buf, table_sems.at[4]
        )
        weight_load.start()
    lane = lax.broadcasted_iota(jnp.int32, (BLOCK, LANES), 1)
    lane_block = (lane % GROUP) // BLOCK
    left_group = lane < GROUP
    row_block = lax.broadcasted_iota(jnp.int32, (GROUP // BLOCK, BLOCK, LANES), 0) * BLOCK
    stores = []
    for n, span in enumerate(spans):
        for copy in loads[n]:
            copy.wait()
        if n == 0:
            for copy in (index_load, *table_loads):
                copy.wait()
        row_fwd, col_fwd, row_inv, col_inv = tables
        count = (span.stop - span.start) // LANES
        moment = DECAY * moment_buf[:, span] + grad_buf[:, span].astype(F32)
        mixed = mix_rows(row_fwd[...], moment)
        stacked = jnp.concatenate(
            [mixed[:, t * LANES : (t + 1) * LANES] for t in range(count)], axis=0
        )
        coefficients = mix_columns(stacked, col_fwd[...])
        start = half * steps * tiles * (LANES // GROUP) + span.start // GROUP
        kept = []
        for t in range(count):
            mask = None
            for k in range(KEEP):
                wanted = jnp.where(
                    left_group, picked[k, start + 2 * t], picked[k, start + 2 * t + 1]
                ) - lane_block
                hit = wanted[None] == row_block
                mask = hit if mask is None else mask | hit
            part = coefficients[t * GROUP : (t + 1) * GROUP].reshape(GROUP // BLOCK, BLOCK, LANES)
            kept.append(jnp.where(mask, part, 0.0).reshape(GROUP, LANES))
        unmixed = mix_columns(jnp.concatenate(kept, axis=0), col_inv[...])
        spread = jnp.concatenate(
            [unmixed[t * GROUP : (t + 1) * GROUP] for t in range(count)], axis=1
        )
        transmitted = mix_rows(row_inv[...], spread)
        new_buf[:, span] = moment - transmitted
        store = pltpu.make_async_copy(
            new_buf.at[:, span], new_momentum.at[0, :, columns(span)], out_sems.at[n]
        )
        store.start()
        stores.append(store)
        for j in range(span.start // wide, span.stop // wide):
            for i in range(GROUP // ROWS):
                outer = jnp.where(half == 0, i, j)
                inner = jnp.where(half == 0, j, i)
                for t in range(tiles):
                    at = j * wide + t * LANES - span.start
                    sent_buf[j, i, t] = transmitted[i * ROWS : (i + 1) * ROWS, at : at + LANES]
                store = pltpu.make_async_copy(
                    sent_buf.at[j, i], sent.at[outer, inner], sent_sems.at[j, i]
                )
                store.start()
                stores.append(store)
    if first:
        weight_load.wait()
        for t in range(tiles):
            own_weight[t] = weight_buf[:, t * LANES : (t + 1) * LANES].astype(F32)
    for store in stores:
        store.wait()


def compress(first, picked, momentum, gradient, weight, tables, partial=None):
    height, breadth = weight.shape
    steps = SIZES[1]
    wide = breadth // 2 // steps
    tiles = wide // LANES
    chunk = (tiles, ROWS, LANES)
    in_specs = [pl.BlockSpec(memory_space=pltpu.HBM)] * (4 + len(tables))
    out_shape = [
        jax.ShapeDtypeStruct((1, height, breadth), F32),
        jax.ShapeDtypeStruct((SIZES[0], steps) + chunk, F32),
    ]
    out_specs = [pl.BlockSpec(memory_space=pltpu.HBM)] * 2
    operands = [picked, momentum, gradient, weight, *tables]
    aliases = {}
    if first:
        out_shape.append(jax.ShapeDtypeStruct(chunk, F32))
        out_specs.append(pl.BlockSpec(memory_space=pltpu.VMEM))
    else:
        aliases = {len(operands): 0}
        operands.append(partial)
        in_specs.append(pl.BlockSpec(memory_space=pltpu.HBM))

    def body(*refs):
        compress_kernel(first, tiles, steps, *refs)

    return pl.pallas_call(
        body,
        in_specs=in_specs,
        out_specs=out_specs,
        out_shape=out_shape,
        scratch_shapes=[
            pltpu.VMEM((height, steps * wide), F32),
            pltpu.VMEM((height, steps * wide), BF16),
            pltpu.VMEM((height, steps * wide), F32),
            pltpu.VMEM((ROWS, wide), BF16),
            *(pltpu.VMEM(table.shape, BF16) for table in tables),
            pltpu.SemaphoreType.DMA((steps, 2)),
            pltpu.SemaphoreType.DMA((steps,)),
            pltpu.SemaphoreType.DMA((6,)),
            pltpu.VMEM((steps, SIZES[0]) + chunk, F32),
            pltpu.SemaphoreType.DMA((steps, SIZES[0])),
            pltpu.SMEM(picked.shape, jnp.int32),
        ],
        input_output_aliases=aliases,
        compiler_params=pltpu.CompilerParams(vmem_limit_bytes=60 * 2**20),
        cost_estimate=pl.CostEstimate(
            flops=2 * 4 * 256 * height * breadth, bytes_accessed=6 * height * breadth, transcendentals=0
        ),
        name="compress_first" if first else "compress_second",
    )(*operands)


def project(tokens, pieces, own, steps, shards, breadth, partial=None):
    count, depth = tokens.shape
    _, side, tiles, rows, lanes = pieces[0].shape
    wide = tiles * lanes
    number = len(pieces)
    slots = sum(len(held) for held in shards)

    def body(tokens, *rest):
        place = whereabouts()
        arrays, (out, held, sems) = rest[:number], rest[-3:]
        turn_of, start = (place[0], place[1]) if own else (place[1], place[0])
        half = place[2] if own else 1 - place[2]
        order = [lax.rem(turn_of - i + side, side) for i in range(side)]
        copies = []
        for n in range(number):
            at = half * side + lax.rem(start - steps[n] + side, side)
            for k, shard in enumerate(shards[n]):
                slot = len(copies)
                table = jnp.concatenate(
                    [
                        jnp.concatenate([arrays[n][k, order[i], t] for i in range(side)], axis=0)
                        for t in range(tiles)
                    ],
                    axis=1,
                )
                held[slot] = jnp.dot(
                    tokens[...], table, preferred_element_type=F32
                ).astype(BF16)
                column = pl.multiple_of(((place[3] ^ shard) * 2 * side + at) * wide, wide)
                copy = pltpu.make_async_copy(
                    held.at[slot], out.at[:, pl.ds(column, wide)], sems.at[slot]
                )
                copy.start()
                copies.append(copy)
        for copy in copies:
            copy.wait()

    operands = [tokens, *pieces]
    in_specs = [pl.BlockSpec(memory_space=pltpu.VMEM)] * (1 + number)
    aliases = {}
    if partial is not None:
        aliases = {len(operands): 0}
        operands.append(partial)
        in_specs.append(pl.BlockSpec(memory_space=pltpu.HBM))
    return pl.pallas_call(
        body,
        in_specs=in_specs,
        out_specs=pl.BlockSpec(memory_space=pltpu.HBM),
        out_shape=jax.ShapeDtypeStruct((count, breadth), BF16),
        scratch_shapes=[
            pltpu.VMEM((slots, count, wide), BF16),
            pltpu.SemaphoreType.DMA((slots,)),
        ],
        input_output_aliases=aliases,
        compiler_params=pltpu.CompilerParams(vmem_limit_bytes=16 * 2**20),
        cost_estimate=pl.CostEstimate(
            flops=2 * count * depth * wide * slots,
            bytes_accessed=30 * 2**20 * number,
            transcendentals=0,
        ),
        name="project",
    )(*operands)


def after(preact, *values):
    def body(*refs):
        pass

    spaces = [pltpu.VMEM] * len(values) + [pltpu.HBM]
    operands = (*values, preact)
    return pl.pallas_call(
        body,
        in_specs=[pl.BlockSpec(memory_space=space) for space in spaces],
        out_specs=[pl.BlockSpec(memory_space=space) for space in spaces],
        out_shape=[jax.ShapeDtypeStruct(v.shape, v.dtype) for v in operands],
        input_output_aliases={n: n for n in range(len(operands))},
        compiler_params=pltpu.CompilerParams(vmem_limit_bytes=16 * 2**20),
        name="after",
    )(*operands)


def shift(value, axis, size, by):
    return lax.ppermute(value, axis, [(i, (i + by) % size) for i in range(size)])


def flip(value, axis, size, mask):
    return lax.ppermute(value, axis, [(i, i ^ mask) for i in range(size)])


def turn(value, by, late):
    rows, cols, _, cores = SIZES
    pairs = []
    for x in range(rows):
        for y in range(cols):
            for core in range(cores):
                along_x = (core == 0) != late
                there = ((x + by) % rows, y) if along_x else (x, (y + by) % cols)
                pairs.append(((x * cols + y) * cores + core, (there[0] * cols + there[1]) * cores + core))
    return lax.ppermute(value, ("x", "y", "core"), pairs)


def on_device(momentum, gradient, weight, tokens, block_index):
    fsdp = lax.axis_size("fsdp")
    side = SIZES[0]
    plane = side * side
    full = fsdp * weight.shape[1]
    picked = block_index[0, 0].T
    cosines = cosine_table()
    tables = [
        jnp.asarray(left_operand(cosines)),
        jnp.asarray(right_operand(cosines.T)),
        jnp.asarray(left_operand(cosines.T)),
        jnp.asarray(right_operand(cosines)),
    ]
    partial, away, own_weight = compress(True, picked, momentum, gradient, weight, tables)
    arrived = shift(away, "core", 2, 1)
    new_momentum, kept = compress(
        False, picked, momentum, gradient, weight, tables, partial
    )
    pair = (kept + arrived).astype(BF16)
    pair = pair.reshape((plane,) + pair.shape[2:])
    parts = lax.all_to_all(pair, ("x", "y"), 0, 0, tiled=True)
    summed = jnp.sum(parts.astype(F32), axis=0)
    total = summed + shift(summed, "zl", 2, 1)
    replicas = float(np.prod(SIZES))
    chunk = (own_weight - (STEP / replicas) * total).astype(BF16)
    row = jnp.stack([chunk] + [flip(chunk, "fsdp", fsdp, k) for k in range(1, fsdp)])
    stack = jnp.stack([row] + [turn(row, d, False) for d in range(1, side)], axis=1)
    every = tuple(range(fsdp))
    lower, upper = every[: fsdp // 2], every[fsdp // 2 :]
    swap = lambda value: shift(value, "core", 2, 1)

    def run(arrays, steps, shards, preact):
        return project(tokens, arrays, True, steps, shards, full, preact)

    def run_other(arrays, steps, shards, preact):
        return project(tokens, arrays, False, steps, shards, full, preact)

    other = swap(stack)
    left, right = turn(stack, 1, True), turn(stack, 3, True)
    preact = run([stack], (0,), (every,), None)
    preact = run_other([other], (0,), (every,), preact)
    left, right, preact = after(preact, left, right)
    far = [turn(left[: fsdp // 2], 1, True), turn(right[fsdp // 2 :], 3, True)]
    others = [swap(left), swap(right)]
    preact = run([left, right], (1, 3), (every, every), preact)
    preact = run_other(others, (1, 3), (every, every), preact)
    *far, preact = after(preact, *far)
    others = [swap(value) for value in far]
    preact = run(far, (2, 2), (lower, upper), preact)
    preact = run_other(others, (2, 2), (lower, upper), preact)
    return new_momentum, preact


def solution(mesh):
    split_mesh = Mesh(mesh.devices.reshape(SIZES + mesh.devices.shape[1:]), AXES)
    dp = AXES[:4]
    return jax.shard_map(
        on_device,
        mesh=split_mesh,
        in_specs=(
            P(dp, None, "fsdp"),
            P(dp, None, "fsdp"),
            P(None, "fsdp"),
            P(dp + ("fsdp",), None),
            P(dp, None, "fsdp", None),
        ),
        out_specs=(P(dp, None, "fsdp"), P(dp + ("fsdp",), None)),
        check_vma=False,
    )
```

time: 91.1 us -> 80 us (0.88)
  blocking collectives: 39 us -> 14.4 us
  waiting for transfers between devices: 5.05 us -> 17.6 us
  starting transfers between devices: 19.8 us -> 28.7 us
  Pallas kernels: 22.8 us -> 16.5 us
  local copies, waits for them, and re-layouts: 1.11 us -> 0.15 us
    all_to_all x1 -> x0, blocking collectives: 24.6 us -> none  [on_device(): lax.all_to_all(jnp.broadcast_to(row[None], (plane,) + row.shape), ('x', '...]
    ppermute x0 -> x10, starting transfers between devices: none -> 16.8 us  [the longest x7 8.74 us: turn(): return lax.ppermute(value, ('x', 'y', 'core'), pairs)]
    ppermute x0 -> x10, waiting for transfers between devices: none -> 15.8 us  [the longest x7 11.2 us: turn(): return lax.ppermute(value, ('x', 'y', 'core'), pairs)]
    ppermute x6 -> x7, starting transfers between devices: 19.8 us -> 11.9 us  [shift(): lax.ppermute(value, axis, [(i, (i + by) % size) for i in range(size)])]
    pallas_call x4 -> x10, Pallas kernels: 22.8 us -> 16.5 us  [the longest x2 8.82 us: compress(): pl.pallas_call(body, in_specs=in_specs, out_specs=out_specs, out_shape=ou...]
    ppermute x6 -> x7, waiting for transfers between devices: 5.05 us -> 1.78 us  [shift(): lax.ppermute(value, axis, [(i, (i + by) % size) for i in range(size)])]
  transfers between devices with their start and end apart: 6 -> 17, of which waited for: 2 -> 9; matrix products, arithmetic and copies ran while one was open for 1% -> 0% of each run, Pallas kernels for 13% -> 13%
where the time goes in v2:
time: 80 us; the launch traced here: 79.8 us
  starting transfers between devices  28.7 us (36%)
  waiting for transfers between devices  17.6 us (22%)
  Pallas kernels  16.5 us (21%)
  blocking collectives  14.4 us (18%)
  other arithmetic  1.47 us (2%)
  between operations  0.95 us (1%)
    all_to_all x1, blocking collectives, on_device(): parts = lax.all_to_all(pair, ('x', 'y'), 0, 0, tiled=True)  14.4 us
    ppermute x7, starting transfers between devices, shift(): lax.ppermute(value, axis, [(i, (i + by) % size) for i in range(size)])  11.9 us
    ppermute x7, waiting for transfers between devices, turn(): return lax.ppermute(value, ('x', 'y', 'core'), pairs)  11.2 us
    pallas_call x2, Pallas kernels, compress(): pl.pallas_call(body, in_specs=in_specs, out_specs=out_specs, out_shape=ou...  8.82 us
    ppermute x7, starting transfers between devices, turn(): return lax.ppermute(value, ('x', 'y', 'core'), pairs)  8.74 us
    ppermute x3, starting transfers between devices, flip(): return lax.ppermute(value, axis, [(i, i ^ mask) for i in range(size)])  8.11 us
    pallas_call x6, Pallas kernels, project(): pl.pallas_call(body, in_specs=in_specs, out_specs=pl.BlockSpec(memory_spa...  7.7 us
    ppermute x3, waiting for transfers between devices, flip(): return lax.ppermute(value, axis, [(i, i ^ mask) for i in range(size)])  4.57 us
  transfers between devices with their start and end apart: 17, of which 9 were waited for; matrix products, arithmetic and copies ran while one was open for 0% of the time, Pallas kernels for 13%

profile of v2, /device:TPU:1, one launch (start us, length us, event | category | flops | bytes accessed | tf_op | source)
XLA Modules:
  0.0 79.8 jit_solution(12165644906641978041)
XLA Ops:
  0.6 0.0 copy-start.1
  0.6 4.7 %compress_first.1 = (f32[1,64,7168]{2,1,0:T(8,128)}, f32[4,4,7,16,128]{4,3,2,1,0:T(8,128)}, f32[7,16,128]{2,1,0:T(8,128)}) custom-call(s32[4,112]{1,0:T(4,128)} %bitcast.27, f32[1,64,7168]{2,1,0:T(8,128)} %refs_1_.3, bf16[1,64,7168]{2,1,0:T(8,128)(2,1)} %refs_2_.3, bf16[64,7168]{1,0:T(8,128)(2,1)} %refs_3_.3, bf16[64,256]{1,0:T(8,128)(2,1)} %constant.12.clone.refs_4_, ...), custom_call_target="tpu_custom_call" | custom-call | flops 939524096 | bytes 2752512 | tf_op jit(solution)/shard_map/compress_first/pallas_call | solution.py:204
  5.3 3.3 %collective-permute-start = (f32[4,4,7,16,128]{4,3,2,1,0:T(8,128)}, f32[4,4,7,16,128]{4,3,2,1,0:T(8,128)S(1)}, u32[]{:S(2)}, u32[]{:S(2)}) collective-permute-start(f32[4,4,7,16,128]{4,3,2,1,0:T(8,128)} %get-tuple-element.17), channel_id=1, source_target_pairs={{0,4},{4,0},{1,5},{5,1},{2,6},{6,2},{3,7},{7,3},{8,12},{12,8},{9,1... | collective-permute-start | bytes 2752520 | tf_op jit(solution)/shard_map/ppermute | solution.py:313
  8.6 4.2 %compress_second.1 = (f32[1,64,7168]{2,1,0:T(8,128)}, f32[4,4,7,16,128]{4,3,2,1,0:T(8,128)}) custom-call(s32[4,112]{1,0:T(4,128)} %bitcast.28, f32[1,64,7168]{2,1,0:T(8,128)} %refs_1_.3, bf16[1,64,7168]{2,1,0:T(8,128)(2,1)} %refs_2_.3, bf16[64,7168]{1,0:T(8,128)(2,1)} %refs_3_.3, ...), custom_call_target="tpu_custom_call", output_to_operand_aliasing={{0}: (8, {})} | custom-call | flops 939524096 | bytes 2752512 | tf_op jit(solution)/shard_map/compress_second/pallas_call | solution.py:204
  12.8 0.0 collective-permute-done
  12.8 1.3 %add_convert_fusion = bf16[4,4,7,16,128]{4,3,2,1,0:T(8,128)(2,1)S(1)} fusion(f32[4,4,7,16,128]{4,3,2,1,0:T(8,128)} %get-tuple-element.16, f32[4,4,7,16,128]{4,3,2,1,0:T(8,128)S(1)} %collective-permute-done), kind=kLoop, calls=%fused_computation.1 | loop fusion | flops 458752 | bytes 2293760 | tf_op jit(solution)/shard_map/convert_element_type | solution.py:350
  14.1 14.4 %all_to_all.5 = bf16[16,7,16,128]{3,2,1,0:T(8,128)(2,1)S(1)} all-to-all(bf16[16,7,16,128]{3,2,1,0:T(8,128)(2,1)S(1)} %bitcast.19), channel_id=1, replica_groups=mesh['x'=4,'y'=4,'zl'=2,'core'=2,'fsdp'=4] {'x','y'}, dimensions={0} | all-to-all | bytes 917504 | tf_op jit(solution)/shard_map/all_to_all | solution.py:352
  28.5 0.1 convert_reduce_fusion
  28.6 1.7 %collective-permute-start.1 = (f32[7,16,128]{2,1,0:T(8,128)S(1)}, f32[7,16,128]{2,1,0:T(8,128)S(1)}, u32[]{:S(2)}, u32[]{:S(2)}) collective-permute-start(f32[7,16,128]{2,1,0:T(8,128)S(1)} %convert_reduce_fusion), channel_id=1, source_target_pairs={{0,8},{8,0},{1,9},{9,1},{2,10},{10,2},{3,11},{11,3},{4,12},{12,4},... | collective-permute-start | bytes 172040 | tf_op jit(solution)/shard_map/ppermute | solution.py:313
  30.3 1.6 %collective-permute-done.1 = f32[7,16,128]{2,1,0:T(8,128)S(1)} collective-permute-done((f32[7,16,128]{2,1,0:T(8,128)S(1)}, f32[7,16,128]{2,1,0:T(8,128)S(1)}, u32[]{:S(2)}, u32[]{:S(2)}) %collective-permute-start.1) | collective-permute-done | bytes 57376 | tf_op jit(solution)/shard_map/ppermute | solution.py:313
  31.9 5.9 %collective-permute-start.4 = (bf16[7,16,128]{2,1,0:T(8,128)(2,1)S(1)}, bf16[7,16,128]{2,1,0:T(8,128)(2,1)S(1)}, u32[]{:S(2)}, u32[]{:S(2)}) collective-permute-start(bf16[7,16,128]{2,1,0:T(8,128)(2,1)S(1)} %subtract_convert_fusion), channel_id=1, source_target_pairs={{0,3},{1,2},{2,1},{3,0},{4,7},{5,6},{6,5},{7,4},{8,11},{9,10},{10,... | collective-permute-start | bytes 86024 | tf_op jit(solution)/shard_map/ppermute | solution.py:317
  37.9 1.0 %collective-permute-start.3 = (bf16[7,16,128]{2,1,0:T(8,128)(2,1)S(1)}, bf16[7,16,128]{2,1,0:T(8,128)(2,1)S(1)}, u32[]{:S(2)}, u32[]{:S(2)}) collective-permute-start(bf16[7,16,128]{2,1,0:T(8,128)(2,1)S(1)} %subtract_convert_fusion), channel_id=1, source_target_pairs={{0,2},{1,3},{2,0},{3,1},{4,6},{5,7},{6,4},{7,5},{8,10},{9,11},{10,... | collective-permute-start | bytes 86024 | tf_op jit(solution)/shard_map/ppermute | solution.py:317
  38.8 1.2 %collective-permute-start.2 = (bf16[7,16,128]{2,1,0:T(8,128)(2,1)S(1)}, bf16[7,16,128]{2,1,0:T(8,128)(2,1)S(1)}, u32[]{:S(2)}, u32[]{:S(2)}) collective-permute-start(bf16[7,16,128]{2,1,0:T(8,128)(2,1)S(1)} %subtract_convert_fusion), channel_id=1, source_target_pairs={{0,1},{1,0},{2,3},{3,2},{4,5},{5,4},{6,7},{7,6},{8,9},{9,8},{10,11... | collective-permute-start | bytes 86024 | tf_op jit(solution)/shard_map/ppermute | solution.py:317
  40.0 0.0 collective-permute-done.4
  40.0 4.6 %collective-permute-done.3 = bf16[7,16,128]{2,1,0:T(8,128)(2,1)S(1)} collective-permute-done((bf16[7,16,128]{2,1,0:T(8,128)(2,1)S(1)}, bf16[7,16,128]{2,1,0:T(8,128)(2,1)S(1)}, u32[]{:S(2)}, u32[]{:S(2)}) %collective-permute-start.3) | collective-permute-done | bytes 28704 | tf_op jit(solution)/shard_map/ppermute | solution.py:317
  44.6 0.0 collective-permute-done.2
  44.6 1.7 %collective-permute-start.6 = (bf16[4,7,16,128]{3,2,1,0:T(8,128)(2,1)S(1)}, bf16[4,7,16,128]{3,2,1,0:T(8,128)(2,1)S(1)}, u32[]{:S(2)}, u32[]{:S(2)}) collective-permute-start(bf16[4,7,16,128]{3,2,1,0:T(8,128)(2,1)S(1)} %get-tuple-element.25), channel_id=1, source_target_pairs={{0,128},{4,36},{16,144},{20,52},{32,160},{36,4},{48,176},{52,20},{... | collective-permute-start | bytes 344072 | tf_op jit(solution)/shard_map/ppermute | solution.py:329
  46.3 0.3 collective-permute-start.5
  46.6 2.4 %collective-permute-start.7 = (bf16[4,7,16,128]{3,2,1,0:T(8,128)(2,1)S(1)}, bf16[4,7,16,128]{3,2,1,0:T(8,128)(2,1)S(1)}, u32[]{:S(2)}, u32[]{:S(2)}) collective-permute-start(bf16[4,7,16,128]{3,2,1,0:T(8,128)(2,1)S(1)} %get-tuple-element.25), channel_id=1, source_target_pairs={{0,192},{4,52},{16,208},{20,4},{32,224},{36,20},{48,240},{52,36},{... | collective-permute-start | bytes 344072 | tf_op jit(solution)/shard_map/ppermute | solution.py:329
  49.0 0.9 %collective-permute-done.6 = bf16[4,7,16,128]{3,2,1,0:T(8,128)(2,1)S(1)} collective-permute-done((bf16[4,7,16,128]{3,2,1,0:T(8,128)(2,1)S(1)}, bf16[4,7,16,128]{3,2,1,0:T(8,128)(2,1)S(1)}, u32[]{:S(2)}, u32[]{:S(2)}) %collective-permute-start.6) | collective-permute-done | bytes 114720 | tf_op jit(solution)/shard_map/ppermute | solution.py:329
  49.9 1.3 %collective-permute-done.5 = bf16[4,7,16,128]{3,2,1,0:T(8,128)(2,1)S(1)} collective-permute-done((bf16[4,7,16,128]{3,2,1,0:T(8,128)(2,1)S(1)}, bf16[4,7,16,128]{3,2,1,0:T(8,128)(2,1)S(1)}, u32[]{:S(2)}, u32[]{:S(2)}) %collective-permute-start.5) | collective-permute-done | bytes 114720 | tf_op jit(solution)/shard_map/ppermute | solution.py:329
  51.1 0.0 collective-permute-done.7
  51.2 0.1 pad_maximum_fusion.rest_0_
  51.2 5.8 %collective-permute-start.10 = (bf16[4,4,7,16,128]{4,3,2,1,0:T(8,128)(2,1)S(1)}, bf16[4,4,7,16,128]{4,3,2,1,0:T(8,128)(2,1)S(1)}, u32[]{:S(2)}, u32[]{:S(2)}) collective-permute-start(bf16[4,4,7,16,128]{4,3,2,1,0:T(8,128)(2,1)S(1)} %pad_maximum_fusion.rest_0_), channel_id=1, source_target_pairs={{0,4},{4,0},{1,5},{5,1},{2,6},{6,2},{3,7},{7,3},{8,12},{12,8},{9,1... | collective-permute-start | bytes 1376264 | tf_op jit(solution)/shard_map/ppermute | solution.py:313
  57.0 2.6 %collective-permute-start.9 = (bf16[4,4,7,16,128]{4,3,2,1,0:T(8,128)(2,1)S(1)}, bf16[4,4,7,16,128]{4,3,2,1,0:T(8,128)(2,1)S(1)}, u32[]{:S(2)}, u32[]{:S(2)}) collective-permute-start(bf16[4,4,7,16,128]{4,3,2,1,0:T(8,128)(2,1)S(1)} %pad_maximum_fusion.rest_0_), channel_id=1, source_target_pairs={{0,48},{4,196},{16,0},{20,212},{32,16},{36,228},{48,32},{52,244},{... | collective-permute-start | bytes 1376264 | tf_op jit(solution)/shard_map/ppermute | solution.py:329
  59.6 0.0 collective-permute-start.8
  59.6 0.1 copy.31.tokens
  59.7 1.2 %project.6.rest_1_ = bf16[128,28672]{1,0:T(8,128)(2,1)} custom-call(bf16[128,64]{1,0:T(8,128)(2,1)S(1)} %copy.31.tokens, bf16[4,4,7,16,128]{4,3,2,1,0:T(8,128)(2,1)S(1)} %pad_maximum_fusion.rest_0_), custom_call_target="tpu_custom_call" | custom-call | flops 58720256 | bytes 31457280 | tf_op jit(solution)/shard_map/project/pallas_call | solution.py:275
  60.9 0.0 collective-permute-done.10.rest_0_
  60.9 1.2 %project.7.refs_2_ = bf16[128,28672]{1,0:T(8,128)(2,1)} custom-call(bf16[128,64]{1,0:T(8,128)(2,1)S(1)} %copy.31.tokens, bf16[4,4,7,16,128]{4,3,2,1,0:T(8,128)(2,1)S(1)} %collective-permute-done.10.rest_0_, bf16[128,28672]{1,0:T(8,128)(2,1)} %project.6.rest_1_), custom_call_target="tpu_custom_call", output_to_operand_aliasing={{}: (2, {})} | custom-call | flops 58720256 | bytes 31457280 | tf_op jit(solution)/shard_map/project/pallas_call | solution.py:275
  62.1 2.9 %collective-permute-done.9.refs_1_ = bf16[4,4,7,16,128]{4,3,2,1,0:T(8,128)(2,1)S(1)} collective-permute-done((bf16[4,4,7,16,128]{4,3,2,1,0:T(8,128)(2,1)S(1)}, bf16[4,4,7,16,128]{4,3,2,1,0:T(8,128)(2,1)S(1)}, u32[]{:S(2)}, u32[]{:S(2)}) %collective-permute-start.9) | collective-permute-done | bytes 458784 | tf_op jit(solution)/shard_map/ppermute | solution.py:329
  65.0 3.1 %collective-permute-done.8.refs_0_ = bf16[4,4,7,16,128]{4,3,2,1,0:T(8,128)(2,1)S(1)} collective-permute-done((bf16[4,4,7,16,128]{4,3,2,1,0:T(8,128)(2,1)S(1)}, bf16[4,4,7,16,128]{4,3,2,1,0:T(8,128)(2,1)S(1)}, u32[]{:S(2)}, u32[]{:S(2)}) %collective-permute-start.8) | collective-permute-done | bytes 458784 | tf_op jit(solution)/shard_map/ppermute | solution.py:329
  68.2 0.0 collective-permute-start.13
  68.2 0.5 collective-permute-start.14
  68.7 1.8 %collective-permute-start.12 = (bf16[2,4,7,16,128]{4,3,2,1,0:T(8,128)(2,1)S(1)}, bf16[2,4,7,16,128]{4,3,2,1,0:T(8,128)(2,1)S(1)}, u32[]{:S(2)}, u32[]{:S(2)}) collective-permute-start(bf16[2,4,7,16,128]{4,3,2,1,0:T(8,128)(2,1)S(1)} %slice.7), channel_id=1, source_target_pairs={{0,48},{4,196},{16,0},{20,212},{32,16},{36,228},{48,32},{52,244},{... | collective-permute-start | bytes 688136 | tf_op jit(solution)/shard_map/ppermute | solution.py:329
  70.5 0.0 collective-permute-start.11
  70.5 1.5 %project.8.rest_2_ = bf16[128,28672]{1,0:T(8,128)(2,1)} custom-call(bf16[128,64]{1,0:T(8,128)(2,1)S(1)} %copy.31.tokens, bf16[4,4,7,16,128]{4,3,2,1,0:T(8,128)(2,1)S(1)} %get-tuple-element.18.rest_0_, bf16[4,4,7,16,128]{4,3,2,1,0:T(8,128)(2,1)S(1)} %get-tuple-element.19.rest_1_, ...), custom_call_target="tpu_custom_call", output_to_operand_aliasing={{}: (3, {})} | custom-call | flops 117440512 | bytes 62914560 | tf_op jit(solution)/shard_map/project/pallas_call | solution.py:275
  72.0 0.0 collective-permute-done.13.rest_0_
  72.0 0.0 collective-permute-done.14.rest_1_
  72.0 1.5 %project.9.refs_2_ = bf16[128,28672]{1,0:T(8,128)(2,1)} custom-call(bf16[128,64]{1,0:T(8,128)(2,1)S(1)} %copy.31.tokens, bf16[4,4,7,16,128]{4,3,2,1,0:T(8,128)(2,1)S(1)} %collective-permute-done.13.rest_0_, bf16[4,4,7,16,128]{4,3,2,1,0:T(8,128)(2,1)S(1)} %collective-permute-done.14.rest_1_, ...), custom_call_target="tpu_custom_call", output_to_operand_aliasing={{}: (3, {})} | custom-call | flops 117440512 | bytes 62914560 | tf_op jit(solution)/shard_map/project/pallas_call | solution.py:275
  73.6 0.4 collective-permute-done.12.refs_1_
  74.0 2.7 %collective-permute-done.11.refs_0_ = bf16[2,4,7,16,128]{4,3,2,1,0:T(8,128)(2,1)S(1)} collective-permute-done((bf16[2,4,7,16,128]{4,3,2,1,0:T(8,128)(2,1)S(1)}, bf16[2,4,7,16,128]{4,3,2,1,0:T(8,128)(2,1)S(1)}, u32[]{:S(2)}, u32[]{:S(2)}) %collective-permute-start.11) | collective-permute-done | bytes 229408 | tf_op jit(solution)/shard_map/ppermute | solution.py:329
  76.6 0.4 collective-permute-start.15
  77.0 0.1 collective-permute-start.16
  77.1 1.2 %project.10.rest_2_ = bf16[128,28672]{1,0:T(8,128)(2,1)} custom-call(bf16[128,64]{1,0:T(8,128)(2,1)S(1)} %copy.31.tokens, bf16[2,4,7,16,128]{4,3,2,1,0:T(8,128)(2,1)S(1)} %get-tuple-element.21.rest_0_, bf16[2,4,7,16,128]{4,3,2,1,0:T(8,128)(2,1)S(1)} %get-tuple-element.22.rest_1_, ...), custom_call_target="tpu_custom_call", output_to_operand_aliasing={{}: (3, {})} | custom-call | flops 58720256 | bytes 62914560 | tf_op jit(solution)/shard_map/project/pallas_call | solution.py:275
  78.3 0.0 collective-permute-done.15.rest_0_
  78.3 0.2 collective-permute-done.16.rest_1_
  78.5 1.2 %project.11 = bf16[128,28672]{1,0:T(8,128)(2,1)} custom-call(bf16[128,64]{1,0:T(8,128)(2,1)S(1)} %copy.31.tokens, bf16[2,4,7,16,128]{4,3,2,1,0:T(8,128)(2,1)S(1)} %collective-permute-done.15.rest_0_, bf16[2,4,7,16,128]{4,3,2,1,0:T(8,128)(2,1)S(1)} %collective-permute-done.16.rest_1_, bf16[128,28672]{1,0:T(8,128)(2,1)} %project.10.rest_2_), custom_call_target="tpu_custom_call", output_to_operand_aliasing={{}: (3, {})} | custom-call | flops 58720256 | bytes 62914560 | tf_op jit(solution)/shard_map/project/pallas_call | solution.py:275
  (9 shorter events, 0.1 us)
Async XLA Ops:
  0.6 59.0 %copy-start.1 = (bf16[128,64]{0,1:T(8,128)(2,1)S(1)}, bf16[128,64]{0,1:T(8,128)(2,1)}, u32[]{:S(2)}) copy-start(bf16[128,64]{0,1:T(8,128)(2,1)} %param.12) | copy-start | bytes 49156
  5.3 26.6 %copy-start = (f32[7,16,128]{2,1,0:T(8,128)S(1)}, f32[7,16,128]{2,1,0:T(8,128)}, u32[]{:S(2)}) copy-start(f32[7,16,128]{2,1,0:T(8,128)} %get-tuple-element.15) | copy-start | bytes 172036
  5.3 7.5 %collective-permute-start = (f32[4,4,7,16,128]{4,3,2,1,0:T(8,128)}, f32[4,4,7,16,128]{4,3,2,1,0:T(8,128)S(1)}, u32[]{:S(2)}, u32[]{:S(2)}) collective-permute-start(f32[4,4,7,16,128]{4,3,2,1,0:T(8,128)} %get-tuple-element.17), channel_id=1, source_target_pairs={{0,4},{4,0},{1,5},{5,1},{2,6},{6,2},{3,7},{7,3},{8,12},{12,8},{9,1... | collective-permute-start | bytes 2752520 | tf_op jit(solution)/shard_map/ppermute | solution.py:313
  28.6 3.3 %collective-permute-start.1 = (f32[7,16,128]{2,1,0:T(8,128)S(1)}, f32[7,16,128]{2,1,0:T(8,128)S(1)}, u32[]{:S(2)}, u32[]{:S(2)}) collective-permute-start(f32[7,16,128]{2,1,0:T(8,128)S(1)} %convert_reduce_fusion), channel_id=1, source_target_pairs={{0,8},{8,0},{1,9},{9,1},{2,10},{10,2},{3,11},{11,3},{4,12},{12,4},... | collective-permute-start | bytes 172040 | tf_op jit(solution)/shard_map/ppermute | solution.py:313
  31.9 8.1 %collective-permute-start.4 = (bf16[7,16,128]{2,1,0:T(8,128)(2,1)S(1)}, bf16[7,16,128]{2,1,0:T(8,128)(2,1)S(1)}, u32[]{:S(2)}, u32[]{:S(2)}) collective-permute-start(bf16[7,16,128]{2,1,0:T(8,128)(2,1)S(1)} %subtract_convert_fusion), channel_id=1, source_target_pairs={{0,3},{1,2},{2,1},{3,0},{4,7},{5,6},{6,5},{7,4},{8,11},{9,10},{10,... | collective-permute-start | bytes 86024 | tf_op jit(solution)/shard_map/ppermute | solution.py:317
  37.9 6.8 %collective-permute-start.3 = (bf16[7,16,128]{2,1,0:T(8,128)(2,1)S(1)}, bf16[7,16,128]{2,1,0:T(8,128)(2,1)S(1)}, u32[]{:S(2)}, u32[]{:S(2)}) collective-permute-start(bf16[7,16,128]{2,1,0:T(8,128)(2,1)S(1)} %subtract_convert_fusion), channel_id=1, source_target_pairs={{0,2},{1,3},{2,0},{3,1},{4,6},{5,7},{6,4},{7,5},{8,10},{9,11},{10,... | collective-permute-start | bytes 86024 | tf_op jit(solution)/shard_map/ppermute | solution.py:317
  38.8 5.8 %collective-permute-start.2 = (bf16[7,16,128]{2,1,0:T(8,128)(2,1)S(1)}, bf16[7,16,128]{2,1,0:T(8,128)(2,1)S(1)}, u32[]{:S(2)}, u32[]{:S(2)}) collective-permute-start(bf16[7,16,128]{2,1,0:T(8,128)(2,1)S(1)} %subtract_convert_fusion), channel_id=1, source_target_pairs={{0,1},{1,0},{2,3},{3,2},{4,5},{5,4},{6,7},{7,6},{8,9},{9,8},{10,11... | collective-permute-start | bytes 86024 | tf_op jit(solution)/shard_map/ppermute | solution.py:317
  44.6 5.2 %collective-permute-start.6 = (bf16[4,7,16,128]{3,2,1,0:T(8,128)(2,1)S(1)}, bf16[4,7,16,128]{3,2,1,0:T(8,128)(2,1)S(1)}, u32[]{:S(2)}, u32[]{:S(2)}) collective-permute-start(bf16[4,7,16,128]{3,2,1,0:T(8,128)(2,1)S(1)} %get-tuple-element.25), channel_id=1, source_target_pairs={{0,128},{4,36},{16,144},{20,52},{32,160},{36,4},{48,176},{52,20},{... | collective-permute-start | bytes 344072 | tf_op jit(solution)/shard_map/ppermute | solution.py:329
  46.3 4.9 %collective-permute-start.5 = (bf16[4,7,16,128]{3,2,1,0:T(8,128)(2,1)S(1)}, bf16[4,7,16,128]{3,2,1,0:T(8,128)(2,1)S(1)}, u32[]{:S(2)}, u32[]{:S(2)}) collective-permute-start(bf16[4,7,16,128]{3,2,1,0:T(8,128)(2,1)S(1)} %get-tuple-element.25), channel_id=1, source_target_pairs={{0,64},{4,20},{16,80},{20,36},{32,96},{36,52},{48,112},{52,4},{64,... | collective-permute-start | bytes 344072 | tf_op jit(solution)/shard_map/ppermute | solution.py:329
  46.6 4.6 %collective-permute-start.7 = (bf16[4,7,16,128]{3,2,1,0:T(8,128)(2,1)S(1)}, bf16[4,7,16,128]{3,2,1,0:T(8,128)(2,1)S(1)}, u32[]{:S(2)}, u32[]{:S(2)}) collective-permute-start(bf16[4,7,16,128]{3,2,1,0:T(8,128)(2,1)S(1)} %get-tuple-element.25), channel_id=1, source_target_pairs={{0,192},{4,52},{16,208},{20,4},{32,224},{36,20},{48,240},{52,36},{... | collective-permute-start | bytes 344072 | tf_op jit(solution)/shard_map/ppermute | solution.py:329
  51.2 9.7 %collective-permute-start.10 = (bf16[4,4,7,16,128]{4,3,2,1,0:T(8,128)(2,1)S(1)}, bf16[4,4,7,16,128]{4,3,2,1,0:T(8,128)(2,1)S(1)}, u32[]{:S(2)}, u32[]{:S(2)}) collective-permute-start(bf16[4,4,7,16,128]{4,3,2,1,0:T(8,128)(2,1)S(1)} %pad_maximum_fusion.rest_0_), channel_id=1, source_target_pairs={{0,4},{4,0},{1,5},{5,1},{2,6},{6,2},{3,7},{7,3},{8,12},{12,8},{9,1... | collective-permute-start | bytes 1376264 | tf_op jit(solution)/shard_map/ppermute | solution.py:313
  57.0 8.0 %collective-permute-start.9 = (bf16[4,4,7,16,128]{4,3,2,1,0:T(8,128)(2,1)S(1)}, bf16[4,4,7,16,128]{4,3,2,1,0:T(8,128)(2,1)S(1)}, u32[]{:S(2)}, u32[]{:S(2)}) collective-permute-start(bf16[4,4,7,16,128]{4,3,2,1,0:T(8,128)(2,1)S(1)} %pad_maximum_fusion.rest_0_), channel_id=1, source_target_pairs={{0,48},{4,196},{16,0},{20,212},{32,16},{36,228},{48,32},{52,244},{... | collective-permute-start | bytes 1376264 | tf_op jit(solution)/shard_map/ppermute | solution.py:329
  59.6 8.5 %collective-permute-start.8 = (bf16[4,4,7,16,128]{4,3,2,1,0:T(8,128)(2,1)S(1)}, bf16[4,4,7,16,128]{4,3,2,1,0:T(8,128)(2,1)S(1)}, u32[]{:S(2)}, u32[]{:S(2)}) collective-permute-start(bf16[4,4,7,16,128]{4,3,2,1,0:T(8,128)(2,1)S(1)} %pad_maximum_fusion.rest_0_), channel_id=1, source_target_pairs={{0,16},{4,68},{16,32},{20,84},{32,48},{36,100},{48,0},{52,116},{64... | collective-permute-start | bytes 1376264 | tf_op jit(solution)/shard_map/ppermute | solution.py:329
  68.2 3.9 %collective-permute-start.13 = (bf16[4,4,7,16,128]{4,3,2,1,0:T(8,128)(2,1)S(1)}, bf16[4,4,7,16,128]{4,3,2,1,0:T(8,128)(2,1)S(1)}, u32[]{:S(2)}, u32[]{:S(2)}) collective-permute-start(bf16[4,4,7,16,128]{4,3,2,1,0:T(8,128)(2,1)S(1)} %get-tuple-element.18.rest_0_), channel_id=1, source_target_pairs={{0,4},{4,0},{1,5},{5,1},{2,6},{6,2},{3,7},{7,3},{8,12},{12,8},{9,1... | collective-permute-start | bytes 1376264 | tf_op jit(solution)/shard_map/ppermute | solution.py:313
  68.2 3.9 %collective-permute-start.14 = (bf16[4,4,7,16,128]{4,3,2,1,0:T(8,128)(2,1)S(1)}, bf16[4,4,7,16,128]{4,3,2,1,0:T(8,128)(2,1)S(1)}, u32[]{:S(2)}, u32[]{:S(2)}) collective-permute-start(bf16[4,4,7,16,128]{4,3,2,1,0:T(8,128)(2,1)S(1)} %get-tuple-element.19.rest_1_), channel_id=1, source_target_pairs={{0,4},{4,0},{1,5},{5,1},{2,6},{6,2},{3,7},{7,3},{8,12},{12,8},{9,1... | collective-permute-start | bytes 1376264 | tf_op jit(solution)/shard_map/ppermute | solution.py:313
  68.7 5.2 %collective-permute-start.12 = (bf16[2,4,7,16,128]{4,3,2,1,0:T(8,128)(2,1)S(1)}, bf16[2,4,7,16,128]{4,3,2,1,0:T(8,128)(2,1)S(1)}, u32[]{:S(2)}, u32[]{:S(2)}) collective-permute-start(bf16[2,4,7,16,128]{4,3,2,1,0:T(8,128)(2,1)S(1)} %slice.7), channel_id=1, source_target_pairs={{0,48},{4,196},{16,0},{20,212},{32,16},{36,228},{48,32},{52,244},{... | collective-permute-start | bytes 688136 | tf_op jit(solution)/shard_map/ppermute | solution.py:329
  70.5 6.1 %collective-permute-start.11 = (bf16[2,4,7,16,128]{4,3,2,1,0:T(8,128)(2,1)S(1)}, bf16[2,4,7,16,128]{4,3,2,1,0:T(8,128)(2,1)S(1)}, u32[]{:S(2)}, u32[]{:S(2)}) collective-permute-start(bf16[2,4,7,16,128]{4,3,2,1,0:T(8,128)(2,1)S(1)} %slice.6), channel_id=1, source_target_pairs={{0,16},{4,68},{16,32},{20,84},{32,48},{36,100},{48,0},{52,116},{64... | collective-permute-start | bytes 688136 | tf_op jit(solution)/shard_map/ppermute | solution.py:329
  76.6 1.7 %collective-permute-start.15 = (bf16[2,4,7,16,128]{4,3,2,1,0:T(8,128)(2,1)S(1)}, bf16[2,4,7,16,128]{4,3,2,1,0:T(8,128)(2,1)S(1)}, u32[]{:S(2)}, u32[]{:S(2)}) collective-permute-start(bf16[2,4,7,16,128]{4,3,2,1,0:T(8,128)(2,1)S(1)} %get-tuple-element.21.rest_0_), channel_id=1, source_target_pairs={{0,4},{4,0},{1,5},{5,1},{2,6},{6,2},{3,7},{7,3},{8,12},{12,8},{9,1... | collective-permute-start | bytes 688136 | tf_op jit(solution)/shard_map/ppermute | solution.py:313
  77.0 1.5 %collective-permute-start.16 = (bf16[2,4,7,16,128]{4,3,2,1,0:T(8,128)(2,1)S(1)}, bf16[2,4,7,16,128]{4,3,2,1,0:T(8,128)(2,1)S(1)}, u32[]{:S(2)}, u32[]{:S(2)}) collective-permute-start(bf16[2,4,7,16,128]{4,3,2,1,0:T(8,128)(2,1)S(1)} %get-tuple-element.22.rest_1_), channel_id=1, source_target_pairs={{0,4},{4,0},{1,5},{5,1},{2,6},{6,2},{3,7},{7,3},{8,12},{12,8},{9,1... | collective-permute-start | bytes 688136 | tf_op jit(solution)/shard_map/ppermute | solution.py:313

commit v3 on v2

--- a/solution.py
+++ b/solution.py
@@ -66,8 +66,12 @@
 
 
 def whereabouts():
-    x, y, core, shard = (lax.axis_index(a) for a in ("x", "y", "core", "fsdp"))
-    return jnp.where(core == 0, x, y), jnp.where(core == 0, y, x), core, shard
+    x, y, low, core, shard = (lax.axis_index(a) for a in AXES)
+    return jnp.where(core == 0, x, y), jnp.where(core == 0, y, x), low, core, shard
+
+
+def chunk_column(second, low):
+    return lax.rem(second + 2 * low, SIZES[1])
 
 
 def compress_kernel(first, tiles, steps, index, momentum, gradient, weight, *rest):
@@ -80,7 +84,7 @@
     moment_buf, grad_buf, new_buf, weight_buf, *rest = rest[3:]
     tables, (in_sems, out_sems, table_sems, sent_buf, sent_sems, picked) = rest[:4], rest[4:]
     wide = tiles * LANES
-    core = place[2]
+    first_axis, second_axis, low, core = place[:4]
     half = (1 - core) if first else core
 
     spans = [slice(a * wide, b * wide) for a, b in zip(BATCHES, BATCHES[1:])]
@@ -108,8 +112,8 @@
     for copy in (*loads[0], index_load, *table_loads, *(copy for pair in loads[1:] for copy in pair)):
         copy.start()
     if first:
-        at = pl.multiple_of((core * steps + place[1]) * wide, wide)
-        row = pl.multiple_of(place[0] * ROWS, ROWS)
+        at = pl.multiple_of((core * steps + chunk_column(second_axis, low)) * wide, wide)
+        row = pl.multiple_of(first_axis * ROWS, ROWS)
         weight_load = pltpu.make_async_copy(
             weight.at[pl.ds(row, ROWS), pl.ds(at, wide)], weight_buf, table_sems.at[4]
         )
@@ -158,8 +162,9 @@
         stores.append(store)
         for j in range(span.start // wide, span.stop // wide):
             for i in range(GROUP // ROWS):
-                outer = jnp.where(half == 0, i, j)
-                inner = jnp.where(half == 0, j, i)
+                goal = chunk_column(j, low)
+                outer = jnp.where(half == 0, i, goal)
+                inner = jnp.where(half == 0, goal, i)
                 for t in range(tiles):
                     at = j * wide + t * LANES - span.start
                     sent_buf[j, i, t] = transmitted[i * ROWS : (i + 1) * ROWS, at : at + LANES]
@@ -228,23 +233,37 @@
     )(*operands)
 
 
+def row_shard(shard, low, k):
+    return shard ^ k
+
+
+def below_shard(shard, low, k):
+    return 2 + (((shard + 1 - low) & 1) ^ k)
+
+
+def above_shard(shard, low, k):
+    return ((shard + low) & 1) ^ k
+
+
 def project(tokens, pieces, own, steps, shards, breadth, partial=None):
     count, depth = tokens.shape
     _, side, tiles, rows, lanes = pieces[0].shape
     wide = tiles * lanes
     number = len(pieces)
-    slots = sum(len(held) for held in shards)
+    slots = sum(piece.shape[0] for piece in pieces)
 
     def body(tokens, *rest):
         place = whereabouts()
         arrays, (out, held, sems) = rest[:number], rest[-3:]
-        turn_of, start = (place[0], place[1]) if own else (place[1], place[0])
-        half = place[2] if own else 1 - place[2]
+        first, second, low, core, mine = place
+        turn_of, start = (first, second) if own else (second, first)
+        start = chunk_column(start, low)
+        half = core if own else 1 - core
         order = [lax.rem(turn_of - i + side, side) for i in range(side)]
         copies = []
         for n in range(number):
             at = half * side + lax.rem(start - steps[n] + side, side)
-            for k, shard in enumerate(shards[n]):
+            for k in range(pieces[n].shape[0]):
                 slot = len(copies)
                 table = jnp.concatenate(
                     [
@@ -256,7 +275,7 @@
                 held[slot] = jnp.dot(
                     tokens[...], table, preferred_element_type=F32
                 ).astype(BF16)
-                column = pl.multiple_of(((place[3] ^ shard) * 2 * side + at) * wide, wide)
+                column = pl.multiple_of((shards[n](mine, low, k) * 2 * side + at) * wide, wide)
                 copy = pltpu.make_async_copy(
                     held.at[slot], out.at[:, pl.ds(column, wide)], sems.at[slot]
                 )
@@ -285,7 +304,7 @@
         compiler_params=pltpu.CompilerParams(vmem_limit_bytes=16 * 2**20),
         cost_estimate=pl.CostEstimate(
             flops=2 * count * depth * wide * slots,
-            bytes_accessed=30 * 2**20 * number,
+            bytes_accessed=4 * count * wide * slots,
             transcendentals=0,
         ),
         name="project",
@@ -309,24 +328,45 @@
     )(*operands)
 
 
-def shift(value, axis, size, by):
-    return lax.ppermute(value, axis, [(i, (i + by) % size) for i in range(size)])
-
-
-def flip(value, axis, size, mask):
-    return lax.ppermute(value, axis, [(i, i ^ mask) for i in range(size)])
+def move(value, goal, *axes):
+    extent = [lax.axis_size(axis) for axis in axes]
+    places = list(np.ndindex(*extent))
+    number = {spot: n for n, spot in enumerate(places)}
+    pairs = []
+    for spot in places:
+        there = tuple(c % e for c, e in zip(goal(*spot), extent))
+        pairs.append((number[spot], number[there]))
+    return lax.ppermute(value, axes, pairs)
+
+
+def swap(value):
+    return move(value, lambda core: (core + 1,), "core")
+
+
+def flip(value, mask):
+    return move(value, lambda shard: (shard ^ mask,), "fsdp")
 
 
 def turn(value, by, late):
-    rows, cols, _, cores = SIZES
-    pairs = []
-    for x in range(rows):
-        for y in range(cols):
-            for core in range(cores):
-                along_x = (core == 0) != late
-                there = ((x + by) % rows, y) if along_x else (x, (y + by) % cols)
-                pairs.append(((x * cols + y) * cores + core, (there[0] * cols + there[1]) * cores + core))
-    return lax.ppermute(value, ("x", "y", "core"), pairs)
+    def goal(x, y, core):
+        return (x + by, y, core) if (core == 0) != late else (x, y + by, core)
+
+    return move(value, goal, "x", "y", "core")
+
+
+def across(value):
+    def goal(x, y, low, core):
+        return (x, y + 2, low + 1, core) if core == 0 else (x + 2, y, low + 1, core)
+
+    return move(value, goal, "x", "y", "zl", "core")
+
+
+def climb(value, by):
+    def goal(low, shard):
+        z = 2 * shard + low + by
+        return z % 2, z // 2
+
+    return move(value, goal, "zl", "fsdp")
 
 
 def on_device(momentum, gradient, weight, tokens, block_index):
@@ -343,7 +383,7 @@
         jnp.asarray(right_operand(cosines)),
     ]
     partial, away, own_weight = compress(True, picked, momentum, gradient, weight, tables)
-    arrived = shift(away, "core", 2, 1)
+    arrived = swap(away)
     new_momentum, kept = compress(
         False, picked, momentum, gradient, weight, tables, partial
     )
@@ -351,34 +391,23 @@
     pair = pair.reshape((plane,) + pair.shape[2:])
     parts = lax.all_to_all(pair, ("x", "y"), 0, 0, tiled=True)
     summed = jnp.sum(parts.astype(F32), axis=0)
-    total = summed + shift(summed, "zl", 2, 1)
+    total = summed + across(summed)
     replicas = float(np.prod(SIZES))
     chunk = (own_weight - (STEP / replicas) * total).astype(BF16)
-    row = jnp.stack([chunk] + [flip(chunk, "fsdp", fsdp, k) for k in range(1, fsdp)])
+    row = jnp.stack([chunk] + [flip(chunk, k) for k in range(1, fsdp)])
     stack = jnp.stack([row] + [turn(row, d, False) for d in range(1, side)], axis=1)
-    every = tuple(range(fsdp))
-    lower, upper = every[: fsdp // 2], every[fsdp // 2 :]
-    swap = lambda value: shift(value, "core", 2, 1)
-
-    def run(arrays, steps, shards, preact):
-        return project(tokens, arrays, True, steps, shards, full, preact)
-
-    def run_other(arrays, steps, shards, preact):
-        return project(tokens, arrays, False, steps, shards, full, preact)
-
-    other = swap(stack)
     left, right = turn(stack, 1, True), turn(stack, 3, True)
-    preact = run([stack], (0,), (every,), None)
-    preact = run_other([other], (0,), (every,), preact)
-    left, right, preact = after(preact, left, right)
-    far = [turn(left[: fsdp // 2], 1, True), turn(right[fsdp // 2 :], 3, True)]
-    others = [swap(left), swap(right)]
-    preact = run([left, right], (1, 3), (every, every), preact)
-    preact = run_other(others, (1, 3), (every, every), preact)
-    *far, preact = after(preact, *far)
-    others = [swap(value) for value in far]
-    preact = run(far, (2, 2), (lower, upper), preact)
-    preact = run_other(others, (2, 2), (lower, upper), preact)
+    near_half, far_half = stack[: fsdp // 2], stack[fsdp // 2 :]
+    low_shards = lax.axis_index("fsdp") < fsdp // 2
+    below = climb(jnp.where(low_shards, far_half, near_half), 1)
+    above = climb(jnp.where(low_shards, near_half, far_half), -1)
+    preact = project(tokens, [stack], True, (0,), (row_shard,), full)
+    *arrays, preact = after(preact, stack, left, right, below, above)
+    others = [swap(value) for value in arrays]
+    steps = (0, 1, 3, 2, 2)
+    shards = (row_shard, row_shard, row_shard, below_shard, above_shard)
+    preact = project(tokens, arrays[1:], True, steps[1:], shards[1:], full, preact)
+    preact = project(tokens, others, False, steps, shards, full, preact)
     return new_momentum, preact
 
 

time: 80 us -> 77 us (0.963)
  Pallas kernels: 16.5 us -> 14.1 us
  waiting for transfers between devices: 17.6 us -> 15.6 us
  starting transfers between devices: 28.7 us -> 30.1 us
    pallas_call x6 -> x3, Pallas kernels: 7.7 us -> 5.25 us  [project(): pl.pallas_call(body, in_specs=in_specs, out_specs=pl.BlockSpec(memory_spa...]
    ppermute x17, waiting for transfers between devices: 17.6 us -> 15.6 us  [move(): return lax.ppermute(value, axes, pairs)]
    ppermute x17, starting transfers between devices: 28.7 us -> 30.1 us  [move(): return lax.ppermute(value, axes, pairs)]
  transfers between devices with their start and end apart: 17 -> 17, of which waited for: 9 -> 9; matrix products, arithmetic and copies ran while one was open for 0% -> 0% of each run, Pallas kernels for 13% -> 9%
where the time goes in v3:
time: 77 us; the launch traced here: 76.7 us
  starting transfers between devices  30.1 us (39%)
  waiting for transfers between devices  15.6 us (20%)
  blocking collectives  14.4 us (19%)
  Pallas kernels  14.1 us (18%)
  other arithmetic  1.5 us (2%)
  between operations  0.89 us (1%)
    ppermute x17, starting transfers between devices, move(): return lax.ppermute(value, axes, pairs)  30.1 us
    ppermute x17, waiting for transfers between devices, move(): return lax.ppermute(value, axes, pairs)  15.6 us
    all_to_all x1, blocking collectives, on_device(): parts = lax.all_to_all(pair, ('x', 'y'), 0, 0, tiled=True)  14.4 us
    pallas_call x2, Pallas kernels, compress(): pl.pallas_call(body, in_specs=in_specs, out_specs=out_specs, out_shape=ou...  8.82 us
    pallas_call x3, Pallas kernels, project(): pl.pallas_call(body, in_specs=in_specs, out_specs=pl.BlockSpec(memory_spa...  5.25 us
  transfers between devices with their start and end apart: 17, of which 9 were waited for; matrix products, arithmetic and copies ran while one was open for 0% of the time, Pallas kernels for 9%

profile of v3, /device:TPU:1, one launch (start us, length us, event | category | flops | bytes accessed | tf_op | source)
XLA Modules:
  0.0 76.7 jit_solution(11030274762740379547)
XLA Ops:
  0.6 0.0 copy-start.1
  0.6 4.7 %compress_first.1 = (f32[1,64,7168]{2,1,0:T(8,128)}, f32[4,4,7,16,128]{4,3,2,1,0:T(8,128)}, f32[7,16,128]{2,1,0:T(8,128)}) custom-call(s32[4,112]{1,0:T(4,128)} %bitcast.27, f32[1,64,7168]{2,1,0:T(8,128)} %refs_1_.3, bf16[1,64,7168]{2,1,0:T(8,128)(2,1)} %refs_2_.3, bf16[64,7168]{1,0:T(8,128)(2,1)} %refs_3_.3, bf16[64,256]{1,0:T(8,128)(2,1)} %constant.18.clone.refs_4_, ...), custom_call_target="tpu_custom_call" | custom-call | flops 939524096 | bytes 2752512 | tf_op jit(solution)/shard_map/compress_first/pallas_call | solution.py:209
  5.3 0.0 copy-start
  5.3 3.3 %collective-permute-start = (f32[4,4,7,16,128]{4,3,2,1,0:T(8,128)}, f32[4,4,7,16,128]{4,3,2,1,0:T(8,128)S(1)}, u32[]{:S(2)}, u32[]{:S(2)}) collective-permute-start(f32[4,4,7,16,128]{4,3,2,1,0:T(8,128)} %get-tuple-element.17), channel_id=1, source_target_pairs={{0,4},{4,0},{1,5},{5,1},{2,6},{6,2},{3,7},{7,3},{8,12},{12,8},{9,1... | collective-permute-start | bytes 2752520 | tf_op jit(solution)/shard_map/ppermute | solution.py:339
  8.6 4.2 %compress_second.1 = (f32[1,64,7168]{2,1,0:T(8,128)}, f32[4,4,7,16,128]{4,3,2,1,0:T(8,128)}) custom-call(s32[4,112]{1,0:T(4,128)} %bitcast.28, f32[1,64,7168]{2,1,0:T(8,128)} %refs_1_.3, bf16[1,64,7168]{2,1,0:T(8,128)(2,1)} %refs_2_.3, bf16[64,7168]{1,0:T(8,128)(2,1)} %refs_3_.3, ...), custom_call_target="tpu_custom_call", output_to_operand_aliasing={{0}: (8, {})} | custom-call | flops 939524096 | bytes 2752512 | tf_op jit(solution)/shard_map/compress_second/pallas_call | solution.py:209
  12.8 0.0 collective-permute-done
  12.8 1.3 %add_convert_fusion = bf16[4,4,7,16,128]{4,3,2,1,0:T(8,128)(2,1)S(1)} fusion(f32[4,4,7,16,128]{4,3,2,1,0:T(8,128)} %get-tuple-element.16, f32[4,4,7,16,128]{4,3,2,1,0:T(8,128)S(1)} %collective-permute-done), kind=kLoop, calls=%fused_computation.1 | loop fusion | flops 458752 | bytes 2293760 | tf_op jit(solution)/shard_map/convert_element_type | solution.py:390
  14.1 14.4 %all_to_all.5 = bf16[16,7,16,128]{3,2,1,0:T(8,128)(2,1)S(1)} all-to-all(bf16[16,7,16,128]{3,2,1,0:T(8,128)(2,1)S(1)} %bitcast.19), channel_id=1, replica_groups=mesh['x'=4,'y'=4,'zl'=2,'core'=2,'fsdp'=4] {'x','y'}, dimensions={0} | all-to-all | bytes 917504 | tf_op jit(solution)/shard_map/all_to_all | solution.py:392
  28.5 0.1 convert_reduce_fusion
  28.6 2.9 %collective-permute-start.1 = (f32[7,16,128]{2,1,0:T(8,128)S(1)}, f32[7,16,128]{2,1,0:T(8,128)S(1)}, u32[]{:S(2)}, u32[]{:S(2)}) collective-permute-start(f32[7,16,128]{2,1,0:T(8,128)S(1)} %convert_reduce_fusion), channel_id=1, source_target_pairs={{0,40},{4,140},{8,32},{12,132},{16,56},{20,156},{24,48},{28,148},{... | collective-permute-start | bytes 172040 | tf_op jit(solution)/shard_map/ppermute | solution.py:339
  31.5 2.7 %collective-permute-done.1 = f32[7,16,128]{2,1,0:T(8,128)S(1)} collective-permute-done((f32[7,16,128]{2,1,0:T(8,128)S(1)}, f32[7,16,128]{2,1,0:T(8,128)S(1)}, u32[]{:S(2)}, u32[]{:S(2)}) %collective-permute-start.1) | collective-permute-done | bytes 57376 | tf_op jit(solution)/shard_map/ppermute | solution.py:339
  34.1 0.0 copy-done
  34.1 6.1 %collective-permute-start.4 = (bf16[7,16,128]{2,1,0:T(8,128)(2,1)S(1)}, bf16[7,16,128]{2,1,0:T(8,128)(2,1)S(1)}, u32[]{:S(2)}, u32[]{:S(2)}) collective-permute-start(bf16[7,16,128]{2,1,0:T(8,128)(2,1)S(1)} %subtract_convert_fusion), channel_id=1, source_target_pairs={{0,3},{1,2},{2,1},{3,0},{4,7},{5,6},{6,5},{7,4},{8,11},{9,10},{10,... | collective-permute-start | bytes 86024 | tf_op jit(solution)/shard_map/ppermute | solution.py:339
  40.3 1.0 %collective-permute-start.3 = (bf16[7,16,128]{2,1,0:T(8,128)(2,1)S(1)}, bf16[7,16,128]{2,1,0:T(8,128)(2,1)S(1)}, u32[]{:S(2)}, u32[]{:S(2)}) collective-permute-start(bf16[7,16,128]{2,1,0:T(8,128)(2,1)S(1)} %subtract_convert_fusion), channel_id=1, source_target_pairs={{0,2},{1,3},{2,0},{3,1},{4,6},{5,7},{6,4},{7,5},{8,10},{9,11},{10,... | collective-permute-start | bytes 86024 | tf_op jit(solution)/shard_map/ppermute | solution.py:339
  41.2 1.2 %collective-permute-start.2 = (bf16[7,16,128]{2,1,0:T(8,128)(2,1)S(1)}, bf16[7,16,128]{2,1,0:T(8,128)(2,1)S(1)}, u32[]{:S(2)}, u32[]{:S(2)}) collective-permute-start(bf16[7,16,128]{2,1,0:T(8,128)(2,1)S(1)} %subtract_convert_fusion), channel_id=1, source_target_pairs={{0,1},{1,0},{2,3},{3,2},{4,5},{5,4},{6,7},{7,6},{8,9},{9,8},{10,11... | collective-permute-start | bytes 86024 | tf_op jit(solution)/shard_map/ppermute | solution.py:339
  42.4 0.0 collective-permute-done.4
  42.4 4.6 %collective-permute-done.3 = bf16[7,16,128]{2,1,0:T(8,128)(2,1)S(1)} collective-permute-done((bf16[7,16,128]{2,1,0:T(8,128)(2,1)S(1)}, bf16[7,16,128]{2,1,0:T(8,128)(2,1)S(1)}, u32[]{:S(2)}, u32[]{:S(2)}) %collective-permute-start.3) | collective-permute-done | bytes 28704 | tf_op jit(solution)/shard_map/ppermute | solution.py:339
  47.0 0.0 collective-permute-done.2
  47.0 1.7 %collective-permute-start.6 = (bf16[4,7,16,128]{3,2,1,0:T(8,128)(2,1)S(1)}, bf16[4,7,16,128]{3,2,1,0:T(8,128)(2,1)S(1)}, u32[]{:S(2)}, u32[]{:S(2)}) collective-permute-start(bf16[4,7,16,128]{3,2,1,0:T(8,128)(2,1)S(1)} %get-tuple-element.27), channel_id=1, source_target_pairs={{0,128},{4,36},{16,144},{20,52},{32,160},{36,4},{48,176},{52,20},{... | collective-permute-start | bytes 344072 | tf_op jit(solution)/shard_map/ppermute | solution.py:339
  48.7 0.3 collective-permute-start.5
  49.0 2.4 %collective-permute-start.7 = (bf16[4,7,16,128]{3,2,1,0:T(8,128)(2,1)S(1)}, bf16[4,7,16,128]{3,2,1,0:T(8,128)(2,1)S(1)}, u32[]{:S(2)}, u32[]{:S(2)}) collective-permute-start(bf16[4,7,16,128]{3,2,1,0:T(8,128)(2,1)S(1)} %get-tuple-element.27), channel_id=1, source_target_pairs={{0,192},{4,52},{16,208},{20,4},{32,224},{36,20},{48,240},{52,36},{... | collective-permute-start | bytes 344072 | tf_op jit(solution)/shard_map/ppermute | solution.py:339
  51.4 0.9 %collective-permute-done.6 = bf16[4,7,16,128]{3,2,1,0:T(8,128)(2,1)S(1)} collective-permute-done((bf16[4,7,16,128]{3,2,1,0:T(8,128)(2,1)S(1)}, bf16[4,7,16,128]{3,2,1,0:T(8,128)(2,1)S(1)}, u32[]{:S(2)}, u32[]{:S(2)}) %collective-permute-start.6) | collective-permute-done | bytes 114720 | tf_op jit(solution)/shard_map/ppermute | solution.py:339
  52.3 1.3 %collective-permute-done.5 = bf16[4,7,16,128]{3,2,1,0:T(8,128)(2,1)S(1)} collective-permute-done((bf16[4,7,16,128]{3,2,1,0:T(8,128)(2,1)S(1)}, bf16[4,7,16,128]{3,2,1,0:T(8,128)(2,1)S(1)}, u32[]{:S(2)}, u32[]{:S(2)}) %collective-permute-start.5) | collective-permute-done | bytes 114720 | tf_op jit(solution)/shard_map/ppermute | solution.py:339
  53.5 0.0 collective-permute-done.7
  53.5 0.1 pad_maximum_fusion.rest_0_.refs_0_
  53.6 1.6 %collective-permute-start.9 = (bf16[4,4,7,16,128]{4,3,2,1,0:T(8,128)(2,1)S(1)}, bf16[4,4,7,16,128]{4,3,2,1,0:T(8,128)(2,1)S(1)}, u32[]{:S(2)}, u32[]{:S(2)}) collective-permute-start(bf16[4,4,7,16,128]{4,3,2,1,0:T(8,128)(2,1)S(1)} %pad_maximum_fusion.rest_0_.refs_0_), channel_id=1, source_target_pairs={{0,48},{4,196},{16,0},{20,212},{32,16},{36,228},{48,32},{52,244},{... | collective-permute-start | bytes 1376264 | tf_op jit(solution)/shard_map/ppermute | solution.py:339
  55.2 0.0 collective-permute-start.8
  55.2 1.2 %collective-permute-start.11 = (bf16[2,4,7,16,128]{4,3,2,1,0:T(8,128)(2,1)S(1)}, bf16[2,4,7,16,128]{4,3,2,1,0:T(8,128)(2,1)S(1)}, u32[]{:S(2)}, u32[]{:S(2)}) collective-permute-start(bf16[2,4,7,16,128]{4,3,2,1,0:T(8,128)(2,1)S(1)} %get-tuple-element.24), channel_id=1, source_target_pairs={{0,11},{1,8},{2,9},{3,10},{8,0},{9,1},{10,2},{11,3},{4,15},{5,12},... | collective-permute-start | bytes 688136 | tf_op jit(solution)/shard_map/ppermute | solution.py:339
  56.4 0.3 collective-permute-start.10
  56.7 0.0 copy-done.1
  56.8 0.1 copy.25.tokens
  56.9 1.2 %project.3.refs_5_ = bf16[128,28672]{1,0:T(8,128)(2,1)} custom-call(bf16[128,64]{1,0:T(8,128)(2,1)S(1)} %copy.25.tokens, bf16[4,4,7,16,128]{4,3,2,1,0:T(8,128)(2,1)S(1)} %pad_maximum_fusion.rest_0_.refs_0_), custom_call_target="tpu_custom_call" | custom-call | flops 58720256 | bytes 1835008 | tf_op jit(solution)/shard_map/project/pallas_call | solution.py:294
  58.1 2.1 %collective-permute-done.11.refs_4_ = bf16[2,4,7,16,128]{4,3,2,1,0:T(8,128)(2,1)S(1)} collective-permute-done((bf16[2,4,7,16,128]{4,3,2,1,0:T(8,128)(2,1)S(1)}, bf16[2,4,7,16,128]{4,3,2,1,0:T(8,128)(2,1)S(1)}, u32[]{:S(2)}, u32[]{:S(2)}) %collective-permute-start.11) | collective-permute-done | bytes 229408 | tf_op jit(solution)/shard_map/ppermute | solution.py:339
  60.2 2.4 %collective-permute-done.10.refs_3_ = bf16[2,4,7,16,128]{4,3,2,1,0:T(8,128)(2,1)S(1)} collective-permute-done((bf16[2,4,7,16,128]{4,3,2,1,0:T(8,128)(2,1)S(1)}, bf16[2,4,7,16,128]{4,3,2,1,0:T(8,128)(2,1)S(1)}, u32[]{:S(2)}, u32[]{:S(2)}) %collective-permute-start.10) | collective-permute-done | bytes 229408 | tf_op jit(solution)/shard_map/ppermute | solution.py:339
  62.5 0.0 collective-permute-done.9.refs_2_
  62.5 1.2 %collective-permute-done.8.refs_1_ = bf16[4,4,7,16,128]{4,3,2,1,0:T(8,128)(2,1)S(1)} collective-permute-done((bf16[4,4,7,16,128]{4,3,2,1,0:T(8,128)(2,1)S(1)}, bf16[4,4,7,16,128]{4,3,2,1,0:T(8,128)(2,1)S(1)}, u32[]{:S(2)}, u32[]{:S(2)}) %collective-permute-start.8) | collective-permute-done | bytes 458784 | tf_op jit(solution)/shard_map/ppermute | solution.py:339
  63.7 7.2 %collective-permute-start.12 = (bf16[4,4,7,16,128]{4,3,2,1,0:T(8,128)(2,1)S(1)}, bf16[4,4,7,16,128]{4,3,2,1,0:T(8,128)(2,1)S(1)}, u32[]{:S(2)}, u32[]{:S(2)}) collective-permute-start(bf16[4,4,7,16,128]{4,3,2,1,0:T(8,128)(2,1)S(1)} %get-tuple-element.18), channel_id=1, source_target_pairs={{0,4},{4,0},{1,5},{5,1},{2,6},{6,2},{3,7},{7,3},{8,12},{12,8},{9,1... | collective-permute-start | bytes 1376264 | tf_op jit(solution)/shard_map/ppermute | solution.py:339
  70.9 0.1 collective-permute-start.13
  71.0 0.4 collective-permute-start.14
  71.4 0.1 collective-permute-start.15
  71.5 0.4 collective-permute-start.16
  71.9 1.8 %project.4.rest_5_ = bf16[128,28672]{1,0:T(8,128)(2,1)} custom-call(bf16[128,64]{1,0:T(8,128)(2,1)S(1)} %copy.25.tokens, bf16[4,4,7,16,128]{4,3,2,1,0:T(8,128)(2,1)S(1)} %get-tuple-element.19.rest_0_, bf16[4,4,7,16,128]{4,3,2,1,0:T(8,128)(2,1)S(1)} %get-tuple-element.20.rest_1_, ...), custom_call_target="tpu_custom_call", output_to_operand_aliasing={{}: (5, {})} | custom-call | flops 176160768 | bytes 5505024 | tf_op jit(solution)/shard_map/project/pallas_call | solution.py:294
  73.8 0.2 collective-permute-done.15.rest_3_
  74.0 0.3 collective-permute-done.16.rest_4_
  74.3 0.0 collective-permute-done.12.rest_0_
  74.3 0.0 collective-permute-done.13.rest_1_
  74.3 0.0 collective-permute-done.14.rest_2_
  74.3 2.2 %project.5 = bf16[128,28672]{1,0:T(8,128)(2,1)} custom-call(bf16[128,64]{1,0:T(8,128)(2,1)S(1)} %copy.25.tokens, bf16[4,4,7,16,128]{4,3,2,1,0:T(8,128)(2,1)S(1)} %collective-permute-done.12.rest_0_, bf16[4,4,7,16,128]{4,3,2,1,0:T(8,128)(2,1)S(1)} %collective-permute-done.13.rest_1_, ...), custom_call_target="tpu_custom_call", output_to_operand_aliasing={{}: (6, {})} | custom-call | flops 234881024 | bytes 7340032 | tf_op jit(solution)/shard_map/project/pallas_call | solution.py:294
  (4 shorter events, 0.1 us)
Async XLA Ops:
  0.6 56.1 %copy-start.1 = (bf16[128,64]{0,1:T(8,128)(2,1)S(1)}, bf16[128,64]{0,1:T(8,128)(2,1)}, u32[]{:S(2)}) copy-start(bf16[128,64]{0,1:T(8,128)(2,1)} %param.12) | copy-start | bytes 49156
  5.3 28.8 %copy-start = (f32[7,16,128]{2,1,0:T(8,128)S(1)}, f32[7,16,128]{2,1,0:T(8,128)}, u32[]{:S(2)}) copy-start(f32[7,16,128]{2,1,0:T(8,128)} %get-tuple-element.15) | copy-start | bytes 172036
  5.3 7.5 %collective-permute-start = (f32[4,4,7,16,128]{4,3,2,1,0:T(8,128)}, f32[4,4,7,16,128]{4,3,2,1,0:T(8,128)S(1)}, u32[]{:S(2)}, u32[]{:S(2)}) collective-permute-start(f32[4,4,7,16,128]{4,3,2,1,0:T(8,128)} %get-tuple-element.17), channel_id=1, source_target_pairs={{0,4},{4,0},{1,5},{5,1},{2,6},{6,2},{3,7},{7,3},{8,12},{12,8},{9,1... | collective-permute-start | bytes 2752520 | tf_op jit(solution)/shard_map/ppermute | solution.py:339
  28.6 5.5 %collective-permute-start.1 = (f32[7,16,128]{2,1,0:T(8,128)S(1)}, f32[7,16,128]{2,1,0:T(8,128)S(1)}, u32[]{:S(2)}, u32[]{:S(2)}) collective-permute-start(f32[7,16,128]{2,1,0:T(8,128)S(1)} %convert_reduce_fusion), channel_id=1, source_target_pairs={{0,40},{4,140},{8,32},{12,132},{16,56},{20,156},{24,48},{28,148},{... | collective-permute-start | bytes 172040 | tf_op jit(solution)/shard_map/ppermute | solution.py:339
  34.1 8.3 %collective-permute-start.4 = (bf16[7,16,128]{2,1,0:T(8,128)(2,1)S(1)}, bf16[7,16,128]{2,1,0:T(8,128)(2,1)S(1)}, u32[]{:S(2)}, u32[]{:S(2)}) collective-permute-start(bf16[7,16,128]{2,1,0:T(8,128)(2,1)S(1)} %subtract_convert_fusion), channel_id=1, source_target_pairs={{0,3},{1,2},{2,1},{3,0},{4,7},{5,6},{6,5},{7,4},{8,11},{9,10},{10,... | collective-permute-start | bytes 86024 | tf_op jit(solution)/shard_map/ppermute | solution.py:339
  40.3 6.8 %collective-permute-start.3 = (bf16[7,16,128]{2,1,0:T(8,128)(2,1)S(1)}, bf16[7,16,128]{2,1,0:T(8,128)(2,1)S(1)}, u32[]{:S(2)}, u32[]{:S(2)}) collective-permute-start(bf16[7,16,128]{2,1,0:T(8,128)(2,1)S(1)} %subtract_convert_fusion), channel_id=1, source_target_pairs={{0,2},{1,3},{2,0},{3,1},{4,6},{5,7},{6,4},{7,5},{8,10},{9,11},{10,... | collective-permute-start | bytes 86024 | tf_op jit(solution)/shard_map/ppermute | solution.py:339
  41.2 5.8 %collective-permute-start.2 = (bf16[7,16,128]{2,1,0:T(8,128)(2,1)S(1)}, bf16[7,16,128]{2,1,0:T(8,128)(2,1)S(1)}, u32[]{:S(2)}, u32[]{:S(2)}) collective-permute-start(bf16[7,16,128]{2,1,0:T(8,128)(2,1)S(1)} %subtract_convert_fusion), channel_id=1, source_target_pairs={{0,1},{1,0},{2,3},{3,2},{4,5},{5,4},{6,7},{7,6},{8,9},{9,8},{10,11... | collective-permute-start | bytes 86024 | tf_op jit(solution)/shard_map/ppermute | solution.py:339
  47.0 5.2 %collective-permute-start.6 = (bf16[4,7,16,128]{3,2,1,0:T(8,128)(2,1)S(1)}, bf16[4,7,16,128]{3,2,1,0:T(8,128)(2,1)S(1)}, u32[]{:S(2)}, u32[]{:S(2)}) collective-permute-start(bf16[4,7,16,128]{3,2,1,0:T(8,128)(2,1)S(1)} %get-tuple-element.27), channel_id=1, source_target_pairs={{0,128},{4,36},{16,144},{20,52},{32,160},{36,4},{48,176},{52,20},{... | collective-permute-start | bytes 344072 | tf_op jit(solution)/shard_map/ppermute | solution.py:339
  48.7 4.9 %collective-permute-start.5 = (bf16[4,7,16,128]{3,2,1,0:T(8,128)(2,1)S(1)}, bf16[4,7,16,128]{3,2,1,0:T(8,128)(2,1)S(1)}, u32[]{:S(2)}, u32[]{:S(2)}) collective-permute-start(bf16[4,7,16,128]{3,2,1,0:T(8,128)(2,1)S(1)} %get-tuple-element.27), channel_id=1, source_target_pairs={{0,64},{4,20},{16,80},{20,36},{32,96},{36,52},{48,112},{52,4},{64,... | collective-permute-start | bytes 344072 | tf_op jit(solution)/shard_map/ppermute | solution.py:339
  49.0 4.6 %collective-permute-start.7 = (bf16[4,7,16,128]{3,2,1,0:T(8,128)(2,1)S(1)}, bf16[4,7,16,128]{3,2,1,0:T(8,128)(2,1)S(1)}, u32[]{:S(2)}, u32[]{:S(2)}) collective-permute-start(bf16[4,7,16,128]{3,2,1,0:T(8,128)(2,1)S(1)} %get-tuple-element.27), channel_id=1, source_target_pairs={{0,192},{4,52},{16,208},{20,4},{32,224},{36,20},{48,240},{52,36},{... | collective-permute-start | bytes 344072 | tf_op jit(solution)/shard_map/ppermute | solution.py:339
  53.6 8.9 %collective-permute-start.9 = (bf16[4,4,7,16,128]{4,3,2,1,0:T(8,128)(2,1)S(1)}, bf16[4,4,7,16,128]{4,3,2,1,0:T(8,128)(2,1)S(1)}, u32[]{:S(2)}, u32[]{:S(2)}) collective-permute-start(bf16[4,4,7,16,128]{4,3,2,1,0:T(8,128)(2,1)S(1)} %pad_maximum_fusion.rest_0_.refs_0_), channel_id=1, source_target_pairs={{0,48},{4,196},{16,0},{20,212},{32,16},{36,228},{48,32},{52,244},{... | collective-permute-start | bytes 1376264 | tf_op jit(solution)/shard_map/ppermute | solution.py:339
  55.2 8.5 %collective-permute-start.8 = (bf16[4,4,7,16,128]{4,3,2,1,0:T(8,128)(2,1)S(1)}, bf16[4,4,7,16,128]{4,3,2,1,0:T(8,128)(2,1)S(1)}, u32[]{:S(2)}, u32[]{:S(2)}) collective-permute-start(bf16[4,4,7,16,128]{4,3,2,1,0:T(8,128)(2,1)S(1)} %pad_maximum_fusion.rest_0_.refs_0_), channel_id=1, source_target_pairs={{0,16},{4,68},{16,32},{20,84},{32,48},{36,100},{48,0},{52,116},{64... | collective-permute-start | bytes 1376264 | tf_op jit(solution)/shard_map/ppermute | solution.py:339
  55.2 4.9 %collective-permute-start.11 = (bf16[2,4,7,16,128]{4,3,2,1,0:T(8,128)(2,1)S(1)}, bf16[2,4,7,16,128]{4,3,2,1,0:T(8,128)(2,1)S(1)}, u32[]{:S(2)}, u32[]{:S(2)}) collective-permute-start(bf16[2,4,7,16,128]{4,3,2,1,0:T(8,128)(2,1)S(1)} %get-tuple-element.24), channel_id=1, source_target_pairs={{0,11},{1,8},{2,9},{3,10},{8,0},{9,1},{10,2},{11,3},{4,15},{5,12},... | collective-permute-start | bytes 688136 | tf_op jit(solution)/shard_map/ppermute | solution.py:339
  56.4 6.1 %collective-permute-start.10 = (bf16[2,4,7,16,128]{4,3,2,1,0:T(8,128)(2,1)S(1)}, bf16[2,4,7,16,128]{4,3,2,1,0:T(8,128)(2,1)S(1)}, u32[]{:S(2)}, u32[]{:S(2)}) collective-permute-start(bf16[2,4,7,16,128]{4,3,2,1,0:T(8,128)(2,1)S(1)} %get-tuple-element.25), channel_id=1, source_target_pairs={{0,8},{1,9},{2,10},{3,11},{8,1},{9,2},{10,3},{11,0},{4,12},{5,13},... | collective-permute-start | bytes 688136 | tf_op jit(solution)/shard_map/ppermute | solution.py:339
  63.7 10.6 %collective-permute-start.12 = (bf16[4,4,7,16,128]{4,3,2,1,0:T(8,128)(2,1)S(1)}, bf16[4,4,7,16,128]{4,3,2,1,0:T(8,128)(2,1)S(1)}, u32[]{:S(2)}, u32[]{:S(2)}) collective-permute-start(bf16[4,4,7,16,128]{4,3,2,1,0:T(8,128)(2,1)S(1)} %get-tuple-element.18), channel_id=1, source_target_pairs={{0,4},{4,0},{1,5},{5,1},{2,6},{6,2},{3,7},{7,3},{8,12},{12,8},{9,1... | collective-permute-start | bytes 1376264 | tf_op jit(solution)/shard_map/ppermute | solution.py:339
  70.9 3.4 %collective-permute-start.13 = (bf16[4,4,7,16,128]{4,3,2,1,0:T(8,128)(2,1)S(1)}, bf16[4,4,7,16,128]{4,3,2,1,0:T(8,128)(2,1)S(1)}, u32[]{:S(2)}, u32[]{:S(2)}) collective-permute-start(bf16[4,4,7,16,128]{4,3,2,1,0:T(8,128)(2,1)S(1)} %get-tuple-element.19.rest_0_), channel_id=1, source_target_pairs={{0,4},{4,0},{1,5},{5,1},{2,6},{6,2},{3,7},{7,3},{8,12},{12,8},{9,1... | collective-permute-start | bytes 1376264 | tf_op jit(solution)/shard_map/ppermute | solution.py:339
  71.0 3.3 %collective-permute-start.14 = (bf16[4,4,7,16,128]{4,3,2,1,0:T(8,128)(2,1)S(1)}, bf16[4,4,7,16,128]{4,3,2,1,0:T(8,128)(2,1)S(1)}, u32[]{:S(2)}, u32[]{:S(2)}) collective-permute-start(bf16[4,4,7,16,128]{4,3,2,1,0:T(8,128)(2,1)S(1)} %get-tuple-element.20.rest_1_), channel_id=1, source_target_pairs={{0,4},{4,0},{1,5},{5,1},{2,6},{6,2},{3,7},{7,3},{8,12},{12,8},{9,1... | collective-permute-start | bytes 1376264 | tf_op jit(solution)/shard_map/ppermute | solution.py:339
  71.4 2.6 %collective-permute-start.15 = (bf16[2,4,7,16,128]{4,3,2,1,0:T(8,128)(2,1)S(1)}, bf16[2,4,7,16,128]{4,3,2,1,0:T(8,128)(2,1)S(1)}, u32[]{:S(2)}, u32[]{:S(2)}) collective-permute-start(bf16[2,4,7,16,128]{4,3,2,1,0:T(8,128)(2,1)S(1)} %get-tuple-element.21.rest_2_), channel_id=1, source_target_pairs={{0,4},{4,0},{1,5},{5,1},{2,6},{6,2},{3,7},{7,3},{8,12},{12,8},{9,1... | collective-permute-start | bytes 688136 | tf_op jit(solution)/shard_map/ppermute | solution.py:339
  71.5 2.8 %collective-permute-start.16 = (bf16[2,4,7,16,128]{4,3,2,1,0:T(8,128)(2,1)S(1)}, bf16[2,4,7,16,128]{4,3,2,1,0:T(8,128)(2,1)S(1)}, u32[]{:S(2)}, u32[]{:S(2)}) collective-permute-start(bf16[2,4,7,16,128]{4,3,2,1,0:T(8,128)(2,1)S(1)} %get-tuple-element.22.rest_3_), channel_id=1, source_target_pairs={{0,4},{4,0},{1,5},{5,1},{2,6},{6,2},{3,7},{7,3},{8,12},{12,8},{9,1... | collective-permute-start | bytes 688136 | tf_op jit(solution)/shard_map/ppermute | solution.py:339

commit v4 on v3

--- a/solution.py
+++ b/solution.py
@@ -74,17 +74,14 @@
     return lax.rem(second + 2 * low, SIZES[1])
 
 
-def compress_kernel(first, tiles, steps, index, momentum, gradient, weight, *rest):
+def compress_kernel(first, tiles, steps, index, momentum, gradient, *rest):
     place = whereabouts()
     operands, rest = rest[:4], rest[4:]
-    if first:
-        new_momentum, sent, own_weight = rest[:3]
-    else:
-        new_momentum, sent = rest[1:3]
-    moment_buf, grad_buf, new_buf, weight_buf, *rest = rest[3:]
+    rest = rest if first else rest[1:]
+    new_momentum, sent, moment_buf, grad_buf, new_buf, *rest = rest
     tables, (in_sems, out_sems, table_sems, sent_buf, sent_sems, picked) = rest[:4], rest[4:]
     wide = tiles * LANES
-    first_axis, second_axis, low, core = place[:4]
+    low, core = place[2:4]
     half = (1 - core) if first else core
 
     spans = [slice(a * wide, b * wide) for a, b in zip(BATCHES, BATCHES[1:])]
@@ -108,16 +105,9 @@
     table_loads = [
         pltpu.make_async_copy(operands[n], tables[n], table_sems.at[n]) for n in range(4)
     ]
-    index_load = pltpu.make_async_copy(index, picked, table_sems.at[5])
+    index_load = pltpu.make_async_copy(index, picked, table_sems.at[4])
     for copy in (*loads[0], index_load, *table_loads, *(copy for pair in loads[1:] for copy in pair)):
         copy.start()
-    if first:
-        at = pl.multiple_of((core * steps + chunk_column(second_axis, low)) * wide, wide)
-        row = pl.multiple_of(first_axis * ROWS, ROWS)
-        weight_load = pltpu.make_async_copy(
-            weight.at[pl.ds(row, ROWS), pl.ds(at, wide)], weight_buf, table_sems.at[4]
-        )
-        weight_load.start()
     lane = lax.broadcasted_iota(jnp.int32, (BLOCK, LANES), 1)
     lane_block = (lane % GROUP) // BLOCK
     left_group = lane < GROUP
@@ -173,32 +163,25 @@
                 )
                 store.start()
                 stores.append(store)
-    if first:
-        weight_load.wait()
-        for t in range(tiles):
-            own_weight[t] = weight_buf[:, t * LANES : (t + 1) * LANES].astype(F32)
     for store in stores:
         store.wait()
 
 
-def compress(first, picked, momentum, gradient, weight, tables, partial=None):
-    height, breadth = weight.shape
+def compress(first, picked, momentum, gradient, tables, partial=None):
+    _, height, breadth = momentum.shape
     steps = SIZES[1]
     wide = breadth // 2 // steps
     tiles = wide // LANES
     chunk = (tiles, ROWS, LANES)
-    in_specs = [pl.BlockSpec(memory_space=pltpu.HBM)] * (4 + len(tables))
+    in_specs = [pl.BlockSpec(memory_space=pltpu.HBM)] * (3 + len(tables))
     out_shape = [
         jax.ShapeDtypeStruct((1, height, breadth), F32),
         jax.ShapeDtypeStruct((SIZES[0], steps) + chunk, F32),
     ]
     out_specs = [pl.BlockSpec(memory_space=pltpu.HBM)] * 2
-    operands = [picked, momentum, gradient, weight, *tables]
+    operands = [picked, momentum, gradient, *tables]
     aliases = {}
-    if first:
-        out_shape.append(jax.ShapeDtypeStruct(chunk, F32))
-        out_specs.append(pl.BlockSpec(memory_space=pltpu.VMEM))
-    else:
+    if not first:
         aliases = {len(operands): 0}
         operands.append(partial)
         in_specs.append(pl.BlockSpec(memory_space=pltpu.HBM))
@@ -215,11 +198,10 @@
             pltpu.VMEM((height, steps * wide), F32),
             pltpu.VMEM((height, steps * wide), BF16),
             pltpu.VMEM((height, steps * wide), F32),
-            pltpu.VMEM((ROWS, wide), BF16),
             *(pltpu.VMEM(table.shape, BF16) for table in tables),
             pltpu.SemaphoreType.DMA((steps, 2)),
             pltpu.SemaphoreType.DMA((steps,)),
-            pltpu.SemaphoreType.DMA((6,)),
+            pltpu.SemaphoreType.DMA((5,)),
             pltpu.VMEM((steps, SIZES[0]) + chunk, F32),
             pltpu.SemaphoreType.DMA((steps, SIZES[0])),
             pltpu.SMEM(picked.shape, jnp.int32),
@@ -243,6 +225,32 @@
 
 def above_shard(shard, low, k):
     return ((shard + low) & 1) ^ k
+
+
+def own_part(weight, summed, scale):
+    tiles, rows, lanes = summed.shape
+    wide = tiles * lanes
+
+    def body(weight, summed, out, held, sem):
+        first, second, low, core = whereabouts()[:4]
+        row = pl.multiple_of(first * rows, rows)
+        at = pl.multiple_of((core * SIZES[1] + chunk_column(second, low)) * wide, wide)
+        load = pltpu.make_async_copy(weight.at[pl.ds(row, rows), pl.ds(at, wide)], held, sem)
+        load.start()
+        load.wait()
+        for t in range(tiles):
+            own = held[:, t * lanes : (t + 1) * lanes].astype(F32)
+            out[t] = own - scale * summed[t]
+
+    return pl.pallas_call(
+        body,
+        in_specs=[pl.BlockSpec(memory_space=pltpu.HBM), pl.BlockSpec(memory_space=pltpu.VMEM)],
+        out_specs=pl.BlockSpec(memory_space=pltpu.VMEM),
+        out_shape=jax.ShapeDtypeStruct(summed.shape, F32),
+        scratch_shapes=[pltpu.VMEM((rows, wide), BF16), pltpu.SemaphoreType.DMA],
+        compiler_params=pltpu.CompilerParams(vmem_limit_bytes=16 * 2**20),
+        name="own_part",
+    )(weight, summed)
 
 
 def project(tokens, pieces, own, steps, shards, breadth, partial=None):
@@ -382,18 +390,18 @@
         jnp.asarray(left_operand(cosines.T)),
         jnp.asarray(right_operand(cosines)),
     ]
-    partial, away, own_weight = compress(True, picked, momentum, gradient, weight, tables)
+    partial, away = compress(True, picked, momentum, gradient, tables)
     arrived = swap(away)
     new_momentum, kept = compress(
-        False, picked, momentum, gradient, weight, tables, partial
+        False, picked, momentum, gradient, tables, partial
     )
     pair = (kept + arrived).astype(BF16)
     pair = pair.reshape((plane,) + pair.shape[2:])
     parts = lax.all_to_all(pair, ("x", "y"), 0, 0, tiled=True)
     summed = jnp.sum(parts.astype(F32), axis=0)
-    total = summed + across(summed)
-    replicas = float(np.prod(SIZES))
-    chunk = (own_weight - (STEP / replicas) * total).astype(BF16)
+    scale = STEP / float(np.prod(SIZES))
+    beyond = across(summed)
+    chunk = (own_part(weight, summed, scale) - scale * beyond).astype(BF16)
     row = jnp.stack([chunk] + [flip(chunk, k) for k in range(1, fsdp)])
     stack = jnp.stack([row] + [turn(row, d, False) for d in range(1, side)], axis=1)
     left, right = turn(stack, 1, True), turn(stack, 3, True)

time: 77 us -> 76.6 us (level)
  no operation moved by 1% of the time
where the time goes in v4:
time: 76.6 us; the launch traced here: 76.3 us
  starting transfers between devices  30.1 us (39%)
  waiting for transfers between devices  15.6 us (20%)
  blocking collectives  14.4 us (19%)
  Pallas kernels  13.7 us (18%)
  other arithmetic  1.49 us (2%)
  between operations  0.9 us (1%)
    ppermute x17, starting transfers between devices, move(): return lax.ppermute(value, axes, pairs)  30.1 us
    ppermute x17, waiting for transfers between devices, move(): return lax.ppermute(value, axes, pairs)  15.6 us
    all_to_all x1, blocking collectives, on_device(): parts = lax.all_to_all(pair, ('x', 'y'), 0, 0, tiled=True)  14.4 us
    pallas_call x2, Pallas kernels, compress(): pl.pallas_call(body, in_specs=in_specs, out_specs=out_specs, out_shape=ou...  8.38 us
    pallas_call x3, Pallas kernels, project(): pl.pallas_call(body, in_specs=in_specs, out_specs=pl.BlockSpec(memory_spa...  5.26 us
  transfers between devices with their start and end apart: 17, of which 9 were waited for; matrix products, arithmetic and copies ran while one was open for 0% of the time, Pallas kernels for 9%

profile of v4, /device:TPU:1, one launch (start us, length us, event | category | flops | bytes accessed | tf_op | source)
XLA Modules:
  0.0 76.3 jit_solution(13790545519227600689)
XLA Ops:
  0.6 0.0 copy-start
  0.6 0.0 copy-start.1
  0.6 4.2 %compress_first.1 = (f32[1,64,7168]{2,1,0:T(8,128)}, f32[4,4,7,16,128]{4,3,2,1,0:T(8,128)}) custom-call(s32[4,112]{1,0:T(4,128)} %bitcast.27, f32[1,64,7168]{2,1,0:T(8,128)} %refs_1_.3, bf16[1,64,7168]{2,1,0:T(8,128)(2,1)} %refs_2_.3, bf16[64,256]{1,0:T(8,128)(2,1)} %constant.18.clone.refs_3_, bf16[256,256]{1,0:T(8,128)(2,1)} %constant.19.clone.refs_4_, ...), custom_call_target="tpu_custom_call" | custom-call | flops 939524096 | bytes 2752512 | tf_op jit(solution)/shard_map/compress_first/pallas_call | solution.py:192
  4.9 3.3 %collective-permute-start = (f32[4,4,7,16,128]{4,3,2,1,0:T(8,128)}, f32[4,4,7,16,128]{4,3,2,1,0:T(8,128)S(1)}, u32[]{:S(2)}, u32[]{:S(2)}) collective-permute-start(f32[4,4,7,16,128]{4,3,2,1,0:T(8,128)} %get-tuple-element.15), channel_id=1, source_target_pairs={{0,4},{4,0},{1,5},{5,1},{2,6},{6,2},{3,7},{7,3},{8,12},{12,8},{9,1... | collective-permute-start | bytes 2752520 | tf_op jit(solution)/shard_map/ppermute | solution.py:347
  8.2 4.1 %compress_second.1 = (f32[1,64,7168]{2,1,0:T(8,128)}, f32[4,4,7,16,128]{4,3,2,1,0:T(8,128)}) custom-call(s32[4,112]{1,0:T(4,128)} %bitcast.28, f32[1,64,7168]{2,1,0:T(8,128)} %refs_1_.3, bf16[1,64,7168]{2,1,0:T(8,128)(2,1)} %refs_2_.3, bf16[64,256]{1,0:T(8,128)(2,1)} %constant.18.clone.refs_3_, ...), custom_call_target="tpu_custom_call", output_to_operand_aliasing={{0}: (7, {})} | custom-call | flops 939524096 | bytes 2752512 | tf_op jit(solution)/shard_map/compress_second/pallas_call | solution.py:192
  12.4 0.0 collective-permute-done
  12.4 1.3 %add_convert_fusion = bf16[4,4,7,16,128]{4,3,2,1,0:T(8,128)(2,1)S(1)} fusion(f32[4,4,7,16,128]{4,3,2,1,0:T(8,128)} %get-tuple-element.14, f32[4,4,7,16,128]{4,3,2,1,0:T(8,128)S(1)} %collective-permute-done), kind=kLoop, calls=%fused_computation.1 | loop fusion | flops 458752 | bytes 2293760 | tf_op jit(solution)/shard_map/convert_element_type | solution.py:398
  13.7 14.4 %all_to_all.5 = bf16[16,7,16,128]{3,2,1,0:T(8,128)(2,1)S(1)} all-to-all(bf16[16,7,16,128]{3,2,1,0:T(8,128)(2,1)S(1)} %bitcast.19), channel_id=1, replica_groups=mesh['x'=4,'y'=4,'zl'=2,'core'=2,'fsdp'=4] {'x','y'}, dimensions={0} | all-to-all | bytes 917504 | tf_op jit(solution)/shard_map/all_to_all | solution.py:400
  28.1 0.1 convert_reduce_fusion.summed
  28.2 2.9 %collective-permute-start.1 = (f32[7,16,128]{2,1,0:T(8,128)S(1)}, f32[7,16,128]{2,1,0:T(8,128)S(1)}, u32[]{:S(2)}, u32[]{:S(2)}) collective-permute-start(f32[7,16,128]{2,1,0:T(8,128)S(1)} %convert_reduce_fusion.summed), channel_id=1, source_target_pairs={{0,40},{4,140},{8,32},{12,132},{16,56},{20,156},{24,48},{28,148},{... | collective-permute-start | bytes 172040 | tf_op jit(solution)/shard_map/ppermute | solution.py:347
  31.0 0.0 copy-done
  31.1 2.6 %collective-permute-done.1 = f32[7,16,128]{2,1,0:T(8,128)S(1)} collective-permute-done((f32[7,16,128]{2,1,0:T(8,128)S(1)}, f32[7,16,128]{2,1,0:T(8,128)S(1)}, u32[]{:S(2)}, u32[]{:S(2)}) %collective-permute-start.1) | collective-permute-done | bytes 57376 | tf_op jit(solution)/shard_map/ppermute | solution.py:347
  33.7 6.1 %collective-permute-start.4 = (bf16[7,16,128]{2,1,0:T(8,128)(2,1)S(1)}, bf16[7,16,128]{2,1,0:T(8,128)(2,1)S(1)}, u32[]{:S(2)}, u32[]{:S(2)}) collective-permute-start(bf16[7,16,128]{2,1,0:T(8,128)(2,1)S(1)} %subtract_convert_fusion), channel_id=1, source_target_pairs={{0,3},{1,2},{2,1},{3,0},{4,7},{5,6},{6,5},{7,4},{8,11},{9,10},{10,... | collective-permute-start | bytes 86024 | tf_op jit(solution)/shard_map/ppermute | solution.py:347
  39.8 1.0 %collective-permute-start.3 = (bf16[7,16,128]{2,1,0:T(8,128)(2,1)S(1)}, bf16[7,16,128]{2,1,0:T(8,128)(2,1)S(1)}, u32[]{:S(2)}, u32[]{:S(2)}) collective-permute-start(bf16[7,16,128]{2,1,0:T(8,128)(2,1)S(1)} %subtract_convert_fusion), channel_id=1, source_target_pairs={{0,2},{1,3},{2,0},{3,1},{4,6},{5,7},{6,4},{7,5},{8,10},{9,11},{10,... | collective-permute-start | bytes 86024 | tf_op jit(solution)/shard_map/ppermute | solution.py:347
  40.8 1.2 %collective-permute-start.2 = (bf16[7,16,128]{2,1,0:T(8,128)(2,1)S(1)}, bf16[7,16,128]{2,1,0:T(8,128)(2,1)S(1)}, u32[]{:S(2)}, u32[]{:S(2)}) collective-permute-start(bf16[7,16,128]{2,1,0:T(8,128)(2,1)S(1)} %subtract_convert_fusion), channel_id=1, source_target_pairs={{0,1},{1,0},{2,3},{3,2},{4,5},{5,4},{6,7},{7,6},{8,9},{9,8},{10,11... | collective-permute-start | bytes 86024 | tf_op jit(solution)/shard_map/ppermute | solution.py:347
  42.0 0.0 collective-permute-done.4
  42.0 4.6 %collective-permute-done.3 = bf16[7,16,128]{2,1,0:T(8,128)(2,1)S(1)} collective-permute-done((bf16[7,16,128]{2,1,0:T(8,128)(2,1)S(1)}, bf16[7,16,128]{2,1,0:T(8,128)(2,1)S(1)}, u32[]{:S(2)}, u32[]{:S(2)}) %collective-permute-start.3) | collective-permute-done | bytes 28704 | tf_op jit(solution)/shard_map/ppermute | solution.py:347
  46.6 0.0 collective-permute-done.2
  46.6 1.7 %collective-permute-start.6 = (bf16[4,7,16,128]{3,2,1,0:T(8,128)(2,1)S(1)}, bf16[4,7,16,128]{3,2,1,0:T(8,128)(2,1)S(1)}, u32[]{:S(2)}, u32[]{:S(2)}) collective-permute-start(bf16[4,7,16,128]{3,2,1,0:T(8,128)(2,1)S(1)} %get-tuple-element.25), channel_id=1, source_target_pairs={{0,128},{4,36},{16,144},{20,52},{32,160},{36,4},{48,176},{52,20},{... | collective-permute-start | bytes 344072 | tf_op jit(solution)/shard_map/ppermute | solution.py:347
  48.2 0.3 collective-permute-start.5
  48.5 2.4 %collective-permute-start.7 = (bf16[4,7,16,128]{3,2,1,0:T(8,128)(2,1)S(1)}, bf16[4,7,16,128]{3,2,1,0:T(8,128)(2,1)S(1)}, u32[]{:S(2)}, u32[]{:S(2)}) collective-permute-start(bf16[4,7,16,128]{3,2,1,0:T(8,128)(2,1)S(1)} %get-tuple-element.25), channel_id=1, source_target_pairs={{0,192},{4,52},{16,208},{20,4},{32,224},{36,20},{48,240},{52,36},{... | collective-permute-start | bytes 344072 | tf_op jit(solution)/shard_map/ppermute | solution.py:347
  50.9 0.9 %collective-permute-done.6 = bf16[4,7,16,128]{3,2,1,0:T(8,128)(2,1)S(1)} collective-permute-done((bf16[4,7,16,128]{3,2,1,0:T(8,128)(2,1)S(1)}, bf16[4,7,16,128]{3,2,1,0:T(8,128)(2,1)S(1)}, u32[]{:S(2)}, u32[]{:S(2)}) %collective-permute-start.6) | collective-permute-done | bytes 114720 | tf_op jit(solution)/shard_map/ppermute | solution.py:347
  51.8 1.3 %collective-permute-done.5 = bf16[4,7,16,128]{3,2,1,0:T(8,128)(2,1)S(1)} collective-permute-done((bf16[4,7,16,128]{3,2,1,0:T(8,128)(2,1)S(1)}, bf16[4,7,16,128]{3,2,1,0:T(8,128)(2,1)S(1)}, u32[]{:S(2)}, u32[]{:S(2)}) %collective-permute-start.5) | collective-permute-done | bytes 114720 | tf_op jit(solution)/shard_map/ppermute | solution.py:347
  53.1 0.0 collective-permute-done.7
  53.1 0.1 pad_maximum_fusion.rest_0_.refs_0_
  53.2 1.6 %collective-permute-start.9 = (bf16[4,4,7,16,128]{4,3,2,1,0:T(8,128)(2,1)S(1)}, bf16[4,4,7,16,128]{4,3,2,1,0:T(8,128)(2,1)S(1)}, u32[]{:S(2)}, u32[]{:S(2)}) collective-permute-start(bf16[4,4,7,16,128]{4,3,2,1,0:T(8,128)(2,1)S(1)} %pad_maximum_fusion.rest_0_.refs_0_), channel_id=1, source_target_pairs={{0,48},{4,196},{16,0},{20,212},{32,16},{36,228},{48,32},{52,244},{... | collective-permute-start | bytes 1376264 | tf_op jit(solution)/shard_map/ppermute | solution.py:347
  54.7 0.0 collective-permute-start.8
  54.8 1.2 %collective-permute-start.11 = (bf16[2,4,7,16,128]{4,3,2,1,0:T(8,128)(2,1)S(1)}, bf16[2,4,7,16,128]{4,3,2,1,0:T(8,128)(2,1)S(1)}, u32[]{:S(2)}, u32[]{:S(2)}) collective-permute-start(bf16[2,4,7,16,128]{4,3,2,1,0:T(8,128)(2,1)S(1)} %get-tuple-element.22), channel_id=1, source_target_pairs={{0,11},{1,8},{2,9},{3,10},{8,0},{9,1},{10,2},{11,3},{4,15},{5,12},... | collective-permute-start | bytes 688136 | tf_op jit(solution)/shard_map/ppermute | solution.py:347
  56.0 0.3 collective-permute-start.10
  56.3 0.0 copy-done.1
  56.3 0.1 copy.25.tokens
  56.4 1.2 %project.3.refs_5_ = bf16[128,28672]{1,0:T(8,128)(2,1)} custom-call(bf16[128,64]{1,0:T(8,128)(2,1)S(1)} %copy.25.tokens, bf16[4,4,7,16,128]{4,3,2,1,0:T(8,128)(2,1)S(1)} %pad_maximum_fusion.rest_0_.refs_0_), custom_call_target="tpu_custom_call" | custom-call | flops 58720256 | bytes 1835008 | tf_op jit(solution)/shard_map/project/pallas_call | solution.py:302
  57.6 2.1 %collective-permute-done.11.refs_4_ = bf16[2,4,7,16,128]{4,3,2,1,0:T(8,128)(2,1)S(1)} collective-permute-done((bf16[2,4,7,16,128]{4,3,2,1,0:T(8,128)(2,1)S(1)}, bf16[2,4,7,16,128]{4,3,2,1,0:T(8,128)(2,1)S(1)}, u32[]{:S(2)}, u32[]{:S(2)}) %collective-permute-start.11) | collective-permute-done | bytes 229408 | tf_op jit(solution)/shard_map/ppermute | solution.py:347
  59.7 2.4 %collective-permute-done.10.refs_3_ = bf16[2,4,7,16,128]{4,3,2,1,0:T(8,128)(2,1)S(1)} collective-permute-done((bf16[2,4,7,16,128]{4,3,2,1,0:T(8,128)(2,1)S(1)}, bf16[2,4,7,16,128]{4,3,2,1,0:T(8,128)(2,1)S(1)}, u32[]{:S(2)}, u32[]{:S(2)}) %collective-permute-start.10) | collective-permute-done | bytes 229408 | tf_op jit(solution)/shard_map/ppermute | solution.py:347
  62.1 0.0 collective-permute-done.9.refs_2_
  62.1 1.2 %collective-permute-done.8.refs_1_ = bf16[4,4,7,16,128]{4,3,2,1,0:T(8,128)(2,1)S(1)} collective-permute-done((bf16[4,4,7,16,128]{4,3,2,1,0:T(8,128)(2,1)S(1)}, bf16[4,4,7,16,128]{4,3,2,1,0:T(8,128)(2,1)S(1)}, u32[]{:S(2)}, u32[]{:S(2)}) %collective-permute-start.8) | collective-permute-done | bytes 458784 | tf_op jit(solution)/shard_map/ppermute | solution.py:347
  63.3 7.2 %collective-permute-start.12 = (bf16[4,4,7,16,128]{4,3,2,1,0:T(8,128)(2,1)S(1)}, bf16[4,4,7,16,128]{4,3,2,1,0:T(8,128)(2,1)S(1)}, u32[]{:S(2)}, u32[]{:S(2)}) collective-permute-start(bf16[4,4,7,16,128]{4,3,2,1,0:T(8,128)(2,1)S(1)} %get-tuple-element.16), channel_id=1, source_target_pairs={{0,4},{4,0},{1,5},{5,1},{2,6},{6,2},{3,7},{7,3},{8,12},{12,8},{9,1... | collective-permute-start | bytes 1376264 | tf_op jit(solution)/shard_map/ppermute | solution.py:347
  70.5 0.1 collective-permute-start.13
  70.6 0.4 collective-permute-start.14
  71.0 0.1 collective-permute-start.15
  71.1 0.4 collective-permute-start.16
  71.5 1.8 %project.4.rest_5_ = bf16[128,28672]{1,0:T(8,128)(2,1)} custom-call(bf16[128,64]{1,0:T(8,128)(2,1)S(1)} %copy.25.tokens, bf16[4,4,7,16,128]{4,3,2,1,0:T(8,128)(2,1)S(1)} %get-tuple-element.17.rest_0_, bf16[4,4,7,16,128]{4,3,2,1,0:T(8,128)(2,1)S(1)} %get-tuple-element.18.rest_1_, ...), custom_call_target="tpu_custom_call", output_to_operand_aliasing={{}: (5, {})} | custom-call | flops 176160768 | bytes 5505024 | tf_op jit(solution)/shard_map/project/pallas_call | solution.py:302
  73.3 0.2 collective-permute-done.15.rest_3_
  73.5 0.3 collective-permute-done.16.rest_4_
  73.9 0.0 collective-permute-done.12.rest_0_
  73.9 0.0 collective-permute-done.13.rest_1_
  73.9 0.0 collective-permute-done.14.rest_2_
  73.9 2.2 %project.5 = bf16[128,28672]{1,0:T(8,128)(2,1)} custom-call(bf16[128,64]{1,0:T(8,128)(2,1)S(1)} %copy.25.tokens, bf16[4,4,7,16,128]{4,3,2,1,0:T(8,128)(2,1)S(1)} %collective-permute-done.12.rest_0_, bf16[4,4,7,16,128]{4,3,2,1,0:T(8,128)(2,1)S(1)} %collective-permute-done.13.rest_1_, ...), custom_call_target="tpu_custom_call", output_to_operand_aliasing={{}: (6, {})} | custom-call | flops 234881024 | bytes 7340032 | tf_op jit(solution)/shard_map/project/pallas_call | solution.py:302
  (5 shorter events, 0.1 us)
Async XLA Ops:
  0.6 30.4 %copy-start = (bf16[64,7168]{1,0:T(8,128)(2,1)S(1)}, bf16[64,7168]{1,0:T(8,128)(2,1)}, u32[]{:S(2)}) copy-start(bf16[64,7168]{1,0:T(8,128)(2,1)} %weight.1) | copy-start | bytes 2752516
  0.6 55.7 %copy-start.1 = (bf16[128,64]{0,1:T(8,128)(2,1)S(1)}, bf16[128,64]{0,1:T(8,128)(2,1)}, u32[]{:S(2)}) copy-start(bf16[128,64]{0,1:T(8,128)(2,1)} %param.12) | copy-start | bytes 49156
  4.9 7.5 %collective-permute-start = (f32[4,4,7,16,128]{4,3,2,1,0:T(8,128)}, f32[4,4,7,16,128]{4,3,2,1,0:T(8,128)S(1)}, u32[]{:S(2)}, u32[]{:S(2)}) collective-permute-start(f32[4,4,7,16,128]{4,3,2,1,0:T(8,128)} %get-tuple-element.15), channel_id=1, source_target_pairs={{0,4},{4,0},{1,5},{5,1},{2,6},{6,2},{3,7},{7,3},{8,12},{12,8},{9,1... | collective-permute-start | bytes 2752520 | tf_op jit(solution)/shard_map/ppermute | solution.py:347
  28.2 5.5 %collective-permute-start.1 = (f32[7,16,128]{2,1,0:T(8,128)S(1)}, f32[7,16,128]{2,1,0:T(8,128)S(1)}, u32[]{:S(2)}, u32[]{:S(2)}) collective-permute-start(f32[7,16,128]{2,1,0:T(8,128)S(1)} %convert_reduce_fusion.summed), channel_id=1, source_target_pairs={{0,40},{4,140},{8,32},{12,132},{16,56},{20,156},{24,48},{28,148},{... | collective-permute-start | bytes 172040 | tf_op jit(solution)/shard_map/ppermute | solution.py:347
  33.7 8.3 %collective-permute-start.4 = (bf16[7,16,128]{2,1,0:T(8,128)(2,1)S(1)}, bf16[7,16,128]{2,1,0:T(8,128)(2,1)S(1)}, u32[]{:S(2)}, u32[]{:S(2)}) collective-permute-start(bf16[7,16,128]{2,1,0:T(8,128)(2,1)S(1)} %subtract_convert_fusion), channel_id=1, source_target_pairs={{0,3},{1,2},{2,1},{3,0},{4,7},{5,6},{6,5},{7,4},{8,11},{9,10},{10,... | collective-permute-start | bytes 86024 | tf_op jit(solution)/shard_map/ppermute | solution.py:347
  39.8 6.8 %collective-permute-start.3 = (bf16[7,16,128]{2,1,0:T(8,128)(2,1)S(1)}, bf16[7,16,128]{2,1,0:T(8,128)(2,1)S(1)}, u32[]{:S(2)}, u32[]{:S(2)}) collective-permute-start(bf16[7,16,128]{2,1,0:T(8,128)(2,1)S(1)} %subtract_convert_fusion), channel_id=1, source_target_pairs={{0,2},{1,3},{2,0},{3,1},{4,6},{5,7},{6,4},{7,5},{8,10},{9,11},{10,... | collective-permute-start | bytes 86024 | tf_op jit(solution)/shard_map/ppermute | solution.py:347
  40.8 5.8 %collective-permute-start.2 = (bf16[7,16,128]{2,1,0:T(8,128)(2,1)S(1)}, bf16[7,16,128]{2,1,0:T(8,128)(2,1)S(1)}, u32[]{:S(2)}, u32[]{:S(2)}) collective-permute-start(bf16[7,16,128]{2,1,0:T(8,128)(2,1)S(1)} %subtract_convert_fusion), channel_id=1, source_target_pairs={{0,1},{1,0},{2,3},{3,2},{4,5},{5,4},{6,7},{7,6},{8,9},{9,8},{10,11... | collective-permute-start | bytes 86024 | tf_op jit(solution)/shard_map/ppermute | solution.py:347
  46.6 5.2 %collective-permute-start.6 = (bf16[4,7,16,128]{3,2,1,0:T(8,128)(2,1)S(1)}, bf16[4,7,16,128]{3,2,1,0:T(8,128)(2,1)S(1)}, u32[]{:S(2)}, u32[]{:S(2)}) collective-permute-start(bf16[4,7,16,128]{3,2,1,0:T(8,128)(2,1)S(1)} %get-tuple-element.25), channel_id=1, source_target_pairs={{0,128},{4,36},{16,144},{20,52},{32,160},{36,4},{48,176},{52,20},{... | collective-permute-start | bytes 344072 | tf_op jit(solution)/shard_map/ppermute | solution.py:347
  48.2 4.9 %collective-permute-start.5 = (bf16[4,7,16,128]{3,2,1,0:T(8,128)(2,1)S(1)}, bf16[4,7,16,128]{3,2,1,0:T(8,128)(2,1)S(1)}, u32[]{:S(2)}, u32[]{:S(2)}) collective-permute-start(bf16[4,7,16,128]{3,2,1,0:T(8,128)(2,1)S(1)} %get-tuple-element.25), channel_id=1, source_target_pairs={{0,64},{4,20},{16,80},{20,36},{32,96},{36,52},{48,112},{52,4},{64,... | collective-permute-start | bytes 344072 | tf_op jit(solution)/shard_map/ppermute | solution.py:347
  48.5 4.6 %collective-permute-start.7 = (bf16[4,7,16,128]{3,2,1,0:T(8,128)(2,1)S(1)}, bf16[4,7,16,128]{3,2,1,0:T(8,128)(2,1)S(1)}, u32[]{:S(2)}, u32[]{:S(2)}) collective-permute-start(bf16[4,7,16,128]{3,2,1,0:T(8,128)(2,1)S(1)} %get-tuple-element.25), channel_id=1, source_target_pairs={{0,192},{4,52},{16,208},{20,4},{32,224},{36,20},{48,240},{52,36},{... | collective-permute-start | bytes 344072 | tf_op jit(solution)/shard_map/ppermute | solution.py:347
  53.2 8.9 %collective-permute-start.9 = (bf16[4,4,7,16,128]{4,3,2,1,0:T(8,128)(2,1)S(1)}, bf16[4,4,7,16,128]{4,3,2,1,0:T(8,128)(2,1)S(1)}, u32[]{:S(2)}, u32[]{:S(2)}) collective-permute-start(bf16[4,4,7,16,128]{4,3,2,1,0:T(8,128)(2,1)S(1)} %pad_maximum_fusion.rest_0_.refs_0_), channel_id=1, source_target_pairs={{0,48},{4,196},{16,0},{20,212},{32,16},{36,228},{48,32},{52,244},{... | collective-permute-start | bytes 1376264 | tf_op jit(solution)/shard_map/ppermute | solution.py:347
  54.7 8.5 %collective-permute-start.8 = (bf16[4,4,7,16,128]{4,3,2,1,0:T(8,128)(2,1)S(1)}, bf16[4,4,7,16,128]{4,3,2,1,0:T(8,128)(2,1)S(1)}, u32[]{:S(2)}, u32[]{:S(2)}) collective-permute-start(bf16[4,4,7,16,128]{4,3,2,1,0:T(8,128)(2,1)S(1)} %pad_maximum_fusion.rest_0_.refs_0_), channel_id=1, source_target_pairs={{0,16},{4,68},{16,32},{20,84},{32,48},{36,100},{48,0},{52,116},{64... | collective-permute-start | bytes 1376264 | tf_op jit(solution)/shard_map/ppermute | solution.py:347
  54.8 4.9 %collective-permute-start.11 = (bf16[2,4,7,16,128]{4,3,2,1,0:T(8,128)(2,1)S(1)}, bf16[2,4,7,16,128]{4,3,2,1,0:T(8,128)(2,1)S(1)}, u32[]{:S(2)}, u32[]{:S(2)}) collective-permute-start(bf16[2,4,7,16,128]{4,3,2,1,0:T(8,128)(2,1)S(1)} %get-tuple-element.22), channel_id=1, source_target_pairs={{0,11},{1,8},{2,9},{3,10},{8,0},{9,1},{10,2},{11,3},{4,15},{5,12},... | collective-permute-start | bytes 688136 | tf_op jit(solution)/shard_map/ppermute | solution.py:347
  56.0 6.1 %collective-permute-start.10 = (bf16[2,4,7,16,128]{4,3,2,1,0:T(8,128)(2,1)S(1)}, bf16[2,4,7,16,128]{4,3,2,1,0:T(8,128)(2,1)S(1)}, u32[]{:S(2)}, u32[]{:S(2)}) collective-permute-start(bf16[2,4,7,16,128]{4,3,2,1,0:T(8,128)(2,1)S(1)} %get-tuple-element.23), channel_id=1, source_target_pairs={{0,8},{1,9},{2,10},{3,11},{8,1},{9,2},{10,3},{11,0},{4,12},{5,13},... | collective-permute-start | bytes 688136 | tf_op jit(solution)/shard_map/ppermute | solution.py:347
  63.3 10.6 %collective-permute-start.12 = (bf16[4,4,7,16,128]{4,3,2,1,0:T(8,128)(2,1)S(1)}, bf16[4,4,7,16,128]{4,3,2,1,0:T(8,128)(2,1)S(1)}, u32[]{:S(2)}, u32[]{:S(2)}) collective-permute-start(bf16[4,4,7,16,128]{4,3,2,1,0:T(8,128)(2,1)S(1)} %get-tuple-element.16), channel_id=1, source_target_pairs={{0,4},{4,0},{1,5},{5,1},{2,6},{6,2},{3,7},{7,3},{8,12},{12,8},{9,1... | collective-permute-start | bytes 1376264 | tf_op jit(solution)/shard_map/ppermute | solution.py:347
  70.5 3.4 %collective-permute-start.13 = (bf16[4,4,7,16,128]{4,3,2,1,0:T(8,128)(2,1)S(1)}, bf16[4,4,7,16,128]{4,3,2,1,0:T(8,128)(2,1)S(1)}, u32[]{:S(2)}, u32[]{:S(2)}) collective-permute-start(bf16[4,4,7,16,128]{4,3,2,1,0:T(8,128)(2,1)S(1)} %get-tuple-element.17.rest_0_), channel_id=1, source_target_pairs={{0,4},{4,0},{1,5},{5,1},{2,6},{6,2},{3,7},{7,3},{8,12},{12,8},{9,1... | collective-permute-start | bytes 1376264 | tf_op jit(solution)/shard_map/ppermute | solution.py:347
  70.6 3.3 %collective-permute-start.14 = (bf16[4,4,7,16,128]{4,3,2,1,0:T(8,128)(2,1)S(1)}, bf16[4,4,7,16,128]{4,3,2,1,0:T(8,128)(2,1)S(1)}, u32[]{:S(2)}, u32[]{:S(2)}) collective-permute-start(bf16[4,4,7,16,128]{4,3,2,1,0:T(8,128)(2,1)S(1)} %get-tuple-element.18.rest_1_), channel_id=1, source_target_pairs={{0,4},{4,0},{1,5},{5,1},{2,6},{6,2},{3,7},{7,3},{8,12},{12,8},{9,1... | collective-permute-start | bytes 1376264 | tf_op jit(solution)/shard_map/ppermute | solution.py:347
  71.0 2.6 %collective-permute-start.15 = (bf16[2,4,7,16,128]{4,3,2,1,0:T(8,128)(2,1)S(1)}, bf16[2,4,7,16,128]{4,3,2,1,0:T(8,128)(2,1)S(1)}, u32[]{:S(2)}, u32[]{:S(2)}) collective-permute-start(bf16[2,4,7,16,128]{4,3,2,1,0:T(8,128)(2,1)S(1)} %get-tuple-element.19.rest_2_), channel_id=1, source_target_pairs={{0,4},{4,0},{1,5},{5,1},{2,6},{6,2},{3,7},{7,3},{8,12},{12,8},{9,1... | collective-permute-start | bytes 688136 | tf_op jit(solution)/shard_map/ppermute | solution.py:347
  71.1 2.8 %collective-permute-start.16 = (bf16[2,4,7,16,128]{4,3,2,1,0:T(8,128)(2,1)S(1)}, bf16[2,4,7,16,128]{4,3,2,1,0:T(8,128)(2,1)S(1)}, u32[]{:S(2)}, u32[]{:S(2)}) collective-permute-start(bf16[2,4,7,16,128]{4,3,2,1,0:T(8,128)(2,1)S(1)} %get-tuple-element.20.rest_3_), channel_id=1, source_target_pairs={{0,4},{4,0},{1,5},{5,1},{2,6},{6,2},{3,7},{7,3},{8,12},{12,8},{9,1... | collective-permute-start | bytes 688136 | tf_op jit(solution)/shard_map/ppermute | solution.py:347

commit v5 on v4

--- a/solution.py
+++ b/solution.py
@@ -157,7 +157,8 @@
                 inner = jnp.where(half == 0, goal, i)
                 for t in range(tiles):
                     at = j * wide + t * LANES - span.start
-                    sent_buf[j, i, t] = transmitted[i * ROWS : (i + 1) * ROWS, at : at + LANES]
+                    part = transmitted[i * ROWS : (i + 1) * ROWS, at : at + LANES]
+                    sent_buf[j, i, t] = part.astype(sent_buf.dtype)
                 store = pltpu.make_async_copy(
                     sent_buf.at[j, i], sent.at[outer, inner], sent_sems.at[j, i]
                 )
@@ -173,10 +174,11 @@
     wide = breadth // 2 // steps
     tiles = wide // LANES
     chunk = (tiles, ROWS, LANES)
+    kind = BF16 if first else F32
     in_specs = [pl.BlockSpec(memory_space=pltpu.HBM)] * (3 + len(tables))
     out_shape = [
         jax.ShapeDtypeStruct((1, height, breadth), F32),
-        jax.ShapeDtypeStruct((SIZES[0], steps) + chunk, F32),
+        jax.ShapeDtypeStruct((SIZES[0], steps) + chunk, kind),
     ]
     out_specs = [pl.BlockSpec(memory_space=pltpu.HBM)] * 2
     operands = [picked, momentum, gradient, *tables]
@@ -202,7 +204,7 @@
             pltpu.SemaphoreType.DMA((steps, 2)),
             pltpu.SemaphoreType.DMA((steps,)),
             pltpu.SemaphoreType.DMA((5,)),
-            pltpu.VMEM((steps, SIZES[0]) + chunk, F32),
+            pltpu.VMEM((steps, SIZES[0]) + chunk, kind),
             pltpu.SemaphoreType.DMA((steps, SIZES[0])),
             pltpu.SMEM(picked.shape, jnp.int32),
         ],
@@ -395,7 +397,7 @@
     new_momentum, kept = compress(
         False, picked, momentum, gradient, tables, partial
     )
-    pair = (kept + arrived).astype(BF16)
+    pair = (kept + arrived.astype(F32)).astype(BF16)
     pair = pair.reshape((plane,) + pair.shape[2:])
     parts = lax.all_to_all(pair, ("x", "y"), 0, 0, tiled=True)
     summed = jnp.sum(parts.astype(F32), axis=0)

time: 76.6 us -> 76.7 us (level)
  no operation moved by 1% of the time
where the time goes in v5:
time: 76.7 us; the launch traced here: 76.4 us
  starting transfers between devices  30.3 us (40%)
  waiting for transfers between devices  15.6 us (20%)
  blocking collectives  14.4 us (19%)
  Pallas kernels  13.6 us (18%)
  other arithmetic  1.47 us (2%)
  between operations  0.9 us (1%)
    ppermute x17, starting transfers between devices, move(): return lax.ppermute(value, axes, pairs)  30.3 us
    ppermute x17, waiting for transfers between devices, move(): return lax.ppermute(value, axes, pairs)  15.6 us
    all_to_all x1, blocking collectives, on_device(): parts = lax.all_to_all(pair, ('x', 'y'), 0, 0, tiled=True)  14.4 us
    pallas_call x2, Pallas kernels, compress(): pl.pallas_call(body, in_specs=in_specs, out_specs=out_specs, out_shape=ou...  8.33 us
    pallas_call x3, Pallas kernels, project(): pl.pallas_call(body, in_specs=in_specs, out_specs=pl.BlockSpec(memory_spa...  5.24 us
  transfers between devices with their start and end apart: 17, of which 9 were waited for; matrix products, arithmetic and copies ran while one was open for 0% of the time, Pallas kernels for 9%

profile of v5, /device:TPU:1, one launch (start us, length us, event | category | flops | bytes accessed | tf_op | source)
XLA Modules:
  0.0 76.4 jit_solution(707250353185332567)
XLA Ops:
  0.6 0.0 copy-start
  0.6 0.0 copy-start.1
  0.6 4.2 %compress_first.1 = (f32[1,64,7168]{2,1,0:T(8,128)}, bf16[4,4,7,16,128]{4,3,2,1,0:T(8,128)(2,1)}) custom-call(s32[4,112]{1,0:T(4,128)} %bitcast.27, f32[1,64,7168]{2,1,0:T(8,128)} %refs_1_.3, bf16[1,64,7168]{2,1,0:T(8,128)(2,1)} %refs_2_.3, bf16[64,256]{1,0:T(8,128)(2,1)} %constant.18.clone.refs_3_, bf16[256,256]{1,0:T(8,128)(2,1)} %constant.19.clone.refs_4_, ...), custom_call_target="tpu_custom_call" | custom-call | flops 939524096 | bytes 2752512 | tf_op jit(solution)/shard_map/compress_first/pallas_call | solution.py:194
  4.8 3.3 %collective-permute-start = (bf16[4,4,7,16,128]{4,3,2,1,0:T(8,128)(2,1)}, bf16[4,4,7,16,128]{4,3,2,1,0:T(8,128)(2,1)S(1)}, u32[]{:S(2)}, u32[]{:S(2)}) collective-permute-start(bf16[4,4,7,16,128]{4,3,2,1,0:T(8,128)(2,1)} %get-tuple-element.15), channel_id=1, source_target_pairs={{0,4},{4,0},{1,5},{5,1},{2,6},{6,2},{3,7},{7,3},{8,12},{12,8},{9,1... | collective-permute-start | bytes 1376264 | tf_op jit(solution)/shard_map/ppermute | solution.py:349
  8.2 4.1 %compress_second.1 = (f32[1,64,7168]{2,1,0:T(8,128)}, f32[4,4,7,16,128]{4,3,2,1,0:T(8,128)}) custom-call(s32[4,112]{1,0:T(4,128)} %bitcast.28, f32[1,64,7168]{2,1,0:T(8,128)} %refs_1_.3, bf16[1,64,7168]{2,1,0:T(8,128)(2,1)} %refs_2_.3, bf16[64,256]{1,0:T(8,128)(2,1)} %constant.18.clone.refs_3_, ...), custom_call_target="tpu_custom_call", output_to_operand_aliasing={{0}: (7, {})} | custom-call | flops 939524096 | bytes 2752512 | tf_op jit(solution)/shard_map/compress_second/pallas_call | solution.py:194
  12.3 0.0 collective-permute-done
  12.3 1.3 %add_convert_fusion = bf16[4,4,7,16,128]{4,3,2,1,0:T(8,128)(2,1)S(1)} fusion(f32[4,4,7,16,128]{4,3,2,1,0:T(8,128)} %get-tuple-element.14, bf16[4,4,7,16,128]{4,3,2,1,0:T(8,128)(2,1)S(1)} %collective-permute-done), kind=kLoop, calls=%fused_computation.1 | loop fusion | flops 688128 | bytes 1835008 | tf_op jit(solution)/shard_map/convert_element_type | solution.py:400
  13.6 14.4 %all_to_all.5 = bf16[16,7,16,128]{3,2,1,0:T(8,128)(2,1)S(1)} all-to-all(bf16[16,7,16,128]{3,2,1,0:T(8,128)(2,1)S(1)} %bitcast.19), channel_id=1, replica_groups=mesh['x'=4,'y'=4,'zl'=2,'core'=2,'fsdp'=4] {'x','y'}, dimensions={0} | all-to-all | bytes 917504 | tf_op jit(solution)/shard_map/all_to_all | solution.py:402
  28.0 0.1 convert_reduce_fusion.summed
  28.1 2.9 %collective-permute-start.1 = (f32[7,16,128]{2,1,0:T(8,128)S(1)}, f32[7,16,128]{2,1,0:T(8,128)S(1)}, u32[]{:S(2)}, u32[]{:S(2)}) collective-permute-start(f32[7,16,128]{2,1,0:T(8,128)S(1)} %convert_reduce_fusion.summed), channel_id=1, source_target_pairs={{0,40},{4,140},{8,32},{12,132},{16,56},{20,156},{24,48},{28,148},{... | collective-permute-start | bytes 172040 | tf_op jit(solution)/shard_map/ppermute | solution.py:349
  31.0 0.0 copy-done
  31.0 2.6 %collective-permute-done.1 = f32[7,16,128]{2,1,0:T(8,128)S(1)} collective-permute-done((f32[7,16,128]{2,1,0:T(8,128)S(1)}, f32[7,16,128]{2,1,0:T(8,128)S(1)}, u32[]{:S(2)}, u32[]{:S(2)}) %collective-permute-start.1) | collective-permute-done | bytes 57376 | tf_op jit(solution)/shard_map/ppermute | solution.py:349
  33.6 6.1 %collective-permute-start.4 = (bf16[7,16,128]{2,1,0:T(8,128)(2,1)S(1)}, bf16[7,16,128]{2,1,0:T(8,128)(2,1)S(1)}, u32[]{:S(2)}, u32[]{:S(2)}) collective-permute-start(bf16[7,16,128]{2,1,0:T(8,128)(2,1)S(1)} %subtract_convert_fusion), channel_id=1, source_target_pairs={{0,3},{1,2},{2,1},{3,0},{4,7},{5,6},{6,5},{7,4},{8,11},{9,10},{10,... | collective-permute-start | bytes 86024 | tf_op jit(solution)/shard_map/ppermute | solution.py:349
  39.7 1.0 %collective-permute-start.3 = (bf16[7,16,128]{2,1,0:T(8,128)(2,1)S(1)}, bf16[7,16,128]{2,1,0:T(8,128)(2,1)S(1)}, u32[]{:S(2)}, u32[]{:S(2)}) collective-permute-start(bf16[7,16,128]{2,1,0:T(8,128)(2,1)S(1)} %subtract_convert_fusion), channel_id=1, source_target_pairs={{0,2},{1,3},{2,0},{3,1},{4,6},{5,7},{6,4},{7,5},{8,10},{9,11},{10,... | collective-permute-start | bytes 86024 | tf_op jit(solution)/shard_map/ppermute | solution.py:349
  40.7 1.2 %collective-permute-start.2 = (bf16[7,16,128]{2,1,0:T(8,128)(2,1)S(1)}, bf16[7,16,128]{2,1,0:T(8,128)(2,1)S(1)}, u32[]{:S(2)}, u32[]{:S(2)}) collective-permute-start(bf16[7,16,128]{2,1,0:T(8,128)(2,1)S(1)} %subtract_convert_fusion), channel_id=1, source_target_pairs={{0,1},{1,0},{2,3},{3,2},{4,5},{5,4},{6,7},{7,6},{8,9},{9,8},{10,11... | collective-permute-start | bytes 86024 | tf_op jit(solution)/shard_map/ppermute | solution.py:349
  41.9 0.0 collective-permute-done.4
  41.9 4.6 %collective-permute-done.3 = bf16[7,16,128]{2,1,0:T(8,128)(2,1)S(1)} collective-permute-done((bf16[7,16,128]{2,1,0:T(8,128)(2,1)S(1)}, bf16[7,16,128]{2,1,0:T(8,128)(2,1)S(1)}, u32[]{:S(2)}, u32[]{:S(2)}) %collective-permute-start.3) | collective-permute-done | bytes 28704 | tf_op jit(solution)/shard_map/ppermute | solution.py:349
  46.5 0.0 collective-permute-done.2
  46.5 1.7 %collective-permute-start.6 = (bf16[4,7,16,128]{3,2,1,0:T(8,128)(2,1)S(1)}, bf16[4,7,16,128]{3,2,1,0:T(8,128)(2,1)S(1)}, u32[]{:S(2)}, u32[]{:S(2)}) collective-permute-start(bf16[4,7,16,128]{3,2,1,0:T(8,128)(2,1)S(1)} %get-tuple-element.25), channel_id=1, source_target_pairs={{0,128},{4,36},{16,144},{20,52},{32,160},{36,4},{48,176},{52,20},{... | collective-permute-start | bytes 344072 | tf_op jit(solution)/shard_map/ppermute | solution.py:349
  48.2 0.3 collective-permute-start.5
  48.5 2.4 %collective-permute-start.7 = (bf16[4,7,16,128]{3,2,1,0:T(8,128)(2,1)S(1)}, bf16[4,7,16,128]{3,2,1,0:T(8,128)(2,1)S(1)}, u32[]{:S(2)}, u32[]{:S(2)}) collective-permute-start(bf16[4,7,16,128]{3,2,1,0:T(8,128)(2,1)S(1)} %get-tuple-element.25), channel_id=1, source_target_pairs={{0,192},{4,52},{16,208},{20,4},{32,224},{36,20},{48,240},{52,36},{... | collective-permute-start | bytes 344072 | tf_op jit(solution)/shard_map/ppermute | solution.py:349
  50.8 0.9 %collective-permute-done.6 = bf16[4,7,16,128]{3,2,1,0:T(8,128)(2,1)S(1)} collective-permute-done((bf16[4,7,16,128]{3,2,1,0:T(8,128)(2,1)S(1)}, bf16[4,7,16,128]{3,2,1,0:T(8,128)(2,1)S(1)}, u32[]{:S(2)}, u32[]{:S(2)}) %collective-permute-start.6) | collective-permute-done | bytes 114720 | tf_op jit(solution)/shard_map/ppermute | solution.py:349
  51.7 1.3 %collective-permute-done.5 = bf16[4,7,16,128]{3,2,1,0:T(8,128)(2,1)S(1)} collective-permute-done((bf16[4,7,16,128]{3,2,1,0:T(8,128)(2,1)S(1)}, bf16[4,7,16,128]{3,2,1,0:T(8,128)(2,1)S(1)}, u32[]{:S(2)}, u32[]{:S(2)}) %collective-permute-start.5) | collective-permute-done | bytes 114720 | tf_op jit(solution)/shard_map/ppermute | solution.py:349
  53.0 0.0 collective-permute-done.7
  53.0 0.1 pad_maximum_fusion.rest_0_.refs_0_
  53.1 1.6 %collective-permute-start.9 = (bf16[4,4,7,16,128]{4,3,2,1,0:T(8,128)(2,1)S(1)}, bf16[4,4,7,16,128]{4,3,2,1,0:T(8,128)(2,1)S(1)}, u32[]{:S(2)}, u32[]{:S(2)}) collective-permute-start(bf16[4,4,7,16,128]{4,3,2,1,0:T(8,128)(2,1)S(1)} %pad_maximum_fusion.rest_0_.refs_0_), channel_id=1, source_target_pairs={{0,48},{4,196},{16,0},{20,212},{32,16},{36,228},{48,32},{52,244},{... | collective-permute-start | bytes 1376264 | tf_op jit(solution)/shard_map/ppermute | solution.py:349
  54.6 0.0 collective-permute-start.8
  54.7 1.2 %collective-permute-start.11 = (bf16[2,4,7,16,128]{4,3,2,1,0:T(8,128)(2,1)S(1)}, bf16[2,4,7,16,128]{4,3,2,1,0:T(8,128)(2,1)S(1)}, u32[]{:S(2)}, u32[]{:S(2)}) collective-permute-start(bf16[2,4,7,16,128]{4,3,2,1,0:T(8,128)(2,1)S(1)} %get-tuple-element.22), channel_id=1, source_target_pairs={{0,11},{1,8},{2,9},{3,10},{8,0},{9,1},{10,2},{11,3},{4,15},{5,12},... | collective-permute-start | bytes 688136 | tf_op jit(solution)/shard_map/ppermute | solution.py:349
  55.9 0.3 collective-permute-start.10
  56.2 0.0 copy-done.1
  56.2 0.1 copy.25.tokens
  56.3 1.2 %project.3.refs_5_ = bf16[128,28672]{1,0:T(8,128)(2,1)} custom-call(bf16[128,64]{1,0:T(8,128)(2,1)S(1)} %copy.25.tokens, bf16[4,4,7,16,128]{4,3,2,1,0:T(8,128)(2,1)S(1)} %pad_maximum_fusion.rest_0_.refs_0_), custom_call_target="tpu_custom_call" | custom-call | flops 58720256 | bytes 1835008 | tf_op jit(solution)/shard_map/project/pallas_call | solution.py:304
  57.5 2.1 %collective-permute-done.11.refs_4_ = bf16[2,4,7,16,128]{4,3,2,1,0:T(8,128)(2,1)S(1)} collective-permute-done((bf16[2,4,7,16,128]{4,3,2,1,0:T(8,128)(2,1)S(1)}, bf16[2,4,7,16,128]{4,3,2,1,0:T(8,128)(2,1)S(1)}, u32[]{:S(2)}, u32[]{:S(2)}) %collective-permute-start.11) | collective-permute-done | bytes 229408 | tf_op jit(solution)/shard_map/ppermute | solution.py:349
  59.6 2.4 %collective-permute-done.10.refs_3_ = bf16[2,4,7,16,128]{4,3,2,1,0:T(8,128)(2,1)S(1)} collective-permute-done((bf16[2,4,7,16,128]{4,3,2,1,0:T(8,128)(2,1)S(1)}, bf16[2,4,7,16,128]{4,3,2,1,0:T(8,128)(2,1)S(1)}, u32[]{:S(2)}, u32[]{:S(2)}) %collective-permute-start.10) | collective-permute-done | bytes 229408 | tf_op jit(solution)/shard_map/ppermute | solution.py:349
  62.0 0.0 collective-permute-done.9.refs_2_
  62.0 1.2 %collective-permute-done.8.refs_1_ = bf16[4,4,7,16,128]{4,3,2,1,0:T(8,128)(2,1)S(1)} collective-permute-done((bf16[4,4,7,16,128]{4,3,2,1,0:T(8,128)(2,1)S(1)}, bf16[4,4,7,16,128]{4,3,2,1,0:T(8,128)(2,1)S(1)}, u32[]{:S(2)}, u32[]{:S(2)}) %collective-permute-start.8) | collective-permute-done | bytes 458784 | tf_op jit(solution)/shard_map/ppermute | solution.py:349
  63.2 7.4 %collective-permute-start.12 = (bf16[4,4,7,16,128]{4,3,2,1,0:T(8,128)(2,1)S(1)}, bf16[4,4,7,16,128]{4,3,2,1,0:T(8,128)(2,1)S(1)}, u32[]{:S(2)}, u32[]{:S(2)}) collective-permute-start(bf16[4,4,7,16,128]{4,3,2,1,0:T(8,128)(2,1)S(1)} %get-tuple-element.16), channel_id=1, source_target_pairs={{0,4},{4,0},{1,5},{5,1},{2,6},{6,2},{3,7},{7,3},{8,12},{12,8},{9,1... | collective-permute-start | bytes 1376264 | tf_op jit(solution)/shard_map/ppermute | solution.py:349
  70.6 0.1 collective-permute-start.13
  70.7 0.4 collective-permute-start.14
  71.1 0.1 collective-permute-start.15
  71.2 0.4 collective-permute-start.16
  71.6 1.8 %project.4.rest_5_ = bf16[128,28672]{1,0:T(8,128)(2,1)} custom-call(bf16[128,64]{1,0:T(8,128)(2,1)S(1)} %copy.25.tokens, bf16[4,4,7,16,128]{4,3,2,1,0:T(8,128)(2,1)S(1)} %get-tuple-element.17.rest_0_, bf16[4,4,7,16,128]{4,3,2,1,0:T(8,128)(2,1)S(1)} %get-tuple-element.18.rest_1_, ...), custom_call_target="tpu_custom_call", output_to_operand_aliasing={{}: (5, {})} | custom-call | flops 176160768 | bytes 5505024 | tf_op jit(solution)/shard_map/project/pallas_call | solution.py:304
  73.4 0.2 collective-permute-done.15.rest_3_
  73.7 0.3 collective-permute-done.16.rest_4_
  74.0 0.0 collective-permute-done.12.rest_0_
  74.0 0.0 collective-permute-done.13.rest_1_
  74.0 0.0 collective-permute-done.14.rest_2_
  74.0 2.2 %project.5 = bf16[128,28672]{1,0:T(8,128)(2,1)} custom-call(bf16[128,64]{1,0:T(8,128)(2,1)S(1)} %copy.25.tokens, bf16[4,4,7,16,128]{4,3,2,1,0:T(8,128)(2,1)S(1)} %collective-permute-done.12.rest_0_, bf16[4,4,7,16,128]{4,3,2,1,0:T(8,128)(2,1)S(1)} %collective-permute-done.13.rest_1_, ...), custom_call_target="tpu_custom_call", output_to_operand_aliasing={{}: (6, {})} | custom-call | flops 234881024 | bytes 7340032 | tf_op jit(solution)/shard_map/project/pallas_call | solution.py:304
  (5 shorter events, 0.1 us)
Async XLA Ops:
  0.6 30.3 %copy-start = (bf16[64,7168]{1,0:T(8,128)(2,1)S(1)}, bf16[64,7168]{1,0:T(8,128)(2,1)}, u32[]{:S(2)}) copy-start(bf16[64,7168]{1,0:T(8,128)(2,1)} %weight.1) | copy-start | bytes 2752516
  0.6 55.6 %copy-start.1 = (bf16[128,64]{0,1:T(8,128)(2,1)S(1)}, bf16[128,64]{0,1:T(8,128)(2,1)}, u32[]{:S(2)}) copy-start(bf16[128,64]{0,1:T(8,128)(2,1)} %param.12) | copy-start | bytes 49156
  4.8 7.5 %collective-permute-start = (bf16[4,4,7,16,128]{4,3,2,1,0:T(8,128)(2,1)}, bf16[4,4,7,16,128]{4,3,2,1,0:T(8,128)(2,1)S(1)}, u32[]{:S(2)}, u32[]{:S(2)}) collective-permute-start(bf16[4,4,7,16,128]{4,3,2,1,0:T(8,128)(2,1)} %get-tuple-element.15), channel_id=1, source_target_pairs={{0,4},{4,0},{1,5},{5,1},{2,6},{6,2},{3,7},{7,3},{8,12},{12,8},{9,1... | collective-permute-start | bytes 1376264 | tf_op jit(solution)/shard_map/ppermute | solution.py:349
  28.1 5.5 %collective-permute-start.1 = (f32[7,16,128]{2,1,0:T(8,128)S(1)}, f32[7,16,128]{2,1,0:T(8,128)S(1)}, u32[]{:S(2)}, u32[]{:S(2)}) collective-permute-start(f32[7,16,128]{2,1,0:T(8,128)S(1)} %convert_reduce_fusion.summed), channel_id=1, source_target_pairs={{0,40},{4,140},{8,32},{12,132},{16,56},{20,156},{24,48},{28,148},{... | collective-permute-start | bytes 172040 | tf_op jit(solution)/shard_map/ppermute | solution.py:349
  33.6 8.3 %collective-permute-start.4 = (bf16[7,16,128]{2,1,0:T(8,128)(2,1)S(1)}, bf16[7,16,128]{2,1,0:T(8,128)(2,1)S(1)}, u32[]{:S(2)}, u32[]{:S(2)}) collective-permute-start(bf16[7,16,128]{2,1,0:T(8,128)(2,1)S(1)} %subtract_convert_fusion), channel_id=1, source_target_pairs={{0,3},{1,2},{2,1},{3,0},{4,7},{5,6},{6,5},{7,4},{8,11},{9,10},{10,... | collective-permute-start | bytes 86024 | tf_op jit(solution)/shard_map/ppermute | solution.py:349
  39.7 6.8 %collective-permute-start.3 = (bf16[7,16,128]{2,1,0:T(8,128)(2,1)S(1)}, bf16[7,16,128]{2,1,0:T(8,128)(2,1)S(1)}, u32[]{:S(2)}, u32[]{:S(2)}) collective-permute-start(bf16[7,16,128]{2,1,0:T(8,128)(2,1)S(1)} %subtract_convert_fusion), channel_id=1, source_target_pairs={{0,2},{1,3},{2,0},{3,1},{4,6},{5,7},{6,4},{7,5},{8,10},{9,11},{10,... | collective-permute-start | bytes 86024 | tf_op jit(solution)/shard_map/ppermute | solution.py:349
  40.7 5.8 %collective-permute-start.2 = (bf16[7,16,128]{2,1,0:T(8,128)(2,1)S(1)}, bf16[7,16,128]{2,1,0:T(8,128)(2,1)S(1)}, u32[]{:S(2)}, u32[]{:S(2)}) collective-permute-start(bf16[7,16,128]{2,1,0:T(8,128)(2,1)S(1)} %subtract_convert_fusion), channel_id=1, source_target_pairs={{0,1},{1,0},{2,3},{3,2},{4,5},{5,4},{6,7},{7,6},{8,9},{9,8},{10,11... | collective-permute-start | bytes 86024 | tf_op jit(solution)/shard_map/ppermute | solution.py:349
  46.5 5.2 %collective-permute-start.6 = (bf16[4,7,16,128]{3,2,1,0:T(8,128)(2,1)S(1)}, bf16[4,7,16,128]{3,2,1,0:T(8,128)(2,1)S(1)}, u32[]{:S(2)}, u32[]{:S(2)}) collective-permute-start(bf16[4,7,16,128]{3,2,1,0:T(8,128)(2,1)S(1)} %get-tuple-element.25), channel_id=1, source_target_pairs={{0,128},{4,36},{16,144},{20,52},{32,160},{36,4},{48,176},{52,20},{... | collective-permute-start | bytes 344072 | tf_op jit(solution)/shard_map/ppermute | solution.py:349
  48.2 4.9 %collective-permute-start.5 = (bf16[4,7,16,128]{3,2,1,0:T(8,128)(2,1)S(1)}, bf16[4,7,16,128]{3,2,1,0:T(8,128)(2,1)S(1)}, u32[]{:S(2)}, u32[]{:S(2)}) collective-permute-start(bf16[4,7,16,128]{3,2,1,0:T(8,128)(2,1)S(1)} %get-tuple-element.25), channel_id=1, source_target_pairs={{0,64},{4,20},{16,80},{20,36},{32,96},{36,52},{48,112},{52,4},{64,... | collective-permute-start | bytes 344072 | tf_op jit(solution)/shard_map/ppermute | solution.py:349
  48.5 4.6 %collective-permute-start.7 = (bf16[4,7,16,128]{3,2,1,0:T(8,128)(2,1)S(1)}, bf16[4,7,16,128]{3,2,1,0:T(8,128)(2,1)S(1)}, u32[]{:S(2)}, u32[]{:S(2)}) collective-permute-start(bf16[4,7,16,128]{3,2,1,0:T(8,128)(2,1)S(1)} %get-tuple-element.25), channel_id=1, source_target_pairs={{0,192},{4,52},{16,208},{20,4},{32,224},{36,20},{48,240},{52,36},{... | collective-permute-start | bytes 344072 | tf_op jit(solution)/shard_map/ppermute | solution.py:349
  53.1 8.9 %collective-permute-start.9 = (bf16[4,4,7,16,128]{4,3,2,1,0:T(8,128)(2,1)S(1)}, bf16[4,4,7,16,128]{4,3,2,1,0:T(8,128)(2,1)S(1)}, u32[]{:S(2)}, u32[]{:S(2)}) collective-permute-start(bf16[4,4,7,16,128]{4,3,2,1,0:T(8,128)(2,1)S(1)} %pad_maximum_fusion.rest_0_.refs_0_), channel_id=1, source_target_pairs={{0,48},{4,196},{16,0},{20,212},{32,16},{36,228},{48,32},{52,244},{... | collective-permute-start | bytes 1376264 | tf_op jit(solution)/shard_map/ppermute | solution.py:349
  54.6 8.5 %collective-permute-start.8 = (bf16[4,4,7,16,128]{4,3,2,1,0:T(8,128)(2,1)S(1)}, bf16[4,4,7,16,128]{4,3,2,1,0:T(8,128)(2,1)S(1)}, u32[]{:S(2)}, u32[]{:S(2)}) collective-permute-start(bf16[4,4,7,16,128]{4,3,2,1,0:T(8,128)(2,1)S(1)} %pad_maximum_fusion.rest_0_.refs_0_), channel_id=1, source_target_pairs={{0,16},{4,68},{16,32},{20,84},{32,48},{36,100},{48,0},{52,116},{64... | collective-permute-start | bytes 1376264 | tf_op jit(solution)/shard_map/ppermute | solution.py:349
  54.7 4.9 %collective-permute-start.11 = (bf16[2,4,7,16,128]{4,3,2,1,0:T(8,128)(2,1)S(1)}, bf16[2,4,7,16,128]{4,3,2,1,0:T(8,128)(2,1)S(1)}, u32[]{:S(2)}, u32[]{:S(2)}) collective-permute-start(bf16[2,4,7,16,128]{4,3,2,1,0:T(8,128)(2,1)S(1)} %get-tuple-element.22), channel_id=1, source_target_pairs={{0,11},{1,8},{2,9},{3,10},{8,0},{9,1},{10,2},{11,3},{4,15},{5,12},... | collective-permute-start | bytes 688136 | tf_op jit(solution)/shard_map/ppermute | solution.py:349
  55.9 6.1 %collective-permute-start.10 = (bf16[2,4,7,16,128]{4,3,2,1,0:T(8,128)(2,1)S(1)}, bf16[2,4,7,16,128]{4,3,2,1,0:T(8,128)(2,1)S(1)}, u32[]{:S(2)}, u32[]{:S(2)}) collective-permute-start(bf16[2,4,7,16,128]{4,3,2,1,0:T(8,128)(2,1)S(1)} %get-tuple-element.23), channel_id=1, source_target_pairs={{0,8},{1,9},{2,10},{3,11},{8,1},{9,2},{10,3},{11,0},{4,12},{5,13},... | collective-permute-start | bytes 688136 | tf_op jit(solution)/shard_map/ppermute | solution.py:349
  63.2 10.8 %collective-permute-start.12 = (bf16[4,4,7,16,128]{4,3,2,1,0:T(8,128)(2,1)S(1)}, bf16[4,4,7,16,128]{4,3,2,1,0:T(8,128)(2,1)S(1)}, u32[]{:S(2)}, u32[]{:S(2)}) collective-permute-start(bf16[4,4,7,16,128]{4,3,2,1,0:T(8,128)(2,1)S(1)} %get-tuple-element.16), channel_id=1, source_target_pairs={{0,4},{4,0},{1,5},{5,1},{2,6},{6,2},{3,7},{7,3},{8,12},{12,8},{9,1... | collective-permute-start | bytes 1376264 | tf_op jit(solution)/shard_map/ppermute | solution.py:349
  70.6 3.4 %collective-permute-start.13 = (bf16[4,4,7,16,128]{4,3,2,1,0:T(8,128)(2,1)S(1)}, bf16[4,4,7,16,128]{4,3,2,1,0:T(8,128)(2,1)S(1)}, u32[]{:S(2)}, u32[]{:S(2)}) collective-permute-start(bf16[4,4,7,16,128]{4,3,2,1,0:T(8,128)(2,1)S(1)} %get-tuple-element.17.rest_0_), channel_id=1, source_target_pairs={{0,4},{4,0},{1,5},{5,1},{2,6},{6,2},{3,7},{7,3},{8,12},{12,8},{9,1... | collective-permute-start | bytes 1376264 | tf_op jit(solution)/shard_map/ppermute | solution.py:349
  70.7 3.3 %collective-permute-start.14 = (bf16[4,4,7,16,128]{4,3,2,1,0:T(8,128)(2,1)S(1)}, bf16[4,4,7,16,128]{4,3,2,1,0:T(8,128)(2,1)S(1)}, u32[]{:S(2)}, u32[]{:S(2)}) collective-permute-start(bf16[4,4,7,16,128]{4,3,2,1,0:T(8,128)(2,1)S(1)} %get-tuple-element.18.rest_1_), channel_id=1, source_target_pairs={{0,4},{4,0},{1,5},{5,1},{2,6},{6,2},{3,7},{7,3},{8,12},{12,8},{9,1... | collective-permute-start | bytes 1376264 | tf_op jit(solution)/shard_map/ppermute | solution.py:349
  71.1 2.6 %collective-permute-start.15 = (bf16[2,4,7,16,128]{4,3,2,1,0:T(8,128)(2,1)S(1)}, bf16[2,4,7,16,128]{4,3,2,1,0:T(8,128)(2,1)S(1)}, u32[]{:S(2)}, u32[]{:S(2)}) collective-permute-start(bf16[2,4,7,16,128]{4,3,2,1,0:T(8,128)(2,1)S(1)} %get-tuple-element.19.rest_2_), channel_id=1, source_target_pairs={{0,4},{4,0},{1,5},{5,1},{2,6},{6,2},{3,7},{7,3},{8,12},{12,8},{9,1... | collective-permute-start | bytes 688136 | tf_op jit(solution)/shard_map/ppermute | solution.py:349
  71.2 2.8 %collective-permute-start.16 = (bf16[2,4,7,16,128]{4,3,2,1,0:T(8,128)(2,1)S(1)}, bf16[2,4,7,16,128]{4,3,2,1,0:T(8,128)(2,1)S(1)}, u32[]{:S(2)}, u32[]{:S(2)}) collective-permute-start(bf16[2,4,7,16,128]{4,3,2,1,0:T(8,128)(2,1)S(1)} %get-tuple-element.20.rest_3_), channel_id=1, source_target_pairs={{0,4},{4,0},{1,5},{5,1},{2,6},{6,2},{3,7},{7,3},{8,12},{12,8},{9,1... | collective-permute-start | bytes 688136 | tf_op jit(solution)/shard_map/ppermute | solution.py:349
